TPU v7x, 128 devices: a whole 4x4x4 slice. The times are simulated.
128 devices in a mesh: row: 16 (over z_lo, x, core), col: 8 (over z_hi, y).
Axes of the slice: x: 4, y: 4, z: 4 (z_hi: 2, z_lo: 2; z = z_hi * 2 + z_lo), core: 2. Of those that a mesh axis runs over, the one named last changes fastest.
Arguments:
- pair_input: bfloat16 [640, 640, 128], P('row', 'col'), may hold values from -6 to 6
- token_mask: int32 [640], replicated, may hold values from 0 to 1, as said below
- ln_gain: float32 [2, 128], replicated, may hold values from 0.1 to 1.9
- w_query: bfloat16 [2, 128, 128], replicated, may hold values from -24 to 24
- w_key: bfloat16 [2, 128, 128], replicated, may hold values from -0.5 to 0.5
- w_value: bfloat16 [2, 128, 128], replicated, may hold values from -0.5 to 0.5
- w_gate: bfloat16 [2, 128, 128], replicated, may hold values from -0.5 to 0.5
- w_bias: bfloat16 [2, 128, 4], replicated, may hold values from -1 to 1
- w_out: bfloat16 [2, 128, 128], replicated, may hold values from -0.5 to 0.5
Outputs:
- pair_out: bfloat16 [640, 640, 128], P('row', 'col')
Inputs may be any that keep to these rules, and one draw needn't show every extreme that they name: `token_mask`: 0 marks a padded token and 1 a real one; at least one token is real and at least one is padded.
All inputs are finite; a program needn't handle non-finite values.
Results may differ from a plain program's by a relative error of at most 0.035.
The roundings to bfloat16 on the way count: a program that leaves them out, or rounds other values in their place, can miss the bound.
Values may be sent and summed in bfloat16 or wider, within the bound.
No kernel may reach another device: no remote copies, remote signals or barrier semaphores. Data moves between devices by JAX's collectives and lax.ppermute only.
A program may use at most 192 MiB of HBM per device.

v0:
```python
import math

import jax
import jax.numpy as jnp
from jax import lax
from jax.sharding import PartitionSpec as P

H = 4
HD = 32


epsilon = 1e-05
masked_score = -1e30


def normalize(pair_block, gain_row):
    upcast = pair_block.astype(jnp.float32)
    centred = upcast - jnp.mean(upcast, axis=-1, keepdims=True)
    variance = jnp.mean(centred * centred, axis=-1, keepdims=True)
    return (centred * lax.rsqrt(variance + epsilon) * gain_row).astype(jnp.bfloat16)


def project(flattened, weight):
    return jnp.dot(flattened, weight, preferred_element_type=jnp.float32).astype(jnp.bfloat16)


def as_heads(array):
    return array.reshape(array.shape[:2] + (H, HD))


def split_blocks(array, blocks):
    return array.reshape((blocks, array.shape[0] // blocks) + array.shape[1:])


def join_blocks(array):
    return array.reshape((-1,) + array.shape[2:])


def block_count(row_count, col_count):
    return row_count // math.gcd(row_count, max(1, 512 // col_count))


def prepare(pair_input, gain_row, w_query, w_gate):
    row_count, col_count, channels = pair_input.shape
    normed = normalize(pair_input, gain_row)
    flattened = normed.reshape(-1, channels)
    head_shape = (row_count, col_count, H, HD)
    queries = project(flattened, w_query).reshape(head_shape)
    gating = jax.nn.sigmoid(jnp.dot(flattened, w_gate, preferred_element_type=jnp.float32)).reshape(
        head_shape
    )
    return (normed, flattened, queries, gating)


def finish(pair_input, accumulated, totals, gating, w_out):
    hidden = (accumulated / totals[..., None] * gating).astype(jnp.bfloat16)
    update = jnp.dot(
        hidden.reshape(-1, pair_input.shape[2]), w_out, preferred_element_type=jnp.float32
    )
    update = update.reshape(pair_input.shape)
    return (pair_input.astype(jnp.float32) + update).astype(jnp.bfloat16)


def key_part(portions):
    return as_heads(portions[0])


def value_part(portions):
    return as_heads(portions[1])


def logits(queries, key_heads, tri_bias, usable, ending):
    if ending:
        scores = jnp.einsum(
            "ijhd,kjhd->ijhk", queries, key_heads, preferred_element_type=jnp.float32
        )
        bias_wide = tri_bias.astype(jnp.float32)[:, None]
    else:
        scores = jnp.einsum(
            "ijhd,ikhd->ijhk", queries, key_heads, preferred_element_type=jnp.float32
        )
        bias_wide = tri_bias.astype(jnp.float32)[None]
    scores = scores * HD ** (-0.5) + bias_wide
    return jnp.where(usable, scores, masked_score)


def online_step(queries, key_heads, value_heads, tri_bias, usable, running, ending, blocks):
    highest, totals, accumulated = running
    rowwise = (tri_bias,) if ending else (key_heads, value_heads)
    usable_float = usable.astype(jnp.float32)

    def advance(operands):
        block_queries, block_rows, block_high, block_total, block_sum = operands
        if ending:
            scores = logits(block_queries, key_heads, block_rows[0], usable, True)
            pattern = "ijhk,kjhd->ijhd"
            sources = value_heads
        else:
            scores = logits(block_queries, block_rows[0], tri_bias, usable, False)
            pattern = "ijhk,ikhd->ijhd"
            sources = block_rows[1]
        updated = jnp.maximum(block_high, jnp.max(scores, axis=-1))
        factor = jnp.exp(block_high - updated)
        exponentials = jnp.exp(scores - updated[..., None]) * usable_float
        block_total = block_total * factor + jnp.sum(exponentials, axis=-1)
        weights = exponentials.astype(jnp.bfloat16)
        block_sum = block_sum * factor[..., None] + jnp.einsum(
            pattern, weights, sources, preferred_element_type=jnp.float32
        )
        return (updated, block_total, block_sum)

    blocked_rows = tuple((split_blocks(member, blocks) for member in rowwise))
    updated, totals, summed = lax.map(
        advance,
        (
            split_blocks(queries, blocks),
            blocked_rows,
            split_blocks(highest, blocks),
            split_blocks(totals, blocks),
            split_blocks(accumulated, blocks),
        ),
    )
    return (join_blocks(updated), join_blocks(totals), join_blocks(summed))


def start_section(pair_input, token_mask, gain_row, w_query, w_key, w_value, w_gate, w_bias, w_out):
    row_count, col_count, channels = pair_input.shape
    normed, flattened, queries, gating = prepare(pair_input, gain_row, w_query, w_gate)
    bias_tile = jnp.einsum(
        "ijc,ch->ihj", normed, w_bias, preferred_element_type=jnp.float32
    ).astype(jnp.bfloat16)
    bias_rows = lax.all_gather(bias_tile, "col", axis=2, tiled=True)
    column = lax.axis_index("col")
    everything = lax.all_gather(bias_rows, "row", axis=0, tiled=True)
    tri_bias = lax.dynamic_slice_in_dim(everything, column * col_count, col_count, 0)
    blocks = block_count(row_count, col_count)
    operand = (
        project(flattened, w_key).reshape(row_count, col_count, channels),
        project(flattened, w_value).reshape(row_count, col_count, channels),
    )
    lowest = jnp.full((row_count, col_count, H), masked_score, jnp.float32)
    nothing = jnp.zeros((row_count, col_count, H), jnp.float32)
    empty = jnp.zeros((row_count, col_count, H, HD), jnp.float32)
    portions = (
        lax.all_gather(operand[0], "col", axis=1, tiled=True),
        lax.all_gather(operand[1], "col", axis=1, tiled=True),
    )
    usable = token_mask > 0
    bias_part = tri_bias
    usable, bias_part = (usable, bias_part)
    highest, totals, accumulated = online_step(
        queries,
        key_part(portions),
        value_part(portions),
        bias_part,
        usable,
        (lowest, nothing, empty),
        False,
        blocks,
    )
    return finish(pair_input, accumulated, totals, gating, w_out)


def end_section(pair_input, token_mask, gain_row, w_query, w_key, w_value, w_gate, w_bias, w_out):
    row_count, col_count, channels = pair_input.shape
    normed, flattened, queries, gating = prepare(pair_input, gain_row, w_query, w_gate)
    bias_tile = jnp.einsum(
        "ijc,ch->jhi", normed, w_bias, preferred_element_type=jnp.float32
    ).astype(jnp.bfloat16)
    bias_cols = lax.all_gather(bias_tile, "row", axis=2, tiled=True)
    row_index = lax.axis_index("row")
    everything = lax.all_gather(bias_cols, "col", axis=0, tiled=True)
    tri_bias = lax.dynamic_slice_in_dim(everything, row_index * row_count, row_count, 0)
    blocks = block_count(row_count, col_count)
    operand = (
        project(flattened, w_key).reshape(row_count, col_count, channels),
        project(flattened, w_value).reshape(row_count, col_count, channels),
    )
    lowest = jnp.full((row_count, col_count, H), masked_score, jnp.float32)
    nothing = jnp.zeros((row_count, col_count, H), jnp.float32)
    empty = jnp.zeros((row_count, col_count, H, HD), jnp.float32)
    portions = (
        lax.all_gather(operand[0], "row", axis=0, tiled=True),
        lax.all_gather(operand[1], "row", axis=0, tiled=True),
    )
    usable = token_mask > 0
    bias_part = tri_bias
    usable, bias_part = (usable, bias_part)
    highest, totals, accumulated = online_step(
        queries,
        key_part(portions),
        value_part(portions),
        bias_part,
        usable,
        (lowest, nothing, empty),
        True,
        blocks,
    )
    return finish(pair_input, accumulated, totals, gating, w_out)


def body(pair_input, token_mask, ln_gain, w_query, w_key, w_value, w_gate, w_bias, w_out):
    after_start = start_section(
        pair_input,
        token_mask,
        ln_gain[0],
        w_query[0],
        w_key[0],
        w_value[0],
        w_gate[0],
        w_bias[0],
        w_out[0],
    )
    return end_section(
        after_start,
        token_mask,
        ln_gain[1],
        w_query[1],
        w_key[1],
        w_value[1],
        w_gate[1],
        w_bias[1],
        w_out[1],
    )


def solution(mesh):
    placed = (P("row", "col", None), P(), P(), P(), P(), P(), P(), P(), P())
    return jax.shard_map(
        body, mesh=mesh, in_specs=placed, out_specs=P("row", "col", None), check_vma=False
    )
```

profile of v0, /device:TPU:8, one launch (start us, length us, event | category | flops | bytes accessed | tf_op | source)
XLA Modules:
  0.0 1069.5 jit_solution(15228703992092472075)
XLA Ops:
  12.5 36.5 %all_gather.25 = bf16[40,4,640]{0,1,2:T(4,128)(2,1)S(1)} all-gather(bf16[40,4,80]{0,1,2:T(4,128)(2,1)S(1)} %copy.68), channel_id=1, replica_groups=mesh['row'=16,'col'=8] {'col'}, dimensions={2}, use_global_device_ids=true | all-gather | bytes 230400 | tf_op jit(solution)/shard_map/all_gather | solution.py:132
  57.6 29.8 %all-gather.9.cloned.1.call-done = bf16[640,4,640]{2,1,0:T(4,128)(2,1)} async-done(((bf16[40,4,640]{2,1,0:T(4,128)(2,1)}), bf16[640,4,640]{2,1,0:T(4,128)(2,1)}) %all-gather.9.cloned.1.call-update) | async-done | bytes 3276816 | tf_op jit(solution)/shard_map/all_gather | solution.py:134
  88.6 91.7 %all-gather.7.cloned.1.call-done = bf16[40,640,128]{2,1,0:T(8,128)(2,1)} async-done(((bf16[40,80,128]{2,1,0:T(8,128)(2,1)}), bf16[40,640,128]{2,1,0:T(8,128)(2,1)}) %all-gather.7.cloned.1.call-update) | async-done | bytes 6553616 | tf_op jit(solution)/shard_map/all_gather | solution.py:145
  180.4 9.5 copy.66
  189.8 82.3 %all-gather.11.cloned.1.call-done = bf16[40,640,128]{2,1,0:T(8,128)(2,1)} async-done(((bf16[40,80,128]{2,1,0:T(8,128)(2,1)}), bf16[40,640,128]{2,1,0:T(8,128)(2,1)}) %all-gather.11.cloned.1.call-update) | async-done | bytes 6553616 | tf_op jit(solution)/shard_map/all_gather | solution.py:146
  272.1 9.5 copy.70
  283.8 88.0 %while.24 = (s32[]{:T(128)}, f32[20,2,80,4]{2,3,1,0:T(4,128)S(1)}, f32[20,2,80,4,32]{2,1,0,4,3:T(2,128)}, pred[640]{0:T(1024)(128)(4,1)S(1)}, bf16[20,2,640,4,32...) while((s32[]{:T(128)}, f32[20,2,80,4]{2,3,1,0:T(4,128)S(1)}, ...), condition=%wide.region_5.6_spmd, body=%wide.region_2.5_spmd.sunk | while | flops 56753280 | bytes 8076525 | solution.py:113
  394.3 20.5 %all_gather.29 = bf16[80,4,640]{0,1,2:T(4,128)(2,1)S(1)} all-gather(bf16[80,4,40]{0,1,2:T(4,128)(2,1)S(1)} %fusion.44), channel_id=1, replica_groups=mesh['row'=16,'col'=8] {'row'}, dimensions={2}, use_global_device_ids=true | all-gather | bytes 435200 | tf_op jit(solution)/shard_map/all_gather | solution.py:170
  422.7 54.5 %all-gather.15.cloned.1.call-done = bf16[640,4,640]{2,1,0:T(4,128)(2,1)} async-done(((bf16[80,4,640]{2,1,0:T(4,128)(2,1)}), bf16[640,4,640]{2,1,0:T(4,128)(2,1)}) %all-gather.15.cloned.1.call-update) | async-done | bytes 3276816 | tf_op jit(solution)/shard_map/all_gather | solution.py:172
  478.9 73.2 %all-gather.13.cloned.1.call-done = bf16[640,80,128]{2,1,0:T(8,128)(2,1)} async-done(((bf16[40,80,128]{2,1,0:T(8,128)(2,1)}), bf16[640,80,128]{2,1,0:T(8,128)(2,1)}) %all-gather.13.cloned.1.call-update) | async-done | bytes 13107216 | tf_op jit(solution)/shard_map/all_gather | solution.py:183
  552.1 20.4 %copy.80 = bf16[640,80,128]{0,2,1:T(8,128)(2,1)} copy(bf16[640,80,128]{2,1,0:T(8,128)(2,1)} %all-gather.13.cloned.1.call-done) | data formatting | bytes 26214400 | tf_op jit(solution)/shard_map/all_gather | solution.py:183
  572.6 56.3 %all-gather.17.cloned.1.call-done = bf16[640,80,128]{2,1,0:T(8,128)(2,1)} async-done(((bf16[40,80,128]{2,1,0:T(8,128)(2,1)}), bf16[640,80,128]{2,1,0:T(8,128)(2,1)}) %all-gather.17.cloned.1.call-update) | async-done | bytes 13107216 | tf_op jit(solution)/shard_map/all_gather | solution.py:184
  628.8 21.0 %copy.82 = bf16[640,80,128]{0,2,1:T(8,128)(2,1)} copy(bf16[640,80,128]{2,1,0:T(8,128)(2,1)} %all-gather.17.cloned.1.call-done) | data formatting | bytes 26214400 | tf_op jit(solution)/shard_map/all_gather | solution.py:184
  652.0 395.0 %while.25 = (s32[]{:T(128)}, f32[20,2,80,4]{2,1,0,3:T(2,128)S(1)}, f32[20,2,80,4,32]{2,1,0,4,3:T(2,128)}, pred[640]{0:T(1024)(128)(4,1)S(1)}, bf16[20,2,80,4,32]...) while((s32[]{:T(128)}, f32[20,2,80,4]{2,1,0,3:T(2,128)S(1)}, ...), condition=%wide.region_11.12_spmd, body=%wide.region_8.11_spmd.sunk | while | flops 56552320 | bytes 31912688 | solution.py:113
  653.7 7.3 fusion.107
  663.3 7.4 fusion.109
  673.5 7.3 fusion.107
  683.0 7.4 fusion.109
  693.3 7.3 fusion.107
  702.8 7.4 fusion.109
  722.5 7.4 fusion.109
  732.8 7.3 fusion.107
  742.3 7.4 fusion.109
  752.5 7.3 fusion.107
  762.0 7.4 fusion.109
  781.8 7.4 fusion.109
  801.5 7.4 fusion.109
  811.8 7.3 fusion.107
  821.3 7.4 fusion.109
  841.0 7.4 fusion.109
  851.3 7.3 fusion.107
  860.8 7.4 fusion.109
  871.0 7.3 fusion.107
  880.6 7.4 fusion.109
  890.8 7.3 fusion.107
  900.3 7.4 fusion.109
  920.0 7.4 fusion.109
  930.3 7.3 fusion.107
  939.8 7.4 fusion.109
  950.0 7.3 fusion.107
  959.6 7.4 fusion.109
  969.8 7.3 fusion.107
  979.3 7.4 fusion.109
  999.0 7.4 fusion.109
  1009.3 7.3 fusion.107
  1018.8 7.4 fusion.109
  1029.0 7.3 fusion.107
  1038.5 7.4 fusion.109
  (480 shorter events, 297.8 us)
Async XLA Ops:
  6.5 4.1 copy-start
  6.5 4.0 copy-start.14
  6.5 5.1 copy-start.13
  6.5 80.9 %all-gather.9.cloned.1.call-start = ((), (), s32[]{:S(2)}) async-start(), calls=%async_computation.1 | async-start | bytes 3481600 | tf_op jit(solution)/shard_map/all_gather | solution.py:134
  11.7 38.7 %copy-start.7 = (bf16[2,128,128]{2,1,0:T(8,128)(2,1)S(1)}, bf16[2,128,128]{2,1,0:T(8,128)(2,1)}, u32[]{:S(2)}) copy-start(bf16[2,128,128]{2,1,0:T(8,128)(2,1)} %param.17) | copy-start | bytes 196612
  49.0 2.8 copy-start.8
  50.4 130.0 %all-gather.7.cloned.1.call-start = ((), (), s32[]{:S(2)}) async-start(), calls=%async_computation | async-start | bytes 7372800 | tf_op jit(solution)/shard_map/all_gather | solution.py:145
  51.7 1.6 copy-start.10
  51.7 220.4 %all-gather.11.cloned.1.call-start = ((), (), s32[]{:S(2)}) async-start(), calls=%async_computation.2 | async-start | bytes 7372800 | tf_op jit(solution)/shard_map/all_gather | solution.py:146
  53.0 424.2 %all-gather.15.cloned.1.call-start = ((), (), s32[]{:S(2)}) async-start(), calls=%async_computation.4 | async-start | bytes 3686400 | tf_op jit(solution)/shard_map/all_gather | solution.py:172
  53.7 3.9 copy-start.12
  385.0 2.7 copy-start.15
  387.7 2.7 copy-start.5
  391.4 3.0 copy-start.1
  416.3 1.4 copy-start.9
  416.3 135.8 %all-gather.13.cloned.1.call-start = ((), (), s32[]{:S(2)}) async-start(), calls=%async_computation.3 | async-start | bytes 13926400 | tf_op jit(solution)/shard_map/all_gather | solution.py:183
  417.6 1.4 copy-start.11
  417.6 211.2 %all-gather.17.cloned.1.call-start = ((), (), s32[]{:S(2)}) async-start(), calls=%async_computation.5 | async-start | bytes 13926400 | tf_op jit(solution)/shard_map/all_gather | solution.py:184
  1048.9 2.8 copy-start.3
  1056.3 2.8 copy-start.4
  1056.3 2.8 copy-start.16
  1059.1 2.3 copy-start.2
  1059.1 2.3 copy-start.6
Sparse Core Ops, SparseCore 0:
  50.5 36.8 all-gather.8
  89.8 90.5 all-gather.6
  182.7 89.3 all-gather.10
  416.4 60.7 all-gather.14
  478.8 73.2 all-gather.12
  553.7 75.1 all-gather.16
where the time goes:
time: 1080 us; the launch traced here: 1070 us
  waiting for transfers between devices  388 us (36%)
  matrix products  367 us (34%)
  local copies, waits for them, and re-layouts  177 us (16%)
  other arithmetic  63.7 us (6%)
  blocking collectives  57 us (5%)
  between operations  13.8 us (1%)
    dot_general x40, matrix products, advance(): jnp.einsum(pattern, weights, sources, preferred_element_type=jnp.float32)  177 us
    dot_general x20, matrix products, logits(): jnp.einsum('ijhd,kjhd->ijhk', queries, key_heads, preferred_element_type=...  145 us
    all_gather x1, waiting for transfers between devices, start_section(): lax.all_gather(operand[0], 'col', axis=1, tiled=True)  91.7 us
    all_gather x1, waiting for transfers between devices, start_section(): lax.all_gather(operand[1], 'col', axis=1, tiled=True)  82.3 us
    all_gather x1, waiting for transfers between devices, end_section(): lax.all_gather(operand[0], 'row', axis=0, tiled=True)  73.2 us
    all_gather x1, waiting for transfers between devices, end_section(): lax.all_gather(operand[1], 'row', axis=0, tiled=True)  56.3 us
    all_gather x1, waiting for transfers between devices, end_section(): everything = lax.all_gather(bias_cols, 'col', axis=0, tiled=True)  54.5 us
    reduce_sum x40, other arithmetic, advance(): block_total = block_total * factor + jnp.sum(exponentials, axis=-1)  51.3 us
  transfers between devices with their start and end apart: 6, of which 6 were waited for; matrix products, arithmetic and copies ran while one was open for 4% of the time, Pallas kernels for 0%

commit v1 on v0

v1 whole, which is shorter than its diff:
```python
import functools

import jax
import jax.numpy as jnp
from jax import lax
from jax.experimental import pallas as pl
from jax.experimental.pallas import tpu as pltpu
from jax.sharding import PartitionSpec as P

H = 4
HD = 32
C = 128
N = 640
HALF = N // 2
PART = 40
OWN = 5

epsilon = 1e-05
masked_score = -1e30
LOG2E = 1.4426950408889634
SCALE = HD ** (-0.5) * LOG2E

SAME_CORE = [[core + 2 * place for place in range(8)] for core in range(2)]
PARTNER = [(place, place ^ 1) for place in range(16)]

CONTRACT_LAST = (((1,), (1,)), ((), ()))


def normalize(block, gain_row):
    upcast = block.astype(jnp.float32)
    centred = upcast - jnp.mean(upcast, axis=-1, keepdims=True)
    variance = jnp.mean(centred * centred, axis=-1, keepdims=True)
    return (centred * lax.rsqrt(variance + epsilon) * gain_row).astype(jnp.bfloat16)


def dot(left, right):
    return jnp.dot(left, right, preferred_element_type=jnp.float32)


def head_lanes(rows, head):
    lane = lax.broadcasted_iota(jnp.int32, (rows, C), 1)
    return (lane >= head * HD) & (lane < (head + 1) * HD)


def attend_row(queries_in, others_in, bias_s, gain, w_own, w_other, w_out):
    own = normalize(queries_in, gain)
    other = normalize(others_in, gain)
    own_all = dot(own, w_own)
    other_all = dot(other, w_other)
    queries = own_all[:, :C].astype(jnp.bfloat16).astype(jnp.float32) * SCALE
    gating = jax.nn.sigmoid(own_all[:, C : 2 * C])
    keys = jnp.concatenate([own_all[:, 2 * C : 3 * C], other_all[:, :C]], axis=0).astype(jnp.bfloat16)
    values = jnp.concatenate([own_all[:, 3 * C :], other_all[:, C:]], axis=0).astype(jnp.bfloat16)
    coarse = queries.astype(jnp.bfloat16)
    fine = (queries - coarse.astype(jnp.float32)).astype(jnp.bfloat16)
    both_keys = jnp.concatenate([keys, keys], axis=1)
    summed = None
    for head in range(H):
        lanes = head_lanes(HALF, head)
        zero = jnp.zeros((HALF, C), jnp.bfloat16)
        picked = jnp.concatenate([jnp.where(lanes, coarse, zero), jnp.where(lanes, fine, zero)], axis=1)
        scores = lax.dot_general(picked, both_keys, CONTRACT_LAST, preferred_element_type=jnp.float32)
        scores = scores + bias_s[head]
        highest = jnp.max(scores, axis=-1, keepdims=True)
        weights = jnp.exp2(scores - highest).astype(jnp.bfloat16)
        key_lanes = head_lanes(N, head)
        zeros = jnp.zeros((N, C), jnp.bfloat16)
        ones = jnp.ones((N, C), jnp.bfloat16)
        sources = jnp.concatenate([jnp.where(key_lanes, values, zeros), jnp.where(key_lanes, ones, zeros)], axis=1)
        mixed = dot(weights, sources)
        summed = mixed if summed is None else summed + mixed
    hidden = (summed[:, :C] / summed[:, C:] * gating).astype(jnp.bfloat16)
    return (queries_in.astype(jnp.float32) + dot(hidden, w_out)).astype(jnp.bfloat16)


def start_kernel(
    xa, xs, bias, mask, gain, w_own, w_other, w_out, next_gain, next_bias, out, tile, bias_s
):
    @pl.when(pl.program_id(0) == 0)
    def _():
        for head in range(H):
            for place in range(8):
                bias_s[head, place * PART : (place + 1) * PART, :] = (
                    bias[place, head].astype(jnp.float32) * LOG2E + mask[...]
                )

    for slot, source in enumerate((xa, xs)):
        after = attend_row(
            source[slot, 0], source[1 - slot, 0], bias_s, gain[...], w_own[...], w_other[...], w_out[...]
        )
        out[slot, 0] = after
        normed = normalize(after, next_gain[...])
        tile[slot, 0] = lax.dot_general(
            next_bias[...], normed, CONTRACT_LAST, preferred_element_type=jnp.float32
        )


def end_kernel(xa, xs, bias, mask, gain, w_own, w_other, w_out, out, bias_s, turned_s):
    @pl.when(pl.program_id(0) == 0)
    def _():
        row = lax.broadcasted_iota(jnp.int32, (HALF, HALF), 0)
        col = lax.broadcasted_iota(jnp.int32, (HALF, HALF), 1)
        identity = jnp.where(row == col, 1.0, 0.0).astype(jnp.bfloat16)
        for head in range(H):
            for side in range(2):
                for place in range(8):
                    first = side * HALF + place * PART
                    turned_s[first : first + PART, :] = bias[place, head, side].astype(jnp.float32)
            turned = lax.dot_general(
                identity,
                turned_s[...].astype(jnp.bfloat16),
                CONTRACT_LAST,
                preferred_element_type=jnp.float32,
            )
            bias_s[head] = turned * LOG2E + mask[...]

    for slot, source in enumerate((xa, xs)):
        out[slot, 0] = attend_row(
            source[slot, 0], source[1 - slot, 0], bias_s, gain[...], w_own[...], w_other[...], w_out[...]
        )


def whole(array):
    return pl.BlockSpec(array.shape, lambda step: (0,) * array.ndim)


def attend(xa, xs, bias, mask, gain, w_own, w_other, w_out, following):
    rows = pl.BlockSpec((2, 1, HALF, C), lambda step: (0, step, 0, 0))
    out_shape = [jax.ShapeDtypeStruct((2, OWN, HALF, C), jnp.bfloat16)]
    out_specs = [rows]
    scratch = [pltpu.VMEM((H, HALF, N), jnp.float32)]
    operands = [bias, mask, gain, w_own, w_other, w_out]
    if following is None:
        kernel = end_kernel
        scratch.append(pltpu.VMEM((N, HALF), jnp.float32))
    else:
        kernel = start_kernel
        operands += following
        out_shape.append(jax.ShapeDtypeStruct((2, OWN, 8, HALF), jnp.float32))
        out_specs.append(pl.BlockSpec((2, 1, 8, HALF), lambda step: (0, step, 0, 0)))
    return pl.pallas_call(
        kernel,
        grid=(OWN,),
        in_specs=[rows, rows] + [whole(member) for member in operands],
        out_specs=out_specs,
        out_shape=out_shape,
        scratch_shapes=scratch,
        compiler_params=pltpu.CompilerParams(vmem_limit_bytes=56 * 1024 * 1024),
    )(xa, xs, *operands)


def by_core(array, axis, core):
    return jnp.where(core == 1, jnp.flip(array, axis), array)


def gather(array, axis, groups=None):
    copies = jnp.broadcast_to(array[None], (8,) + array.shape)
    return lax.all_to_all(copies, axis, 0, 0, axis_index_groups=groups)


def body(pair_input, token_mask, ln_gain, w_query, w_key, w_value, w_gate, w_bias, w_out):
    core = lax.axis_index("row") % 2
    mask_row = jnp.where(token_mask > 0, 0.0, masked_score).astype(jnp.float32)
    mask_row = by_core(mask_row.reshape(8, 2, PART), 1, core).transpose(1, 0, 2).reshape(1, N)
    w_own = jnp.concatenate([w_query, w_gate, w_key, w_value], axis=2)
    w_other = jnp.concatenate([w_key, w_value], axis=2)
    next_bias = jnp.pad(w_bias[1].T, ((0, 4), (0, 0)))

    halves = by_core(pair_input.reshape(PART, 2, PART, C), 1, core)
    normed = normalize(halves, ln_gain[0])
    tile = jnp.einsum("jskc,ch->hjsk", normed, w_bias[0], preferred_element_type=jnp.float32)
    tile = gather(tile.astype(jnp.bfloat16), "col")
    tile = tile.transpose(1, 2, 3, 0, 4).reshape(H, PART, N)
    bias = gather(tile, "row", SAME_CORE)
    xa = lax.all_to_all(halves.transpose(1, 0, 2, 3), "col", 1, 2, tiled=True)
    xs = lax.ppermute(xa, "row", PARTNER)
    after, tile = attend(
        xa,
        xs,
        bias,
        mask_row,
        ln_gain[0:1],
        w_own[0],
        w_other[0],
        w_out[0],
        [ln_gain[1:2], next_bias],
    )

    tile = tile[:, :, :H].transpose(2, 0, 1, 3).astype(jnp.bfloat16)
    tile = gather(tile, "col").transpose(1, 2, 0, 3, 4).reshape(H, 2, PART, HALF)
    bias = gather(tile, "row", SAME_CORE)
    block = lax.all_to_all(after.reshape(2, OWN, 8, PART, C), "col", 2, 1, tiled=True)
    block = block.reshape(2, PART, PART, C).transpose(0, 2, 1, 3)
    pieces = block.reshape(2, 8, OWN, PART, C)
    xa = lax.all_to_all(pieces, "row", 1, 3, axis_index_groups=SAME_CORE, tiled=True)
    xa = xa.reshape(2, OWN, HALF, C)
    xs = lax.ppermute(xa, "row", PARTNER)
    (after,) = attend(
        xa, xs, bias, mask_row, ln_gain[1:2], w_own[1], w_other[1], w_out[1], None
    )
    pieces = after.reshape(2, OWN, 8, PART, C)
    block = lax.all_to_all(pieces, "row", 2, 1, axis_index_groups=SAME_CORE, tiled=True)
    block = by_core(block.reshape(2, PART, PART, C), 0, core)
    return block.transpose(2, 0, 1, 3).reshape(PART, 2 * PART, C)


def solution(mesh):
    placed = (P("row", "col", None), P(), P(), P(), P(), P(), P(), P(), P())
    return jax.shard_map(
        body, mesh=mesh, in_specs=placed, out_specs=P("row", "col", None), check_vma=False
    )
```

time: 1080 us -> 230 us (0.21)
  matrix products: 367 us -> 2.25 us
  waiting for transfers between devices: 388 us -> 77.8 us
  local copies, waits for them, and re-layouts: 177 us -> 27.1 us
  other arithmetic: 63.7 us -> 5.06 us
  Pallas kernels: 0 us -> 54.8 us
  starting transfers between devices: 0.39 us -> 27.7 us
  blocking collectives: 57 us -> 33 us
  between operations: 13.8 us -> 0.29 us
    all_gather x6 -> x0, waiting for transfers between devices: 388 us -> none  [the longest x1 91.7 us: start_section(): lax.all_gather(operand[0], 'col', axis=1, tiled=True)]
    dot_general x92 -> x1, matrix products: 367 us -> 2.25 us  [body(): jnp.einsum('jskc,ch->hjsk', normed, w_bias[0], preferred_element_type=jnp...]
    all_to_all x0 -> x6, waiting for transfers between devices: none -> 77.8 us  [the longest x3 43.1 us: gather(): return lax.all_to_all(copies, axis, 0, 0, axis_index_groups=groups)]
    all_gather x6 -> x0, local copies, waits for them, and re-layouts: 63.3 us -> none  [the longest x1 21 us: end_section(): lax.all_gather(operand[1], 'row', axis=0, tiled=True)]
    all_gather x2 -> x0, blocking collectives: 57 us -> none  [the longest x1 36.5 us: start_section(): bias_rows = lax.all_gather(bias_tile, 'col', axis=2, tiled=True)]
    pallas_call x0 -> x2, Pallas kernels: none -> 54.8 us  [attend(): pl.pallas_call(kernel, grid=(OWN,), in_specs=[rows, rows] + [whole(member...]
    reduce_sum x40 -> x0, other arithmetic: 51.3 us -> none  [advance(): block_total = block_total * factor + jnp.sum(exponentials, axis=-1)]
    dynamic_slice x82 -> x0, local copies, waits for them, and re-layouts: 39 us -> none  [the longest x80 36.1 us: online_step(): lax.map(advance, (split_blocks(queries, blocks), blocked_rows, split_bloc...]
  transfers between devices with their start and end apart: 6 -> 8, of which waited for: 6 -> 6; matrix products, arithmetic and copies ran while one was open for 4% -> 6% of each run, Pallas kernels for 0% -> 0%
where the time goes in v1:
time: 230 us; the launch traced here: 228 us
  waiting for transfers between devices  77.8 us (34%)
  Pallas kernels  54.8 us (24%)
  blocking collectives  33 us (14%)
  starting transfers between devices  27.7 us (12%)
  local copies, waits for them, and re-layouts  27.1 us (12%)
  other arithmetic  5.06 us (2%)
    pallas_call x2, Pallas kernels, attend(): pl.pallas_call(kernel, grid=(OWN,), in_specs=[rows, rows] + [whole(member...  54.8 us
    all_to_all x3, waiting for transfers between devices, gather(): return lax.all_to_all(copies, axis, 0, 0, axis_index_groups=groups)  43.1 us
    all_to_all x1, blocking collectives, body(): lax.all_to_all(pieces, 'row', 2, 1, axis_index_groups=SAME_CORE, tiled=True)  17.6 us
    all_to_all x1, blocking collectives, gather(): return lax.all_to_all(copies, axis, 0, 0, axis_index_groups=groups)  15.3 us
    all_to_all x3, starting transfers between devices, gather(): return lax.all_to_all(copies, axis, 0, 0, axis_index_groups=groups)  13 us
    all_to_all x1, waiting for transfers between devices, body(): lax.all_to_all(after.reshape(2, OWN, 8, PART, C), 'col', 2, 1, tiled=True)  12.8 us
    all_to_all x1, waiting for transfers between devices, body(): lax.all_to_all(pieces, 'row', 1, 3, axis_index_groups=SAME_CORE, tiled=True)  12 us
    all_to_all x1, waiting for transfers between devices, body(): xa = lax.all_to_all(halves.transpose(1, 0, 2, 3), 'col', 1, 2, tiled=True)  9.94 us
  transfers between devices with their start and end apart: 8, of which 6 were waited for; matrix products, arithmetic and copies ran while one was open for 6% of the time, Pallas kernels for 0%

profile of v1, /device:TPU:8, one launch (start us, length us, event | category | flops | bytes accessed | tf_op | source)
XLA Modules:
  0.0 227.8 jit_solution(5393819102803030531)
XLA Ops:
  0.0 1.3 fusion.12
  1.3 2.7 %convert_reduce_fusion = (f32[40,2,40]{2,1,0:T(2,128)S(1)}, bf16[40,2,40,128]{3,2,1,0:T(8,128)(2,1)}) fusion(bf16[40,2,40,128]{3,2,1,0:T(8,128)(2,1)} %bitcast.78, pred[]{:T(512)S(6)} %eq.4), kind=kLoop, calls=%fused_computation.1 | loop fusion | flops 1225600 | bytes 1651201 | tf_op jit(solution)/shard_map/reduce_sum | solution.py:31
  4.1 2.1 fusion.2
  6.3 2.3 fusion.5
  8.6 0.3 broadcast_in_dim.36
  9.0 1.0 reshape.61
  10.0 15.3 %all_to_all.83 = bf16[8,2,6400]{2,1,0:T(2,128)(2,1)S(1)} all-to-all(bf16[8,2,6400]{2,1,0:T(2,128)(2,1)S(1)} %reshape.61), channel_id=1, replica_groups=mesh['row'=16,'col'=8] {'col'}, dimensions={0} | all-to-all | bytes 409600 | tf_op jit(solution)/shard_map/all_to_all | solution.py:158
  25.3 4.6 %all-to-all-start = ((bf16[2,40,40,128]{3,2,0,1:T(8,128)(2,1)}), bf16[2,40,40,128]{3,2,0,1:T(8,128)(2,1)S(1)}, u32[]{:S(2)}, u32[]{:S(2)}) async-start(bf16[2,40,40,128]{3,2,0,1:T(8,128)(2,1)} %bitcast.1), calls=%async_computation | async-start | bytes 1638400 | tf_op jit(solution)/shard_map/all_to_all | solution.py:175
  30.1 1.0 reshape.62
  31.2 0.8 copy.39
  31.9 0.6 broadcast_in_dim.37
  32.6 9.9 %all-to-all-done = bf16[2,40,40,128]{3,2,0,1:T(8,128)(2,1)S(1)} async-done(((bf16[2,40,40,128]{3,2,0,1:T(8,128)(2,1)}), bf16[2,40,40,128]{3,2,0,1:T(8,128)(2,1)S(1)}, u32[]{:S(2)}, u32[]{:S(2)}) %all-to-all-start) | async-done | bytes 819232 | tf_op jit(solution)/shard_map/all_to_all | solution.py:175
  42.5 1.3 broadcast_in_dim.38
  43.9 4.9 %all-to-all-start.2 = ((bf16[8,4,40,640]{3,2,1,0:T(8,128)(2,1)}), bf16[8,4,40,640]{3,2,1,0:T(8,128)(2,1)S(1)}, u32[]{:S(2)}, u32[]{:S(2)}) async-start(bf16[8,4,40,640]{3,2,1,0:T(8,128)(2,1)} %broadcast_in_dim.38), calls=%async_computation.2 | async-start | bytes 3276800 | tf_op jit(solution)/shard_map/all_to_all | solution.py:158
  48.9 0.3 collective-permute-start
  49.2 0.4 copy-done.6
  49.6 0.7 constant_dynamic-update-slice_fusion.5
  50.3 0.7 reshape.52.mask
  50.9 0.6 pad.4.next_bias
  51.5 1.5 constant_dynamic-update-slice_fusion.4
  53.0 1.4 slice_bitcast_fusion.4
  54.4 1.5 slice_bitcast_fusion.2
  55.9 0.7 slice_bitcast_fusion
  56.7 12.6 %all-to-all-done.2.bias = bf16[8,4,40,640]{3,2,1,0:T(8,128)(2,1)S(1)} async-done(((bf16[8,4,40,640]{3,2,1,0:T(8,128)(2,1)}), bf16[8,4,40,640]{3,2,1,0:T(8,128)(2,1)S(1)}, u32[]{:S(2)}, u32[]{:S(2)}) %all-to-all-start.2) | async-done | bytes 1638432 | tf_op jit(solution)/shard_map/all_to_all | solution.py:158
  69.3 1.2 copy-done.1
  70.5 28.5 %shard_map.91 = (bf16[2,5,320,128]{3,2,1,0:T(8,128)(2,1)}, f32[2,5,8,320]{3,2,1,0:T(8,128)}) custom-call(bf16[2,5,320,128]{3,2,1,0:T(8,128)(2,1)} %bitcast.68, bf16[2,5,320,128]{3,2,1,0:T(8,128)(2,1)} %copy-done.5, bf16[8,4,40,640]{3,2,1,0:T(8,128)(2,1)} %copy-done.1, f32[1,640]{1,0:T(1,128)} %reshape.52.mask, f32[1,128]{1,0:T(1,128)} %get-tuple-element.23.gain, ...), custom_call_target="tpu_custom_call" | custom-call | tf_op jit(solution)/shard_map/pallas_call | solution.py:141
  99.0 2.1 copy.41
  101.1 5.9 %all-to-all-start.3 = ((bf16[2,5,8,40,128]{4,3,1,0,2:T(8,128)(2,1)}), bf16[2,5,8,40,128]{4,3,1,0,2:T(8,128)(2,1)S(1)}, u32[]{:S(2)}, u32[]{:S(2)}) async-start(bf16[2,5,8,40,128]{4,3,1,0,2:T(8,128)(2,1)} %copy.41), calls=%async_computation.3 | async-start | bytes 1638400 | tf_op jit(solution)/shard_map/all_to_all | solution.py:192
  107.1 0.9 fusion.9
  108.0 12.8 %all-to-all-done.3 = bf16[2,5,8,40,128]{4,3,1,0,2:T(8,128)(2,1)S(1)} async-done(((bf16[2,5,8,40,128]{4,3,1,0,2:T(8,128)(2,1)}), bf16[2,5,8,40,128]{4,3,1,0,2:T(8,128)(2,1)S(1)}, u32[]{:S(2)}, u32[]{:S(2)}) %all-to-all-start.3) | async-done | bytes 819232 | tf_op jit(solution)/shard_map/all_to_all | solution.py:192
  120.8 0.8 broadcast_in_dim.41
  121.6 4.5 %all-to-all-start.5 = ((bf16[8,4,2,5,320]{4,2,3,1,0:T(2,128)(2,1)}), bf16[8,4,2,5,320]{4,2,3,1,0:T(2,128)(2,1)S(1)}, u32[]{:S(2)}, u32[]{:S(2)}) async-start(bf16[8,4,2,5,320]{4,2,3,1,0:T(2,128)(2,1)} %broadcast_in_dim.41), calls=%async_computation.5 | async-start | bytes 491520 | tf_op jit(solution)/shard_map/all_to_all | solution.py:158
  126.3 1.0 copy.44
  127.2 6.4 %all-to-all-done.5 = bf16[8,4,2,5,320]{4,2,3,1,0:T(2,128)(2,1)S(1)} async-done(((bf16[8,4,2,5,320]{4,2,3,1,0:T(2,128)(2,1)}), bf16[8,4,2,5,320]{4,2,3,1,0:T(2,128)(2,1)S(1)}, u32[]{:S(2)}, u32[]{:S(2)}) %all-to-all-start.5) | async-done | bytes 204832 | tf_op jit(solution)/shard_map/all_to_all | solution.py:158
  133.7 3.5 %all-to-all-start.4 = ((bf16[2,8,5,40,128]{4,3,2,0,1:T(8,128)(2,1)}), bf16[2,8,5,40,128]{4,3,2,0,1:T(8,128)(2,1)S(1)}, u32[]{:S(2)}, u32[]{:S(2)}) async-start(bf16[2,8,5,40,128]{4,3,2,0,1:T(8,128)(2,1)} %copy.44), calls=%async_computation.4 | async-start | bytes 1638400 | tf_op jit(solution)/shard_map/all_to_all | solution.py:195
  137.2 0.2 copy.47
  137.5 12.0 %all-to-all-done.4 = bf16[2,8,5,40,128]{4,3,2,0,1:T(8,128)(2,1)S(1)} async-done(((bf16[2,8,5,40,128]{4,3,2,0,1:T(8,128)(2,1)}), bf16[2,8,5,40,128]{4,3,2,0,1:T(8,128)(2,1)S(1)}, u32[]{:S(2)}, u32[]{:S(2)}) %all-to-all-start.4) | async-done | bytes 819232 | tf_op jit(solution)/shard_map/all_to_all | solution.py:195
  149.4 1.6 broadcast_in_dim.43
  151.0 3.6 %all-to-all-start.6 = ((bf16[8,4,2,40,320]{4,3,2,1,0:T(8,128)(2,1)}), bf16[8,4,2,40,320]{4,3,2,1,0:T(8,128)(2,1)S(1)}, u32[]{:S(2)}, u32[]{:S(2)}) async-start(bf16[8,4,2,40,320]{4,3,2,1,0:T(8,128)(2,1)} %broadcast_in_dim.43), calls=%async_computation.6 | async-start | bytes 3932160 | tf_op jit(solution)/shard_map/all_to_all | solution.py:158
  154.6 1.2 copy.45
  155.9 0.3 collective-permute-start.1
  156.2 24.0 %all-to-all-done.6.bias = bf16[8,4,2,40,320]{4,3,2,1,0:T(8,128)(2,1)S(1)} async-done(((bf16[8,4,2,40,320]{4,3,2,1,0:T(8,128)(2,1)}), bf16[8,4,2,40,320]{4,3,2,1,0:T(8,128)(2,1)S(1)}, u32[]{:S(2)}, u32[]{:S(2)}) %all-to-all-start.6) | async-done | bytes 1638432 | tf_op jit(solution)/shard_map/all_to_all | solution.py:158
  180.2 1.3 copy-done
  181.5 26.2 %shard_map.92 = bf16[2,5,320,128]{3,2,1,0:T(8,128)(2,1)} custom-call(bf16[2,5,320,128]{3,2,1,0:T(8,128)(2,1)} %bitcast.65, bf16[2,5,320,128]{3,2,1,0:T(8,128)(2,1)} %collective-permute-done.1.xs, bf16[8,4,2,40,320]{4,3,2,1,0:T(8,128)(2,1)} %copy-done, f32[1,640]{1,0:T(1,128)} %reshape.52.mask, f32[1,128]{1,0:T(1,128)} %get-tuple-element.21.next_gain.gain, ...), custom_call_target="tpu_custom_call" | custom-call | tf_op jit(solution)/shard_map/pallas_call | solution.py:141
  207.7 1.2 copy.49
  209.0 17.6 %all_to_all.84 = bf16[2,5,8,40,128]{4,3,1,0,2:T(8,128)(2,1)S(1)} all-to-all(bf16[2,5,8,40,128]{4,3,1,0,2:T(8,128)(2,1)S(1)} %copy.49), channel_id=1, replica_groups={{0,16,32,48,64,80,96,112},{8,24,40,56,72,88,104,120},{1,17,33,49,65,81,..., dimensions={2} | all-to-all | bytes 1638400 | tf_op jit(solution)/shard_map/all_to_all | solution.py:202
  226.7 0.2 reverse_select_fusion
  226.8 1.0 copy.51
  (38 shorter events, 0.7 us)
Async XLA Ops:
  0.0 6.2 %copy-start.10 = (bf16[2,128,4]{1,2,0:T(4,128)(2,1)S(1)}, bf16[2,128,4]{1,2,0:T(4,128)(2,1)}, u32[]{:S(2)}) copy-start(bf16[2,128,4]{1,2,0:T(4,128)(2,1)} %param.16) | copy-start | bytes 6148
  8.9 21.0 %copy-start.9 = (s32[640]{0:T(1024)S(1)}, s32[640]{0:T(1024)}, u32[]{:S(2)}) copy-start(s32[640]{0:T(1024)} %param.10) | copy-start | bytes 7684
  9.0 21.1 %copy-start.7 = (bf16[2,128,128]{2,1,0:T(8,128)(2,1)S(1)}, bf16[2,128,128]{2,1,0:T(8,128)(2,1)}, u32[]{:S(2)}) copy-start(bf16[2,128,128]{2,1,0:T(8,128)(2,1)} %param.12) | copy-start | bytes 196612
  25.3 17.2 %all-to-all-start = ((bf16[2,40,40,128]{3,2,0,1:T(8,128)(2,1)}), bf16[2,40,40,128]{3,2,0,1:T(8,128)(2,1)S(1)}, u32[]{:S(2)}, u32[]{:S(2)}) async-start(bf16[2,40,40,128]{3,2,0,1:T(8,128)(2,1)} %bitcast.1), calls=%async_computation | async-start | bytes 1638400 | tf_op jit(solution)/shard_map/all_to_all | solution.py:175
  43.9 4.9 %copy-start.8 = (bf16[2,128,128]{2,1,0:T(8,128)(2,1)S(1)}, bf16[2,128,128]{2,1,0:T(8,128)(2,1)}, u32[]{:S(2)}) copy-start(bf16[2,128,128]{2,1,0:T(8,128)(2,1)} %param.15) | copy-start | bytes 196612
  43.9 25.4 %all-to-all-start.2 = ((bf16[8,4,40,640]{3,2,1,0:T(8,128)(2,1)}), bf16[8,4,40,640]{3,2,1,0:T(8,128)(2,1)S(1)}, u32[]{:S(2)}, u32[]{:S(2)}) async-start(bf16[8,4,40,640]{3,2,1,0:T(8,128)(2,1)} %broadcast_in_dim.38), calls=%async_computation.2 | async-start | bytes 3276800 | tf_op jit(solution)/shard_map/all_to_all | solution.py:158
  48.8 0.8 copy-start.6
  48.9 20.4 %copy-start.3 = (bf16[2,8,5,40,128]{4,3,1,2,0:T(8,128)(2,1)}, bf16[2,8,5,40,128]{4,3,1,2,0:T(8,128)(2,1)S(1)}, u32[]{:S(2)}) copy-start(bf16[2,8,5,40,128]{4,3,1,2,0:T(8,128)(2,1)S(1)} %copy.37) | copy-start | bytes 2457604
  48.9 7.7 %collective-permute-start = (bf16[2,5,320,128]{3,2,1,0:T(8,128)(2,1)S(1)}, bf16[2,5,320,128]{3,2,1,0:T(8,128)(2,1)S(1)}, u32[]{:S(2)}, u32[]{:S(2)}) collective-permute-start(bf16[2,5,320,128]{3,2,1,0:T(8,128)(2,1)S(1)} %bitcast.67), channel_id=1, source_target_pairs={{0,8},{8,0},{16,24},{24,16},{32,40},{40,32},{48,56},{56,48},{64,72... | collective-permute-start | bytes 2457608 | tf_op jit(solution)/shard_map/ppermute | solution.py:176
  56.7 12.6 %copy-start.5 = (bf16[2,5,320,128]{3,2,1,0:T(8,128)(2,1)}, bf16[2,5,320,128]{3,2,1,0:T(8,128)(2,1)S(1)}, u32[]{:S(2)}) copy-start(bf16[2,5,320,128]{3,2,1,0:T(8,128)(2,1)S(1)} %collective-permute-done.xs) | copy-start | bytes 2457604
  69.3 1.2 copy-start.1
  101.1 19.7 %all-to-all-start.3 = ((bf16[2,5,8,40,128]{4,3,1,0,2:T(8,128)(2,1)}), bf16[2,5,8,40,128]{4,3,1,0,2:T(8,128)(2,1)S(1)}, u32[]{:S(2)}, u32[]{:S(2)}) async-start(bf16[2,5,8,40,128]{4,3,1,0,2:T(8,128)(2,1)} %copy.41), calls=%async_computation.3 | async-start | bytes 1638400 | tf_op jit(solution)/shard_map/all_to_all | solution.py:192
  121.6 12.1 %all-to-all-start.5 = ((bf16[8,4,2,5,320]{4,2,3,1,0:T(2,128)(2,1)}), bf16[8,4,2,5,320]{4,2,3,1,0:T(2,128)(2,1)S(1)}, u32[]{:S(2)}, u32[]{:S(2)}) async-start(bf16[8,4,2,5,320]{4,2,3,1,0:T(2,128)(2,1)} %broadcast_in_dim.41), calls=%async_computation.5 | async-start | bytes 491520 | tf_op jit(solution)/shard_map/all_to_all | solution.py:158
  133.7 15.8 %all-to-all-start.4 = ((bf16[2,8,5,40,128]{4,3,2,0,1:T(8,128)(2,1)}), bf16[2,8,5,40,128]{4,3,2,0,1:T(8,128)(2,1)S(1)}, u32[]{:S(2)}, u32[]{:S(2)}) async-start(bf16[2,8,5,40,128]{4,3,2,0,1:T(8,128)(2,1)} %copy.44), calls=%async_computation.4 | async-start | bytes 1638400 | tf_op jit(solution)/shard_map/all_to_all | solution.py:195
  149.4 1.6 copy-start.4
  151.0 29.2 %all-to-all-start.6 = ((bf16[8,4,2,40,320]{4,3,2,1,0:T(8,128)(2,1)}), bf16[8,4,2,40,320]{4,3,2,1,0:T(8,128)(2,1)S(1)}, u32[]{:S(2)}, u32[]{:S(2)}) async-start(bf16[8,4,2,40,320]{4,3,2,1,0:T(8,128)(2,1)} %broadcast_in_dim.43), calls=%async_computation.6 | async-start | bytes 3932160 | tf_op jit(solution)/shard_map/all_to_all | solution.py:158
  155.9 24.3 %copy-start.2 = (bf16[2,1,5,8,40,128]{5,4,3,2,0,1:T(8,128)(2,1)}, bf16[2,1,5,8,40,128]{5,4,3,2,0,1:T(8,128)(2,1)S(1)}, u32[]{:S(2)}) copy-start(bf16[2,1,5,8,40,128]{5,4,3,2,0,1:T(8,128)(2,1)S(1)} %copy.45) | copy-start | bytes 2457604
  155.9 24.3 %collective-permute-start.1 = (bf16[2,5,320,128]{3,2,1,0:T(8,128)(2,1)S(1)}, bf16[2,5,320,128]{3,2,1,0:T(8,128)(2,1)}, u32[]{:S(2)}, u32[]{:S(2)}) collective-permute-start(bf16[2,5,320,128]{3,2,1,0:T(8,128)(2,1)S(1)} %bitcast.64), channel_id=1, source_target_pairs={{0,8},{8,0},{16,24},{24,16},{32,40},{40,32},{48,56},{56,48},{64,72... | collective-permute-start | bytes 2457608 | tf_op jit(solution)/shard_map/ppermute | solution.py:197
  180.2 1.3 copy-start

commit v2 on v1

v2 whole, which is shorter than its diff:
```python
import functools

import jax
import jax.numpy as jnp
from jax import lax
from jax.experimental import pallas as pl
from jax.experimental.pallas import tpu as pltpu
from jax.sharding import PartitionSpec as P

H = 4
HD = 32
C = 128
N = 640
HALF = N // 2
PART = 40
OWN = 5

epsilon = 1e-05
masked_score = -1e30
LOG2E = 1.4426950408889634
SCALE = HD ** (-0.5) * LOG2E

SAME_CORE = [[core + 2 * place for place in range(8)] for core in range(2)]
CORE_PLANES = [
    [(core + 2 * place) * 8 + column for place in range(8) for column in range(8)]
    for core in range(2)
]
PARTNER = [(place, place ^ 1) for place in range(16)]

CHUNKS = N // C
VMEM = 30 * 1024 * 1024
CONTRACT_LAST = (((1,), (1,)), ((), ()))


def normalize(upcast, gain_row):
    centred = upcast - jnp.mean(upcast, axis=-1, keepdims=True)
    variance = jnp.mean(centred * centred, axis=-1, keepdims=True)
    return (centred * lax.rsqrt(variance + epsilon) * gain_row).astype(jnp.bfloat16)


def dot(left, right):
    return jnp.dot(left, right, preferred_element_type=jnp.float32)


def head_lanes(rows, head):
    lane = lax.broadcasted_iota(jnp.int32, (rows, C), 1)
    return (lane >= head * HD) & (lane < (head + 1) * HD)


def attend_row(queries_in, others_in, bias_s, gain, w_query, w_key, w_value, w_gate, w_out):
    own = normalize(queries_in, gain)
    other = normalize(others_in, gain)
    own_all = dot(own, jnp.concatenate([w_query, w_gate, w_key, w_value], axis=1))
    other_all = dot(other, jnp.concatenate([w_key, w_value], axis=1))
    queries = own_all[:, :C].astype(jnp.bfloat16).astype(jnp.float32) * SCALE
    gating = jax.nn.sigmoid(own_all[:, C : 2 * C])
    keys = jnp.concatenate([own_all[:, 2 * C : 3 * C], other_all[:, :C]], axis=0).astype(jnp.bfloat16)
    values = jnp.concatenate([own_all[:, 3 * C :], other_all[:, C:]], axis=0).astype(jnp.bfloat16)
    coarse = queries.astype(jnp.bfloat16)
    fine = (queries - coarse.astype(jnp.float32)).astype(jnp.bfloat16)
    both_queries = jnp.concatenate([coarse, fine], axis=1)
    zeros = jnp.zeros((N, C), jnp.bfloat16)
    ones = jnp.ones((N, C), jnp.bfloat16)
    head_keys, head_sources = [], []
    for head in range(H):
        lanes = head_lanes(N, head)
        picked = jnp.where(lanes, keys, zeros)
        head_keys.append(jnp.concatenate([picked, picked], axis=1))
        head_sources.append(
            jnp.concatenate([jnp.where(lanes, values, zeros), jnp.where(lanes, ones, zeros)], axis=1)
        )
    all_scores = lax.dot_general(
        both_queries,
        jnp.concatenate(head_keys, axis=0),
        CONTRACT_LAST,
        preferred_element_type=jnp.float32,
    )
    head_weights = []
    for head in range(H):
        scores = all_scores[:, head * N : (head + 1) * N] + bias_s[head]
        highest = jnp.max(scores, axis=-1, keepdims=True)
        head_weights.append(jnp.exp2(scores - highest).astype(jnp.bfloat16))
    summed = dot(jnp.concatenate(head_weights, axis=1), jnp.concatenate(head_sources, axis=0))
    hidden = (summed[:, :C] / summed[:, C:] * gating).astype(jnp.bfloat16)
    return (queries_in + dot(hidden, w_out)).astype(jnp.bfloat16).astype(jnp.float32)


def start_kernel(own_q, own_o, far_q, far_o, mask, gain, next_bias, *rest):
    weights, bias = rest[:2]
    out, tile, bias_s = rest[2:]

    @pl.when(pl.program_id(0) == 0)
    def _():
        for place in range(8):
            for head in range(H):
                for part in range(CHUNKS):
                    lanes = slice(part * C, (part + 1) * C)
                    bias_s[head, place * PART : (place + 1) * PART, lanes] = (
                        bias[place, head, part].astype(jnp.float32) * LOG2E + mask[:, lanes]
                    )

    for slot, (queries, others) in enumerate(((own_q, own_o), (far_q, far_o))):
        after = attend_row(
            merged(queries), merged(others), bias_s, gain[0:1], *(weights[position] for position in range(5))
        )
        out[:, 0, slot] = after.reshape(8, PART, C).astype(jnp.bfloat16)
        normed = normalize(after, gain[1:2])
        tile[slot, 0] = lax.dot_general(
            next_bias[1], normed, CONTRACT_LAST, preferred_element_type=jnp.float32
        )


def end_kernel(own_q, own_o, far_q, far_o, mask, gain, *rest):
    weights, bias = rest[:2]
    out, bias_s, turned_s = rest[2:]

    @pl.when(pl.program_id(0) == 0)
    def _():
        row = lax.broadcasted_iota(jnp.int32, (HALF, 2 * HALF), 0)
        col = lax.broadcasted_iota(jnp.int32, (HALF, 2 * HALF), 1)
        for pair in range(2):
            for place in range(8):
                for side in range(2):
                    first = side * HALF + place * PART
                    for part in range(CHUNKS):
                        turned_s[pair, first : first + PART, part * C : (part + 1) * C] = bias[
                            place, pair, side, part
                        ].astype(jnp.float32)
        for head in range(H):
            chosen = jnp.where(row + (head % 2) * HALF == col, 1.0, 0.0).astype(jnp.bfloat16)
            turned = lax.dot_general(
                chosen,
                turned_s[head // 2].astype(jnp.bfloat16),
                CONTRACT_LAST,
                preferred_element_type=jnp.float32,
            )
            bias_s[head] = turned * LOG2E + mask[...]

    for slot, (queries, others) in enumerate(((own_q, own_o), (far_q, far_o))):
        after = attend_row(
            merged(queries), merged(others), bias_s, gain[1:2], *(weights[position] for position in range(5))
        )
        out[:, 0, slot] = after.reshape(8, PART, C).astype(jnp.bfloat16)


def merged(block):
    return block[...].astype(jnp.float32).reshape(HALF, C)


def tile_kernel(block, gain, head_bias, *rest):
    weights, (tile, stacked) = rest[:5], rest[5:]

    @pl.when(pl.program_id(0) == 0)
    def _():
        for position, weight in enumerate(weights):
            stacked[:, position] = weight[...]

    tokens = block[...].astype(jnp.float32).reshape(8 * 2 * PART, C)
    normed = normalize(tokens, gain[0:1])
    tile[...] = lax.dot_general(
        head_bias[0], normed, CONTRACT_LAST, preferred_element_type=jnp.float32
    )


def whole(array):
    return pl.BlockSpec(array.shape, lambda *_: (0,) * array.ndim)


def attend(section, xa, xs, mask, gain, next_bias, weights, bias):
    first = pl.BlockSpec((8, None, PART, C), lambda step: (0, step, 0, 0))
    second = pl.BlockSpec((8, None, PART, C), lambda step: (0, OWN + step, 0, 0))
    weight = pl.BlockSpec((None, 5, C, C), lambda step: (section, 0, 0, 0))
    out_shape = [jax.ShapeDtypeStruct((8, OWN, 2, PART, C), jnp.bfloat16)]
    out_specs = [pl.BlockSpec((8, 1, 2, PART, C), lambda step: (0, step, 0, 0, 0))]
    scratch = [pltpu.VMEM((H, HALF, N), jnp.float32)]
    shared = [mask, gain]
    if section == 0:
        shared.append(next_bias)
        out_shape.append(jax.ShapeDtypeStruct((2, OWN, 8, HALF), jnp.float32))
        out_specs.append(pl.BlockSpec((2, 1, 8, HALF), lambda step: (0, step, 0, 0)))
    else:
        scratch.append(pltpu.VMEM((2, N, 2 * HALF), jnp.float32))
    return pl.pallas_call(
        (start_kernel, end_kernel)[section],
        grid=(OWN,),
        in_specs=[first, second, second, first]
        + [whole(member) for member in shared]
        + [weight, whole(bias)],
        out_specs=out_specs,
        scratch_shapes=scratch,
        out_shape=out_shape,
        compiler_params=pltpu.CompilerParams(vmem_limit_bytes=VMEM),
        cost_estimate=pl.CostEstimate(
            flops=8_000_000_000, bytes_accessed=6_000_000, transcendentals=8_000_000
        ),
        name=("start_node", "end_node")[section],
    )(xa, xa, xs, xs, *shared, weights, bias)


def by_core(array, axis, core):
    return jnp.where(core == 1, jnp.flip(array, axis), array)


def to_columns(array):
    flat = array.reshape(8, -1, C)
    return lax.all_to_all(flat, "col", 0, 0, tiled=True).reshape(array.shape)


def to_rows(array):
    flat = array.reshape(8, -1, C)
    flat = lax.all_to_all(flat, "row", 0, 0, axis_index_groups=SAME_CORE, tiled=True)
    return flat.reshape(array.shape)


def to_all(array):
    return lax.all_to_all(array, ("row", "col"), 0, 0, axis_index_groups=CORE_PLANES, tiled=True)


def copies(array):
    return jnp.broadcast_to(array[None], (8,) + array.shape)


def body(pair_input, token_mask, ln_gain, w_query, w_key, w_value, w_gate, w_bias, w_out):
    core = lax.axis_index("row") % 2
    mask_row = jnp.where(token_mask > 0, 0.0, masked_score).astype(jnp.float32)
    mask_row = by_core(mask_row.reshape(8, 2, PART), 1, core).transpose(1, 0, 2).reshape(1, N)
    head_bias = jnp.pad(w_bias.transpose(0, 2, 1), ((0, 0), (0, 4), (0, 0)))
    weights = [w_query, w_key, w_value, w_gate, w_out]

    tile, weights = pl.pallas_call(
        tile_kernel,
        grid=(5,),
        in_specs=[
            pl.BlockSpec((8, 2 * PART, C), lambda step: (step, 0, 0)),
            whole(ln_gain),
            whole(head_bias),
        ]
        + [whole(weight) for weight in weights],
        out_specs=[
            pl.BlockSpec((8, 16 * PART), lambda step: (0, step)),
            pl.BlockSpec((2, 5, C, C), lambda step: (0, 0, 0, 0)),
        ],
        out_shape=[
            jax.ShapeDtypeStruct((8, 2 * PART * PART), jnp.float32),
            jax.ShapeDtypeStruct((2, 5, C, C), jnp.bfloat16),
        ],
        name="bias_tile",
    )(pair_input, ln_gain, head_bias, *weights)
    tile = by_core(tile[:H].reshape(H, PART, 2, PART), 2, core).astype(jnp.bfloat16)
    tile = jnp.pad(
        tile.transpose(1, 0, 2, 3).reshape(PART, HALF), ((0, 0), (0, 3 * C - HALF))
    )
    tile = tile.reshape(PART, 3, C).transpose(1, 0, 2)
    halves = by_core(pair_input.reshape(8, OWN, 2, PART, C), 2, core)
    halves = halves.transpose(0, 2, 1, 3, 4).reshape(8, 2 * OWN, PART, C)
    xa = to_columns(jnp.concatenate([halves, copies(tile)], axis=1))
    xs = lax.ppermute(xa, "row", PARTNER)
    tile = xa[:, 2 * OWN :].transpose(0, 2, 1, 3).reshape(8, PART, 3 * C)[..., :HALF]
    tile = tile.reshape(8, PART, H, 2, PART).transpose(2, 1, 3, 0, 4).reshape(H, PART, N)
    tile = tile.reshape(H, PART, CHUNKS, C).transpose(0, 2, 1, 3)
    tile, xs = lax.optimization_barrier((tile, xs))
    bias = to_rows(copies(tile))
    after, tile = attend(0, xa, xs, mask_row, ln_gain, head_bias, weights, bias)

    sent = after.reshape(8, OWN, 2, 8, OWN, C).transpose(3, 0, 2, 4, 1, 5)
    tile = tile[:, :, :H].astype(jnp.bfloat16).transpose(0, 1, 2, 3).reshape(2 * OWN, 2 * CHUNKS, C)
    tile = jnp.broadcast_to(
        tile.transpose(1, 0, 2).reshape(1, 100, C), (64, 100, C)
    )
    got = to_all(jnp.concatenate([sent.reshape(64, 2 * OWN * OWN, C), tile], axis=1))
    xa = got[:, : 2 * OWN * OWN].reshape(8, 8, 2 * OWN, OWN, C)
    xa = xa.transpose(0, 2, 1, 3, 4).reshape(8, 2 * OWN, PART, C)
    xs = lax.ppermute(xa, "row", PARTNER)
    bias = got[:, 2 * OWN * OWN :].reshape(8, 8, 2, CHUNKS, 2, OWN, C)
    bias = bias.transpose(0, 2, 4, 3, 1, 5, 6).reshape(8, 2, 2, CHUNKS, PART, C)
    (after,) = attend(1, xa, xs, mask_row, ln_gain, None, weights, bias)
    block = by_core(to_rows(after), 2, core)
    return block.transpose(3, 2, 0, 1, 4).reshape(PART, 2 * PART, C)


def solution(mesh):
    placed = (P("row", "col", None), P(), P(), P(), P(), P(), P(), P(), P())
    return jax.shard_map(
        body, mesh=mesh, in_specs=placed, out_specs=P("row", "col", None), check_vma=False
    )
```

time: 230 us -> 177 us (0.77)
  waiting for transfers between devices: 77.8 us -> 23.1 us
  blocking collectives: 33 us -> 82.9 us
  starting transfers between devices: 27.7 us -> 4.99 us
  local copies, waits for them, and re-layouts: 27.1 us -> 14.9 us
  Pallas kernels: 54.8 us -> 48.7 us
  other arithmetic: 5.06 us -> 1.34 us
    all_to_all x6 -> x1, waiting for transfers between devices: 77.8 us -> 22.4 us  [to_rows(): lax.all_to_all(flat, 'row', 0, 0, axis_index_groups=SAME_CORE, tiled=True)]
    all_to_all x2 -> x3, blocking collectives: 33 us -> 82.9 us  [the longest x1 41 us: to_all(): lax.all_to_all(array, ('row', 'col'), 0, 0, axis_index_groups=CORE_PLANES...]
    all_to_all x6 -> x1, starting transfers between devices: 27.1 us -> 4.9 us  [to_rows(): lax.all_to_all(flat, 'row', 0, 0, axis_index_groups=SAME_CORE, tiled=True)]
    pallas_call x2 -> x3, Pallas kernels: 54.8 us -> 48.7 us  [the longest x2 43.9 us: attend(): pl.pallas_call((start_kernel, end_kernel)[section], grid=(OWN,), in_specs...]
    reduce_sum x2 -> x0, other arithmetic: 4.83 us -> none  [the longest x1 2.73 us: normalize(): centred = upcast - jnp.mean(upcast, axis=-1, keepdims=True)]
    unnamed x27 -> x16, local copies, waits for them, and re-layouts: 5.68 us -> 1.86 us
    squeeze x3 -> x0, local copies, waits for them, and re-layouts: 3.66 us -> none  [the longest x1 1.55 us: body(): w_other[1]]
    broadcast_in_dim x6 -> x4, local copies, waits for them, and re-layouts: 4.76 us -> 1.75 us  [the longest x2 1.52 us: copies(): return jnp.broadcast_to(array[None], (8,) + array.shape)]
  transfers between devices with their start and end apart: 8 -> 3, of which waited for: 6 -> 2; matrix products, arithmetic and copies ran while one was open for 6% -> 3% of each run, Pallas kernels for 0% -> 0%
where the time goes in v2:
time: 177 us; the launch traced here: 176 us
  blocking collectives  82.9 us (47%)
  Pallas kernels  48.7 us (28%)
  waiting for transfers between devices  23.1 us (13%)
  local copies, waits for them, and re-layouts  14.9 us (8%)
  starting transfers between devices  4.99 us (3%)
    pallas_call x2, Pallas kernels, attend(): pl.pallas_call((start_kernel, end_kernel)[section], grid=(OWN,), in_specs...  43.9 us
    all_to_all x1, blocking collectives, to_all(): lax.all_to_all(array, ('row', 'col'), 0, 0, axis_index_groups=CORE_PLANES...  41 us
    all_to_all x1, blocking collectives, to_columns(): return lax.all_to_all(flat, 'col', 0, 0, tiled=True).reshape(array.shape)  24.4 us
    all_to_all x1, waiting for transfers between devices, to_rows(): lax.all_to_all(flat, 'row', 0, 0, axis_index_groups=SAME_CORE, tiled=True)  22.4 us
    all_to_all x1, blocking collectives, to_rows(): lax.all_to_all(flat, 'row', 0, 0, axis_index_groups=SAME_CORE, tiled=True)  17.6 us
    all_to_all x1, starting transfers between devices, to_rows(): lax.all_to_all(flat, 'row', 0, 0, axis_index_groups=SAME_CORE, tiled=True)  4.9 us
    pallas_call x1, Pallas kernels, body(): pl.pallas_call(tile_kernel, grid=(5,), in_specs=[pl.BlockSpec((8, 2 * PAR...  4.78 us
  transfers between devices with their start and end apart: 3, of which 2 were waited for; matrix products, arithmetic and copies ran while one was open for 3% of the time, Pallas kernels for 0%

profile of v2, /device:TPU:8, one launch (start us, length us, event | category | flops | bytes accessed | tf_op | source)
XLA Modules:
  0.0 176.2 jit_solution(11964377595441938398)
XLA Ops:
  0.0 1.4 pad.8.head_bias.next_bias
  1.4 4.8 %bias_tile.1 = (f32[8,3200]{1,0:T(8,128)}, bf16[2,5,128,128]{3,2,1,0:T(8,128)(2,1)}) custom-call(bf16[40,80,128]{2,1,0:T(8,128)(2,1)} %block.1, f32[2,128]{1,0:T(2,128)} %gain.5, bf16[2,8,128]{2,1,0:T(8,128)(2,1)} %pad.8.head_bias.next_bias, bf16[2,128,128]{2,1,0:T(8,128)(2,1)} %rest_0_.1, bf16[2,128,128]{2,1,0:T(8,128)(2,1)} %rest_1_.1, ...), custom_call_target="tpu_custom_call" | custom-call | tf_op jit(solution)/shard_map/bias_tile/pallas_call | solution.py:230
  6.1 0.9 slice.19
  7.0 0.1 reshape.75
  7.2 0.1 copy.51
  7.3 0.6 rev.16
  7.9 0.1 fusion.2
  8.0 0.1 reshape.76
  8.2 0.0 copy-done.5
  8.2 0.2 fusion
  8.4 0.1 copy.50
  8.5 0.1 pad_maximum_fusion.1
  8.6 24.4 %all_to_all.20 = bf16[8,520,128]{2,1,0:T(8,128)(2,1)S(1)} all-to-all(bf16[8,520,128]{2,1,0:T(8,128)(2,1)S(1)} %bitcast.55), channel_id=1, replica_groups=mesh['row'=16,'col'=8] {'col'}, dimensions={0} | all-to-all | bytes 2129920 | tf_op jit(solution)/shard_map/all_to_all | solution.py:206
  33.0 0.0 collective-permute-start
  33.0 0.5 reshape.81
  33.6 1.6 copy.79
  35.2 1.8 %reshape_reshape.3 = bf16[4,40,5,128]{3,2,1,0:T(8,128)(2,1)S(1)} reshape(bf16[4,40,2,8,40]{4,3,2,1,0:T(8,128)(2,1)} %bitcast.64) | data formatting | bytes 409600 | tf_op jit(solution)/shard_map/reshape;reshape | solution.py:260
  37.0 0.0 collective-permute-done.far_q.far_o
  37.1 1.5 broadcast_in_dim.33
  38.6 4.9 %all-to-all-start.1 = ((bf16[8,800,128]{2,1,0:T(8,128)(2,1)}), bf16[8,800,128]{2,1,0:T(8,128)(2,1)S(1)}, u32[]{:S(2)}, u32[]{:S(2)}) async-start(bf16[8,800,128]{2,1,0:T(8,128)(2,1)} %broadcast_in_dim.33), calls=%async_computation.1 | async-start | bytes 3276800 | tf_op jit(solution)/shard_map/all_to_all | solution.py:211
  43.5 0.1 reshape.82
  43.6 0.1 reshape.83.mask
  43.7 22.4 %all-to-all-done.1 = bf16[8,800,128]{2,1,0:T(8,128)(2,1)S(1)} async-done(((bf16[8,800,128]{2,1,0:T(8,128)(2,1)}), bf16[8,800,128]{2,1,0:T(8,128)(2,1)S(1)}, u32[]{:S(2)}, u32[]{:S(2)}) %all-to-all-start.1) | async-done | bytes 1638432 | tf_op jit(solution)/shard_map/all_to_all | solution.py:211
  66.2 0.0 copy-done.1
  66.2 1.2 copy-done.3
  67.4 22.8 %start_node.1 = (bf16[8,5,2,40,128]{4,3,2,1,0:T(8,128)(2,1)S(1)}, f32[2,5,8,320]{3,2,1,0:T(8,128)S(1)}) custom-call(bf16[8,13,40,128]{3,2,1,0:T(8,128)(2,1)S(1)} %bitcast.50, bf16[8,13,40,128]{3,2,1,0:T(8,128)(2,1)S(1)} %bitcast.51, bf16[8,13,40,128]{3,2,1,0:T(8,128)(2,1)S(1)} %copy-done.3, bf16[8,13,40,128]{3,2,1,0:T(8,128)(2,1)S(1)} %copy-done.3, ...), custom_call_target="tpu_custom_call" | custom-call | flops 8000000000 | bytes 6000000 | tf_op jit(solution)/shard_map/start_node/pallas_call | solution.py:183
  90.2 0.2 copy.58
  90.4 0.2 copy.59
  90.7 0.1 reshape.87
  90.8 0.5 copy.61
  91.4 0.2 broadcast_in_dim.35
  91.6 0.7 pad_maximum_fusion
  92.4 41.0 %all_to_all.21 = bf16[64,150,128]{2,1,0:T(8,128)(2,1)S(1)} all-to-all(bf16[64,150,128]{2,1,0:T(8,128)(2,1)S(1)} %pad_maximum_fusion), channel_id=1, replica_groups={{0,1,2,3,4,5,6,7,16,17,18,19,20,21,22,23,32,33,34,35,36,37,38,39,48,49,..., dimensions={0} | all-to-all | bytes 4915200 | tf_op jit(solution)/shard_map/all_to_all | solution.py:216
  133.3 0.1 slice.28
  133.4 0.2 copy.72
  133.6 0.1 copy.63
  133.7 0.1 copy.67.own_q.own_o
  133.8 0.1 collective-permute-start.1
  133.9 0.7 slice.29
  134.6 0.4 copy.73
  135.0 0.3 copy.66
  135.4 0.2 copy.69.rest_1_
  135.6 0.7 collective-permute-done.1.far_q.far_o
  136.3 21.1 %end_node.1 = bf16[8,5,2,40,128]{4,3,2,1,0:T(8,128)(2,1)S(1)} custom-call(bf16[8,10,40,128]{3,2,1,0:T(8,128)(2,1)S(1)} %copy.67.own_q.own_o, bf16[8,10,40,128]{3,2,1,0:T(8,128)(2,1)S(1)} %copy.67.own_q.own_o, bf16[8,10,40,128]{3,2,1,0:T(8,128)(2,1)S(1)} %collective-permute-done.1.far_q.far_o, ...), custom_call_target="tpu_custom_call" | custom-call | flops 8000000000 | bytes 6000000 | tf_op jit(solution)/shard_map/end_node/pallas_call | solution.py:183
  157.4 17.6 %all_to_all.22 = bf16[8,400,128]{2,1,0:T(8,128)(2,1)S(1)} all-to-all(bf16[8,400,128]{2,1,0:T(8,128)(2,1)S(1)} %bitcast.52), channel_id=1, replica_groups={{0,16,32,48,64,80,96,112},{8,24,40,56,72,88,104,120},{1,17,33,49,65,81,..., dimensions={0} | all-to-all | bytes 1638400 | tf_op jit(solution)/shard_map/all_to_all | solution.py:211
  175.0 0.2 fusion.1
  175.2 0.1 copy.70
  175.2 1.0 copy.71
  (24 shorter events, 0.2 us)
Async XLA Ops:
  0.0 8.2 %copy-start.5 = (bf16[40,80,128]{2,1,0:T(8,128)(2,1)S(1)}, bf16[40,80,128]{2,1,0:T(8,128)(2,1)}, u32[]{:S(2)}) copy-start(bf16[40,80,128]{2,1,0:T(8,128)(2,1)} %block.1) | copy-start | bytes 2457604
  33.0 4.0 %collective-permute-start = (bf16[8,13,40,128]{3,2,1,0:T(8,128)(2,1)S(1)}, bf16[8,13,40,128]{3,2,1,0:T(8,128)(2,1)S(1)}, u32[]{:S(2)}, u32[]{:S(2)}) collective-permute-start(bf16[8,13,40,128]{3,2,1,0:T(8,128)(2,1)S(1)} %bitcast.48), channel_id=1, source_target_pairs={{0,8},{8,0},{16,24},{24,16},{32,40},{40,32},{48,56},{56,48},{64,72... | collective-permute-start | bytes 3194888 | tf_op jit(solution)/shard_map/ppermute | solution.py:257
  37.0 1.5 copy-start.2
  38.5 4.9 %copy-start.6 = (s32[640]{0:T(1024)S(1)}, s32[640]{0:T(1024)}, u32[]{:S(2)}) copy-start(s32[640]{0:T(1024)} %param.10) | copy-start | bytes 7684
  38.5 27.6 %copy-start = (bf16[2,8,128]{2,1,0:T(8,128)(2,1)S(1)}, bf16[2,8,128]{2,1,0:T(8,128)(2,1)}, u32[]{:S(2)}) copy-start(bf16[2,8,128]{2,1,0:T(8,128)(2,1)} %pad.8.head_bias.next_bias) | copy-start | bytes 12292
  38.5 27.6 %copy-start.1 = (f32[2,128]{1,0:T(2,128)S(1)}, f32[2,128]{1,0:T(2,128)}, u32[]{:S(2)}) copy-start(f32[2,128]{1,0:T(2,128)} %gain.5) | copy-start | bytes 3076
  38.6 27.6 %copy-start.4 = (bf16[2,5,128,128]{3,2,1,0:T(8,128)(2,1)S(1)}, bf16[2,5,128,128]{3,2,1,0:T(8,128)(2,1)}, u32[]{:S(2)}) copy-start(bf16[2,5,128,128]{3,2,1,0:T(8,128)(2,1)} %get-tuple-element.13.rest_0_) | copy-start | bytes 983044
  38.6 27.6 %all-to-all-start.1 = ((bf16[8,800,128]{2,1,0:T(8,128)(2,1)}), bf16[8,800,128]{2,1,0:T(8,128)(2,1)S(1)}, u32[]{:S(2)}, u32[]{:S(2)}) async-start(bf16[8,800,128]{2,1,0:T(8,128)(2,1)} %broadcast_in_dim.33), calls=%async_computation.1 | async-start | bytes 3276800 | tf_op jit(solution)/shard_map/all_to_all | solution.py:211
  66.2 1.2 copy-start.3
  133.8 2.4 %collective-permute-start.1 = (bf16[8,10,40,128]{3,2,1,0:T(8,128)(2,1)S(1)}, bf16[8,10,40,128]{3,2,1,0:T(8,128)(2,1)S(1)}, u32[]{:S(2)}, u32[]{:S(2)}) collective-permute-start(bf16[8,10,40,128]{3,2,1,0:T(8,128)(2,1)S(1)} %copy.67.own_q.own_o), channel_id=1, source_target_pairs={{0,8},{8,0},{16,24},{24,16},{32,40},{40,32},{48,56},{56,48},{64,72... | collective-permute-start | bytes 2457608 | tf_op jit(solution)/shard_map/ppermute | solution.py:273

commit v3 on v2

--- a/solution.py
+++ b/solution.py
@@ -42,12 +42,12 @@
     return jnp.dot(left, right, preferred_element_type=jnp.float32)
 
 
-def head_lanes(rows, head):
-    lane = lax.broadcasted_iota(jnp.int32, (rows, C), 1)
-    return (lane >= head * HD) & (lane < (head + 1) * HD)
-
-
-def attend_row(queries_in, others_in, bias_s, gain, w_query, w_key, w_value, w_gate, w_out):
+def head_lanes(head):
+    lane = lax.broadcasted_iota(jnp.int32, (1, C), 1)
+    return jnp.where((lane >= head * HD) & (lane < (head + 1) * HD), 1.0, 0.0).astype(jnp.bfloat16)
+
+
+def prepare(queries_in, others_in, gain, w_query, w_key, w_value, w_gate):
     own = normalize(queries_in, gain)
     other = normalize(others_in, gain)
     own_all = dot(own, jnp.concatenate([w_query, w_gate, w_key, w_value], axis=1))
@@ -59,30 +59,46 @@
     coarse = queries.astype(jnp.bfloat16)
     fine = (queries - coarse.astype(jnp.float32)).astype(jnp.bfloat16)
     both_queries = jnp.concatenate([coarse, fine], axis=1)
-    zeros = jnp.zeros((N, C), jnp.bfloat16)
-    ones = jnp.ones((N, C), jnp.bfloat16)
     head_keys, head_sources = [], []
     for head in range(H):
-        lanes = head_lanes(N, head)
-        picked = jnp.where(lanes, keys, zeros)
+        lanes = head_lanes(head)
+        picked = keys * lanes
         head_keys.append(jnp.concatenate([picked, picked], axis=1))
         head_sources.append(
-            jnp.concatenate([jnp.where(lanes, values, zeros), jnp.where(lanes, ones, zeros)], axis=1)
+            jnp.concatenate([values * lanes, jnp.broadcast_to(lanes, (N, C))], axis=1)
         )
-    all_scores = lax.dot_general(
-        both_queries,
-        jnp.concatenate(head_keys, axis=0),
-        CONTRACT_LAST,
-        preferred_element_type=jnp.float32,
-    )
-    head_weights = []
-    for head in range(H):
-        scores = all_scores[:, head * N : (head + 1) * N] + bias_s[head]
-        highest = jnp.max(scores, axis=-1, keepdims=True)
-        head_weights.append(jnp.exp2(scores - highest).astype(jnp.bfloat16))
-    summed = dot(jnp.concatenate(head_weights, axis=1), jnp.concatenate(head_sources, axis=0))
+    return both_queries, gating, head_keys, head_sources
+
+
+def score(both_queries, head_keys):
+    return lax.dot_general(
+        both_queries, head_keys, CONTRACT_LAST, preferred_element_type=jnp.float32
+    )
+
+
+def softmax(scores, bias):
+    scores = scores + bias
+    highest = jnp.max(scores, axis=-1, keepdims=True)
+    return jnp.exp2(scores - highest).astype(jnp.bfloat16)
+
+
+def mix(head_weights, head_sources):
+    return dot(jnp.concatenate(head_weights, axis=1), jnp.concatenate(head_sources, axis=0))
+
+
+def finish(queries_in, summed, gating, w_out):
     hidden = (summed[:, :C] / summed[:, C:] * gating).astype(jnp.bfloat16)
     return (queries_in + dot(hidden, w_out)).astype(jnp.bfloat16).astype(jnp.float32)
+
+
+def attend_rows(rows, bias_s, gain, w_query, w_key, w_value, w_gate, w_out):
+    pre = [prepare(q, o, gain, w_query, w_key, w_value, w_gate) for q, o in rows]
+    scores = [score(p[0], jnp.concatenate(p[2], axis=0)) for p in pre]
+    summed = []
+    for p, sc in zip(pre, scores):
+        weights = [softmax(sc[:, h * N : (h + 1) * N], bias_s[h]) for h in range(H)]
+        summed.append(mix(weights, p[3]))
+    return [finish(q, m, p[1], w_out) for (q, o), m, p in zip(rows, summed, pre)]
 
 
 def start_kernel(own_q, own_o, far_q, far_o, mask, gain, next_bias, *rest):
@@ -99,10 +115,14 @@
                         bias[place, head, part].astype(jnp.float32) * LOG2E + mask[:, lanes]
                     )
 
-    for slot, (queries, others) in enumerate(((own_q, own_o), (far_q, far_o))):
-        after = attend_row(
-            merged(queries), merged(others), bias_s, gain[0:1], *(weights[position] for position in range(5))
-        )
+    afters = attend_rows(
+        ((merged(own_q), merged(own_o)), (merged(far_q), merged(far_o))),
+        bias_s,
+        gain[0:1],
+        *(weights[position] for position in range(5)),
+    )
+    for slot in range(2):
+        after = afters[slot]
         out[:, 0, slot] = after.reshape(8, PART, C).astype(jnp.bfloat16)
         normed = normalize(after, gain[1:2])
         tile[slot, 0] = lax.dot_general(
@@ -112,34 +132,31 @@
 
 def end_kernel(own_q, own_o, far_q, far_o, mask, gain, *rest):
     weights, bias = rest[:2]
-    out, bias_s, turned_s = rest[2:]
+    out, bias_s = rest[2:]
 
     @pl.when(pl.program_id(0) == 0)
     def _():
-        row = lax.broadcasted_iota(jnp.int32, (HALF, 2 * HALF), 0)
-        col = lax.broadcasted_iota(jnp.int32, (HALF, 2 * HALF), 1)
-        for pair in range(2):
-            for place in range(8):
-                for side in range(2):
-                    first = side * HALF + place * PART
-                    for part in range(CHUNKS):
-                        turned_s[pair, first : first + PART, part * C : (part + 1) * C] = bias[
-                            place, pair, side, part
-                        ].astype(jnp.float32)
+        row = lax.broadcasted_iota(jnp.int32, (HALF, HALF), 0)
+        col = lax.broadcasted_iota(jnp.int32, (HALF, HALF), 1)
+        identity = jnp.where(row == col, 1.0, 0.0).astype(jnp.bfloat16)
         for head in range(H):
-            chosen = jnp.where(row + (head % 2) * HALF == col, 1.0, 0.0).astype(jnp.bfloat16)
+            first = (head % 2) * HALF
             turned = lax.dot_general(
-                chosen,
-                turned_s[head // 2].astype(jnp.bfloat16),
+                identity,
+                bias[head // 2, :, first : first + HALF],
                 CONTRACT_LAST,
                 preferred_element_type=jnp.float32,
             )
             bias_s[head] = turned * LOG2E + mask[...]
 
-    for slot, (queries, others) in enumerate(((own_q, own_o), (far_q, far_o))):
-        after = attend_row(
-            merged(queries), merged(others), bias_s, gain[1:2], *(weights[position] for position in range(5))
-        )
+    afters = attend_rows(
+        ((merged(own_q), merged(own_o)), (merged(far_q), merged(far_o))),
+        bias_s,
+        gain[1:2],
+        *(weights[position] for position in range(5)),
+    )
+    for slot in range(2):
+        after = afters[slot]
         out[:, 0, slot] = after.reshape(8, PART, C).astype(jnp.bfloat16)
 
 
@@ -178,8 +195,6 @@
         shared.append(next_bias)
         out_shape.append(jax.ShapeDtypeStruct((2, OWN, 8, HALF), jnp.float32))
         out_specs.append(pl.BlockSpec((2, 1, 8, HALF), lambda step: (0, step, 0, 0)))
-    else:
-        scratch.append(pltpu.VMEM((2, N, 2 * HALF), jnp.float32))
     return pl.pallas_call(
         (start_kernel, end_kernel)[section],
         grid=(OWN,),
@@ -272,7 +287,7 @@
     xa = xa.transpose(0, 2, 1, 3, 4).reshape(8, 2 * OWN, PART, C)
     xs = lax.ppermute(xa, "row", PARTNER)
     bias = got[:, 2 * OWN * OWN :].reshape(8, 8, 2, CHUNKS, 2, OWN, C)
-    bias = bias.transpose(0, 2, 4, 3, 1, 5, 6).reshape(8, 2, 2, CHUNKS, PART, C)
+    bias = bias.transpose(2, 4, 0, 1, 5, 3, 6).reshape(2, N, N)
     (after,) = attend(1, xa, xs, mask_row, ln_gain, None, weights, bias)
     block = by_core(to_rows(after), 2, core)
     return block.transpose(3, 2, 0, 1, 4).reshape(PART, 2 * PART, C)

time: 177 us -> 175 us (0.989)
  Pallas kernels: 48.7 us -> 39.3 us
  local copies, waits for them, and re-layouts: 14.9 us -> 21.7 us
    pallas_call x2, Pallas kernels: 43.9 us -> 34.6 us  [attend(): pl.pallas_call((start_kernel, end_kernel)[section], grid=(OWN,), in_specs...]
    reshape x1, local copies, waits for them, and re-layouts: 0.21 us -> 3.72 us  [body(): bias = bias.transpose(2, 4, 0, 1, 5, 3, 6).reshape(2, N, N)]
    transpose x1, local copies, waits for them, and re-layouts: 0.33 us -> 2.7 us  [body(): bias = bias.transpose(2, 4, 0, 1, 5, 3, 6).reshape(2, N, N)]
  transfers between devices with their start and end apart: 3 -> 3, of which waited for: 2 -> 1; matrix products, arithmetic and copies ran while one was open for 3% -> 7% of each run, Pallas kernels for 0% -> 0%
where the time goes in v3:
time: 175 us; the launch traced here: 174 us
  blocking collectives  83.2 us (48%)
  Pallas kernels  39.3 us (22%)
  waiting for transfers between devices  22.4 us (13%)
  local copies, waits for them, and re-layouts  21.7 us (12%)
  starting transfers between devices  5.17 us (3%)
    all_to_all x1, blocking collectives, to_all(): lax.all_to_all(array, ('row', 'col'), 0, 0, axis_index_groups=CORE_PLANES...  40.9 us
    pallas_call x2, Pallas kernels, attend(): pl.pallas_call((start_kernel, end_kernel)[section], grid=(OWN,), in_specs...  34.6 us
    all_to_all x1, blocking collectives, to_columns(): return lax.all_to_all(flat, 'col', 0, 0, tiled=True).reshape(array.shape)  24.4 us
    all_to_all x1, waiting for transfers between devices, to_rows(): lax.all_to_all(flat, 'row', 0, 0, axis_index_groups=SAME_CORE, tiled=True)  22.4 us
    all_to_all x1, blocking collectives, to_rows(): lax.all_to_all(flat, 'row', 0, 0, axis_index_groups=SAME_CORE, tiled=True)  17.9 us
    all_to_all x1, starting transfers between devices, to_rows(): lax.all_to_all(flat, 'row', 0, 0, axis_index_groups=SAME_CORE, tiled=True)  4.9 us
    pallas_call x1, Pallas kernels, body(): pl.pallas_call(tile_kernel, grid=(5,), in_specs=[pl.BlockSpec((8, 2 * PAR...  4.78 us
    reshape x1, local copies, waits for them, and re-layouts, body(): bias = bias.transpose(2, 4, 0, 1, 5, 3, 6).reshape(2, N, N)  3.72 us
  transfers between devices with their start and end apart: 3, of which 1 were waited for; matrix products, arithmetic and copies ran while one was open for 7% of the time, Pallas kernels for 0%

profile of v3, /device:TPU:8, one launch (start us, length us, event | category | flops | bytes accessed | tf_op | source)
XLA Modules:
  0.0 173.6 jit_solution(5848200204614193094)
XLA Ops:
  0.0 1.3 pad.8.head_bias.next_bias
  1.3 4.8 %bias_tile.1 = (f32[8,3200]{1,0:T(8,128)}, bf16[2,5,128,128]{3,2,1,0:T(8,128)(2,1)}) custom-call(bf16[40,80,128]{2,1,0:T(8,128)(2,1)} %block.1, f32[2,128]{1,0:T(2,128)} %gain.5, bf16[2,8,128]{2,1,0:T(8,128)(2,1)} %pad.8.head_bias.next_bias, bf16[2,128,128]{2,1,0:T(8,128)(2,1)} %rest_0_.1, bf16[2,128,128]{2,1,0:T(8,128)(2,1)} %rest_1_.1, ...), custom_call_target="tpu_custom_call" | custom-call | tf_op jit(solution)/shard_map/bias_tile/pallas_call | solution.py:245
  6.1 0.9 slice.19
  7.0 0.1 reshape.75
  7.2 0.1 copy.49
  7.2 0.6 rev.16
  7.9 0.1 fusion.2
  8.0 0.1 reshape.76
  8.2 0.2 fusion
  8.4 0.1 copy.48
  8.5 0.1 pad_maximum_fusion.1
  8.6 24.4 %all_to_all.20 = bf16[8,520,128]{2,1,0:T(8,128)(2,1)S(1)} all-to-all(bf16[8,520,128]{2,1,0:T(8,128)(2,1)S(1)} %bitcast.53), channel_id=1, replica_groups=mesh['row'=16,'col'=8] {'col'}, dimensions={0} | all-to-all | bytes 2129920 | tf_op jit(solution)/shard_map/all_to_all | solution.py:221
  33.0 0.0 collective-permute-start
  33.0 0.5 reshape.81
  33.6 1.6 copy.76
  35.2 1.8 %reshape_reshape.3 = bf16[4,40,5,128]{3,2,1,0:T(8,128)(2,1)S(1)} reshape(bf16[4,40,2,8,40]{4,3,2,1,0:T(8,128)(2,1)} %bitcast.62) | data formatting | bytes 409600 | tf_op jit(solution)/shard_map/reshape;reshape | solution.py:275
  37.0 0.0 collective-permute-done.far_q.far_o
  37.1 1.5 broadcast_in_dim.33
  38.6 4.9 %all-to-all-start.1 = ((bf16[8,800,128]{2,1,0:T(8,128)(2,1)}), bf16[8,800,128]{2,1,0:T(8,128)(2,1)S(1)}, u32[]{:S(2)}, u32[]{:S(2)}) async-start(bf16[8,800,128]{2,1,0:T(8,128)(2,1)} %broadcast_in_dim.33), calls=%async_computation.1 | async-start | bytes 3276800 | tf_op jit(solution)/shard_map/all_to_all | solution.py:226
  43.5 0.0 copy-done.7
  43.5 0.1 reshape.82
  43.6 0.1 reshape.83.mask
  43.7 22.4 %all-to-all-done.1 = bf16[8,800,128]{2,1,0:T(8,128)(2,1)S(1)} async-done(((bf16[8,800,128]{2,1,0:T(8,128)(2,1)}), bf16[8,800,128]{2,1,0:T(8,128)(2,1)S(1)}, u32[]{:S(2)}, u32[]{:S(2)}) %all-to-all-start.1) | async-done | bytes 1638432 | tf_op jit(solution)/shard_map/all_to_all | solution.py:226
  66.2 1.2 copy-done.3
  67.4 17.5 %start_node.1 = (bf16[8,5,2,40,128]{4,3,2,1,0:T(8,128)(2,1)S(1)}, f32[2,5,8,320]{3,2,1,0:T(8,128)S(1)}) custom-call(bf16[8,13,40,128]{3,2,1,0:T(8,128)(2,1)S(1)} %bitcast.49, bf16[8,13,40,128]{3,2,1,0:T(8,128)(2,1)S(1)} %bitcast.50, bf16[8,13,40,128]{3,2,1,0:T(8,128)(2,1)S(1)} %copy-done.3, bf16[8,13,40,128]{3,2,1,0:T(8,128)(2,1)S(1)} %copy-done.3, ...), custom_call_target="tpu_custom_call" | custom-call | flops 8000000000 | bytes 6000000 | tf_op jit(solution)/shard_map/start_node/pallas_call | solution.py:198
  84.9 0.2 copy.56
  85.1 0.2 copy.57
  85.3 0.1 reshape.87
  85.5 0.5 copy.59
  86.0 0.2 broadcast_in_dim.35
  86.3 0.7 pad_maximum_fusion
  87.0 40.9 %all_to_all.21 = bf16[64,150,128]{2,1,0:T(8,128)(2,1)S(1)} all-to-all(bf16[64,150,128]{2,1,0:T(8,128)(2,1)S(1)} %pad_maximum_fusion), channel_id=1, replica_groups={{0,1,2,3,4,5,6,7,16,17,18,19,20,21,22,23,32,33,34,35,36,37,38,39,48,49,..., dimensions={0} | all-to-all | bytes 4915200 | tf_op jit(solution)/shard_map/all_to_all | solution.py:231
  128.0 0.1 slice.28
  128.0 0.2 copy.69
  128.2 0.1 copy.61
  128.4 0.1 copy.65.own_q.own_o
  128.5 0.3 collective-permute-start.1
  128.8 0.7 slice.29
  129.4 0.4 copy.70
  129.9 2.7 %copy.64 = bf16[2,2,8,8,5,5,128]{6,5,4,3,2,1,0:T(8,128)(2,1)} copy(bf16[2,2,8,8,5,5,128]{6,3,2,4,1,5,0:T(8,128)(2,1)S(1)} %bitcast.52) | data formatting | bytes 3276800 | tf_op jit(solution)/shard_map/transpose | solution.py:290
  132.6 3.7 %reshape.91.rest_1_ = bf16[2,640,640]{2,1,0:T(8,128)(2,1)S(1)} reshape(bf16[2,2,8,8,5,5,128]{6,5,4,3,2,1,0:T(8,128)(2,1)} %copy.64) | data formatting | bytes 3276800 | tf_op jit(solution)/shard_map/reshape | solution.py:290
  136.3 0.0 collective-permute-done.1.far_q.far_o
  136.3 1.0 copy-done.5
  137.3 17.1 %end_node.1 = bf16[8,5,2,40,128]{4,3,2,1,0:T(8,128)(2,1)S(1)} custom-call(bf16[8,10,40,128]{3,2,1,0:T(8,128)(2,1)S(1)} %copy.65.own_q.own_o, bf16[8,10,40,128]{3,2,1,0:T(8,128)(2,1)S(1)} %copy.65.own_q.own_o, bf16[8,10,40,128]{3,2,1,0:T(8,128)(2,1)S(1)} %collective-permute-done.1.far_q.far_o, ...), custom_call_target="tpu_custom_call" | custom-call | flops 8000000000 | bytes 6000000 | tf_op jit(solution)/shard_map/end_node/pallas_call | solution.py:198
  154.4 17.9 %all_to_all.22 = bf16[8,400,128]{2,1,0:T(8,128)(2,1)S(1)} all-to-all(bf16[8,400,128]{2,1,0:T(8,128)(2,1)S(1)} %bitcast.51), channel_id=1, replica_groups={{0,16,32,48,64,80,96,112},{8,24,40,56,72,88,104,120},{1,17,33,49,65,81,..., dimensions={0} | all-to-all | bytes 1638400 | tf_op jit(solution)/shard_map/all_to_all | solution.py:226
  172.3 0.2 fusion.1
  172.5 0.1 copy.67
  172.6 1.0 copy.68
  (26 shorter events, 0.2 us)
Async XLA Ops:
  0.0 8.2 %copy-start.6 = (bf16[40,80,128]{2,1,0:T(8,128)(2,1)S(1)}, bf16[40,80,128]{2,1,0:T(8,128)(2,1)}, u32[]{:S(2)}) copy-start(bf16[40,80,128]{2,1,0:T(8,128)(2,1)} %block.1) | copy-start | bytes 2457604
  33.0 4.0 %collective-permute-start = (bf16[8,13,40,128]{3,2,1,0:T(8,128)(2,1)S(1)}, bf16[8,13,40,128]{3,2,1,0:T(8,128)(2,1)S(1)}, u32[]{:S(2)}, u32[]{:S(2)}) collective-permute-start(bf16[8,13,40,128]{3,2,1,0:T(8,128)(2,1)S(1)} %bitcast.47), channel_id=1, source_target_pairs={{0,8},{8,0},{16,24},{24,16},{32,40},{40,32},{48,56},{56,48},{64,72... | collective-permute-start | bytes 3194888 | tf_op jit(solution)/shard_map/ppermute | solution.py:272
  37.0 1.6 copy-start.2
  38.5 4.9 %copy-start.7 = (s32[640]{0:T(1024)S(1)}, s32[640]{0:T(1024)}, u32[]{:S(2)}) copy-start(s32[640]{0:T(1024)} %param.10) | copy-start | bytes 7684
  38.5 27.6 %copy-start = (bf16[2,8,128]{2,1,0:T(8,128)(2,1)S(1)}, bf16[2,8,128]{2,1,0:T(8,128)(2,1)}, u32[]{:S(2)}) copy-start(bf16[2,8,128]{2,1,0:T(8,128)(2,1)} %pad.8.head_bias.next_bias) | copy-start | bytes 12292
  38.6 27.6 %copy-start.1 = (f32[2,128]{1,0:T(2,128)S(1)}, f32[2,128]{1,0:T(2,128)}, u32[]{:S(2)}) copy-start(f32[2,128]{1,0:T(2,128)} %gain.5) | copy-start | bytes 3076
  38.6 27.6 %copy-start.4 = (bf16[2,5,128,128]{3,2,1,0:T(8,128)(2,1)S(1)}, bf16[2,5,128,128]{3,2,1,0:T(8,128)(2,1)}, u32[]{:S(2)}) copy-start(bf16[2,5,128,128]{3,2,1,0:T(8,128)(2,1)} %get-tuple-element.13.rest_0_) | copy-start | bytes 983044
  38.6 27.6 %all-to-all-start.1 = ((bf16[8,800,128]{2,1,0:T(8,128)(2,1)}), bf16[8,800,128]{2,1,0:T(8,128)(2,1)S(1)}, u32[]{:S(2)}, u32[]{:S(2)}) async-start(bf16[8,800,128]{2,1,0:T(8,128)(2,1)} %broadcast_in_dim.33), calls=%async_computation.1 | async-start | bytes 3276800 | tf_op jit(solution)/shard_map/all_to_all | solution.py:226
  66.2 1.2 copy-start.3
  128.5 7.8 %collective-permute-start.1 = (bf16[8,10,40,128]{3,2,1,0:T(8,128)(2,1)S(1)}, bf16[8,10,40,128]{3,2,1,0:T(8,128)(2,1)S(1)}, u32[]{:S(2)}, u32[]{:S(2)}) collective-permute-start(bf16[8,10,40,128]{3,2,1,0:T(8,128)(2,1)S(1)} %copy.65.own_q.own_o), channel_id=1, source_target_pairs={{0,8},{8,0},{16,24},{24,16},{32,40},{40,32},{48,56},{56,48},{64,72... | collective-permute-start | bytes 2457608 | tf_op jit(solution)/shard_map/ppermute | solution.py:288
  136.3 1.0 copy-start.5

commit v4 on v3

--- a/solution.py
+++ b/solution.py
@@ -42,9 +42,9 @@
     return jnp.dot(left, right, preferred_element_type=jnp.float32)
 
 
-def head_lanes(head):
-    lane = lax.broadcasted_iota(jnp.int32, (1, C), 1)
-    return jnp.where((lane >= head * HD) & (lane < (head + 1) * HD), 1.0, 0.0).astype(jnp.bfloat16)
+def head_lanes(rows, head):
+    lane = lax.broadcasted_iota(jnp.int32, (rows, C), 1)
+    return (lane >= head * HD) & (lane < (head + 1) * HD)
 
 
 def prepare(queries_in, others_in, gain, w_query, w_key, w_value, w_gate):
@@ -59,13 +59,15 @@
     coarse = queries.astype(jnp.bfloat16)
     fine = (queries - coarse.astype(jnp.float32)).astype(jnp.bfloat16)
     both_queries = jnp.concatenate([coarse, fine], axis=1)
+    zeros = jnp.zeros((N, C), jnp.bfloat16)
+    ones = jnp.ones((N, C), jnp.bfloat16)
     head_keys, head_sources = [], []
     for head in range(H):
-        lanes = head_lanes(head)
-        picked = keys * lanes
+        lanes = head_lanes(N, head)
+        picked = jnp.where(lanes, keys, zeros)
         head_keys.append(jnp.concatenate([picked, picked], axis=1))
         head_sources.append(
-            jnp.concatenate([values * lanes, jnp.broadcast_to(lanes, (N, C))], axis=1)
+            jnp.concatenate([jnp.where(lanes, values, zeros), jnp.where(lanes, ones, zeros)], axis=1)
         )
     return both_queries, gating, head_keys, head_sources
 
@@ -125,25 +127,30 @@
         after = afters[slot]
         out[:, 0, slot] = after.reshape(8, PART, C).astype(jnp.bfloat16)
         normed = normalize(after, gain[1:2])
-        tile[slot, 0] = lax.dot_general(
-            next_bias[1], normed, CONTRACT_LAST, preferred_element_type=jnp.float32
-        )
+        tile[slot, 0] = head_rows(next_bias[1], normed)
 
 
 def end_kernel(own_q, own_o, far_q, far_o, mask, gain, *rest):
     weights, bias = rest[:2]
-    out, bias_s = rest[2:]
+    out, bias_s, turned_s = rest[2:]
 
     @pl.when(pl.program_id(0) == 0)
     def _():
-        row = lax.broadcasted_iota(jnp.int32, (HALF, HALF), 0)
-        col = lax.broadcasted_iota(jnp.int32, (HALF, HALF), 1)
-        identity = jnp.where(row == col, 1.0, 0.0).astype(jnp.bfloat16)
+        row = lax.broadcasted_iota(jnp.int32, (HALF, 2 * HALF), 0)
+        col = lax.broadcasted_iota(jnp.int32, (HALF, 2 * HALF), 1)
+        for pair in range(2):
+            for place in range(8):
+                for side in range(2):
+                    first = side * HALF + place * PART
+                    for part in range(CHUNKS):
+                        turned_s[pair, first : first + PART, part * C : (part + 1) * C] = bias[
+                            place, pair, side, part
+                        ].astype(jnp.float32)
         for head in range(H):
-            first = (head % 2) * HALF
+            chosen = jnp.where(row + (head % 2) * HALF == col, 1.0, 0.0).astype(jnp.bfloat16)
             turned = lax.dot_general(
-                identity,
-                bias[head // 2, :, first : first + HALF],
+                chosen,
+                turned_s[head // 2].astype(jnp.bfloat16),
                 CONTRACT_LAST,
                 preferred_element_type=jnp.float32,
             )
@@ -160,6 +167,12 @@
         out[:, 0, slot] = after.reshape(8, PART, C).astype(jnp.bfloat16)
 
 
+def head_rows(head_bias, normed):
+    return lax.dot_general(
+        head_bias, normed, (((0,), (1,)), ((), ())), preferred_element_type=jnp.float32
+    )
+
+
 def merged(block):
     return block[...].astype(jnp.float32).reshape(HALF, C)
 
@@ -174,9 +187,23 @@
 
     tokens = block[...].astype(jnp.float32).reshape(8 * 2 * PART, C)
     normed = normalize(tokens, gain[0:1])
-    tile[...] = lax.dot_general(
-        head_bias[0], normed, CONTRACT_LAST, preferred_element_type=jnp.float32
-    )
+    tile[...] = head_rows(head_bias[0], normed)
+
+
+def spread_kernel(arrived, spread):
+    blocks = [
+        jnp.concatenate([arrived[column, 2 * OWN + part].astype(jnp.float32) for part in range(3)], axis=1)
+        for column in range(8)
+    ]
+    for head in range(H):
+        lanes = []
+        for side in range(2):
+            first = (head * 2 + side) * PART
+            lanes += [block[:, first : first + PART] for block in blocks]
+        joined = jnp.concatenate(lanes, axis=1).astype(jnp.bfloat16)
+        for part in range(CHUNKS):
+            for copy in range(8):
+                spread[copy, head, part] = joined[:, part * C : (part + 1) * C]
 
 
 def whole(array):
@@ -193,8 +220,10 @@
     shared = [mask, gain]
     if section == 0:
         shared.append(next_bias)
-        out_shape.append(jax.ShapeDtypeStruct((2, OWN, 8, HALF), jnp.float32))
-        out_specs.append(pl.BlockSpec((2, 1, 8, HALF), lambda step: (0, step, 0, 0)))
+        out_shape.append(jax.ShapeDtypeStruct((2, OWN, H, HALF), jnp.float32))
+        out_specs.append(pl.BlockSpec((2, 1, H, HALF), lambda step: (0, step, 0, 0)))
+    else:
+        scratch.append(pltpu.VMEM((2, N, 2 * HALF), jnp.float32))
     return pl.pallas_call(
         (start_kernel, end_kernel)[section],
         grid=(OWN,),
@@ -239,7 +268,6 @@
     core = lax.axis_index("row") % 2
     mask_row = jnp.where(token_mask > 0, 0.0, masked_score).astype(jnp.float32)
     mask_row = by_core(mask_row.reshape(8, 2, PART), 1, core).transpose(1, 0, 2).reshape(1, N)
-    head_bias = jnp.pad(w_bias.transpose(0, 2, 1), ((0, 0), (0, 4), (0, 0)))
     weights = [w_query, w_key, w_value, w_gate, w_out]
 
     tile, weights = pl.pallas_call(
@@ -248,20 +276,20 @@
         in_specs=[
             pl.BlockSpec((8, 2 * PART, C), lambda step: (step, 0, 0)),
             whole(ln_gain),
-            whole(head_bias),
+            whole(w_bias),
         ]
         + [whole(weight) for weight in weights],
         out_specs=[
-            pl.BlockSpec((8, 16 * PART), lambda step: (0, step)),
+            pl.BlockSpec((H, 16 * PART), lambda step: (0, step)),
             pl.BlockSpec((2, 5, C, C), lambda step: (0, 0, 0, 0)),
         ],
         out_shape=[
-            jax.ShapeDtypeStruct((8, 2 * PART * PART), jnp.float32),
+            jax.ShapeDtypeStruct((H, 2 * PART * PART), jnp.float32),
             jax.ShapeDtypeStruct((2, 5, C, C), jnp.bfloat16),
         ],
         name="bias_tile",
-    )(pair_input, ln_gain, head_bias, *weights)
-    tile = by_core(tile[:H].reshape(H, PART, 2, PART), 2, core).astype(jnp.bfloat16)
+    )(pair_input, ln_gain, w_bias, *weights)
+    tile = by_core(tile.reshape(H, PART, 2, PART), 2, core).astype(jnp.bfloat16)
     tile = jnp.pad(
         tile.transpose(1, 0, 2, 3).reshape(PART, HALF), ((0, 0), (0, 3 * C - HALF))
     )
@@ -270,15 +298,19 @@
     halves = halves.transpose(0, 2, 1, 3, 4).reshape(8, 2 * OWN, PART, C)
     xa = to_columns(jnp.concatenate([halves, copies(tile)], axis=1))
     xs = lax.ppermute(xa, "row", PARTNER)
-    tile = xa[:, 2 * OWN :].transpose(0, 2, 1, 3).reshape(8, PART, 3 * C)[..., :HALF]
-    tile = tile.reshape(8, PART, H, 2, PART).transpose(2, 1, 3, 0, 4).reshape(H, PART, N)
-    tile = tile.reshape(H, PART, CHUNKS, C).transpose(0, 2, 1, 3)
-    tile, xs = lax.optimization_barrier((tile, xs))
-    bias = to_rows(copies(tile))
-    after, tile = attend(0, xa, xs, mask_row, ln_gain, head_bias, weights, bias)
+    tile = pl.pallas_call(
+        spread_kernel,
+        grid=(1,),
+        in_specs=[pl.BlockSpec((8, 13, PART, C), lambda step: (0, 0, 0, 0))],
+        out_specs=pl.BlockSpec((8, H, CHUNKS, PART, C), lambda step: (0,) * 5),
+        out_shape=jax.ShapeDtypeStruct((8, H, CHUNKS, PART, C), jnp.bfloat16),
+        name="spread_tile",
+    )(xa)
+    bias = to_rows(tile)
+    after, tile = attend(0, xa, xs, mask_row, ln_gain, w_bias, weights, bias)
 
     sent = after.reshape(8, OWN, 2, 8, OWN, C).transpose(3, 0, 2, 4, 1, 5)
-    tile = tile[:, :, :H].astype(jnp.bfloat16).transpose(0, 1, 2, 3).reshape(2 * OWN, 2 * CHUNKS, C)
+    tile = tile.astype(jnp.bfloat16).reshape(2 * OWN, 2 * CHUNKS, C)
     tile = jnp.broadcast_to(
         tile.transpose(1, 0, 2).reshape(1, 100, C), (64, 100, C)
     )
@@ -287,7 +319,7 @@
     xa = xa.transpose(0, 2, 1, 3, 4).reshape(8, 2 * OWN, PART, C)
     xs = lax.ppermute(xa, "row", PARTNER)
     bias = got[:, 2 * OWN * OWN :].reshape(8, 8, 2, CHUNKS, 2, OWN, C)
-    bias = bias.transpose(2, 4, 0, 1, 5, 3, 6).reshape(2, N, N)
+    bias = bias.transpose(0, 2, 4, 3, 1, 5, 6).reshape(8, 2, 2, CHUNKS, PART, C)
     (after,) = attend(1, xa, xs, mask_row, ln_gain, None, weights, bias)
     block = by_core(to_rows(after), 2, core)
     return block.transpose(3, 2, 0, 1, 4).reshape(PART, 2 * PART, C)

time: 175 us -> 162 us (0.926)
  local copies, waits for them, and re-layouts: 21.7 us -> 8.16 us
  Pallas kernels: 39.3 us -> 43.5 us
  blocking collectives: 83.2 us -> 81.4 us
    reshape x8 -> x5, local copies, waits for them, and re-layouts: 6.21 us -> 1.34 us  [the longest x2 1.01 us: body(): tile = by_core(tile.reshape(H, PART, 2, PART), 2, core).astype(jnp.bfloat16)]
    all_to_all x1, waiting for transfers between devices: 22.4 us -> 17.9 us  [to_rows(): lax.all_to_all(flat, 'row', 0, 0, axis_index_groups=SAME_CORE, tiled=True)]
    ppermute x2, waiting for transfers between devices: 0.01 us -> 3.21 us  [body(): xs = lax.ppermute(xa, 'row', PARTNER)]
    pallas_call x0 -> x1, Pallas kernels: none -> 2.7 us  [body(): pl.pallas_call(spread_kernel, grid=(1,), in_specs=[pl.BlockSpec((8, 13, P...]
    all_to_all x1, blocking collectives: 40.9 us -> 38.4 us  [to_all(): lax.all_to_all(array, ('row', 'col'), 0, 0, axis_index_groups=CORE_PLANES...]
    transpose x1, local copies, waits for them, and re-layouts: 2.7 us -> 0.33 us  [body(): bias = bias.transpose(0, 2, 4, 3, 1, 5, 6).reshape(8, 2, 2, CHUNKS, PART, C)]
    another operation x1 -> x0, local copies, waits for them, and re-layouts: 1.81 us -> none  [body(): tile = tile.reshape(H, PART, CHUNKS, C).transpose(0, 2, 1, 3)]
  transfers between devices with their start and end apart: 3 -> 3, of which waited for: 1 -> 3; matrix products, arithmetic and copies ran while one was open for 7% -> 1% of each run, Pallas kernels for 0% -> 0%
where the time goes in v4:
time: 162 us; the launch traced here: 161 us
  blocking collectives  81.4 us (50%)
  Pallas kernels  43.5 us (27%)
  waiting for transfers between devices  21.1 us (13%)
  local copies, waits for them, and re-layouts  8.16 us (5%)
  starting transfers between devices  5.25 us (3%)
    all_to_all x1, blocking collectives, to_all(): lax.all_to_all(array, ('row', 'col'), 0, 0, axis_index_groups=CORE_PLANES...  38.4 us
    pallas_call x2, Pallas kernels, attend(): pl.pallas_call((start_kernel, end_kernel)[section], grid=(OWN,), in_specs...  36 us
    all_to_all x1, blocking collectives, to_columns(): return lax.all_to_all(flat, 'col', 0, 0, tiled=True).reshape(array.shape)  24.5 us
    all_to_all x1, blocking collectives, to_rows(): lax.all_to_all(flat, 'row', 0, 0, axis_index_groups=SAME_CORE, tiled=True)  18.5 us
    all_to_all x1, waiting for transfers between devices, to_rows(): lax.all_to_all(flat, 'row', 0, 0, axis_index_groups=SAME_CORE, tiled=True)  17.9 us
    all_to_all x1, starting transfers between devices, to_rows(): lax.all_to_all(flat, 'row', 0, 0, axis_index_groups=SAME_CORE, tiled=True)  4.9 us
    pallas_call x1, Pallas kernels, body(): pl.pallas_call(tile_kernel, grid=(5,), in_specs=[pl.BlockSpec((8, 2 * PAR...  4.84 us
  transfers between devices with their start and end apart: 3, of which 3 were waited for; matrix products, arithmetic and copies ran while one was open for 1% of the time, Pallas kernels for 0%

profile of v4, /device:TPU:8, one launch (start us, length us, event | category | flops | bytes accessed | tf_op | source)
XLA Modules:
  0.0 161.1 jit_solution(6155462943264395000)
XLA Ops:
  0.0 1.5 copy.52.head_bias.next_bias
  1.5 4.8 %bias_tile.1 = (f32[4,3200]{1,0:T(4,128)}, bf16[2,5,128,128]{3,2,1,0:T(8,128)(2,1)}) custom-call(bf16[40,80,128]{2,1,0:T(8,128)(2,1)} %block.1, f32[2,128]{1,0:T(2,128)} %gain.5, bf16[2,128,4]{2,1,0:T(8,128)(2,1)} %copy.52.head_bias.next_bias, bf16[2,128,128]{2,1,0:T(8,128)(2,1)} %rest_0_.1, bf16[2,128,128]{2,1,0:T(8,128)(2,1)} %rest_1_.1, ...), custom_call_target="tpu_custom_call" | custom-call | tf_op jit(solution)/shard_map/bias_tile/pallas_call | solution.py:273
  6.3 1.0 reshape.68
  7.3 0.1 copy.53
  7.4 0.6 rev.16
  8.0 0.1 fusion.2
  8.1 0.1 reshape.69
  8.3 0.0 copy-done.4
  8.3 0.2 fusion
  8.5 0.1 copy.51
  8.6 0.1 pad_maximum_fusion.1
  8.7 24.5 %all_to_all.20 = bf16[8,520,128]{2,1,0:T(8,128)(2,1)} all-to-all(bf16[8,520,128]{2,1,0:T(8,128)(2,1)S(1)} %bitcast.42), channel_id=1, replica_groups=mesh['row'=16,'col'=8] {'col'}, dimensions={0} | all-to-all | bytes 2129920 | tf_op jit(solution)/shard_map/all_to_all | solution.py:250
  33.2 2.7 %spread_tile.1 = bf16[8,4,5,40,128]{4,3,2,1,0:T(8,128)(2,1)} custom-call(bf16[8,13,40,128]{3,2,1,0:T(8,128)(2,1)} %bitcast.33), custom_call_target="tpu_custom_call" | custom-call | tf_op jit(solution)/shard_map/spread_tile/pallas_call | solution.py:301
  35.9 0.0 copy-start.3
  35.9 4.9 %all-to-all-start.1 = ((bf16[8,800,128]{2,1,0:T(8,128)(2,1)}), bf16[8,800,128]{2,1,0:T(8,128)(2,1)S(1)}, u32[]{:S(2)}, u32[]{:S(2)}) async-start(bf16[8,800,128]{2,1,0:T(8,128)(2,1)} %bitcast.39), calls=%async_computation.1 | async-start | bytes 3276800 | tf_op jit(solution)/shard_map/all_to_all | solution.py:255
  40.8 0.0 copy-done
  40.8 0.1 collective-permute-start
  40.9 0.0 copy-done.5
  40.9 0.1 reshape.73
  41.1 0.1 reshape.74.mask
  41.2 2.5 %collective-permute-done.far_q.far_o = bf16[8,13,40,128]{3,2,1,0:T(8,128)(2,1)} collective-permute-done((bf16[8,13,40,128]{3,2,1,0:T(8,128)(2,1)S(1)}, bf16[8,13,40,128]{3,2,1,0:T(8,128)(2,1)}, u32[]{:S(2)}, u32[]{:S(2)}) %collective-permute-start) | collective-permute-done | bytes 1064992 | tf_op jit(solution)/shard_map/ppermute | solution.py:300
  43.7 17.9 %all-to-all-done.1 = bf16[8,800,128]{2,1,0:T(8,128)(2,1)S(1)} async-done(((bf16[8,800,128]{2,1,0:T(8,128)(2,1)}), bf16[8,800,128]{2,1,0:T(8,128)(2,1)S(1)}, u32[]{:S(2)}, u32[]{:S(2)}) %all-to-all-start.1) | async-done | bytes 1638432 | tf_op jit(solution)/shard_map/all_to_all | solution.py:255
  61.6 0.0 copy-done.1
  61.6 0.0 copy-done.2
  61.6 0.0 copy-done.3
  61.6 18.4 %start_node.1 = (bf16[8,5,2,40,128]{4,3,2,1,0:T(8,128)(2,1)S(1)}, f32[2,5,4,320]{3,2,1,0:T(4,128)S(1)}) custom-call(bf16[8,13,40,128]{3,2,1,0:T(8,128)(2,1)S(1)} %bitcast.35, bf16[8,13,40,128]{3,2,1,0:T(8,128)(2,1)S(1)} %bitcast.36, bf16[8,13,40,128]{3,2,1,0:T(8,128)(2,1)} %collective-permute-done.far_q.far_o, ...), custom_call_target="tpu_custom_call" | custom-call | flops 8000000000 | bytes 6000000 | tf_op jit(solution)/shard_map/start_node/pallas_call | solution.py:227
  80.0 0.2 copy.58
  80.3 0.2 copy.59
  80.5 0.1 reshape.79
  80.6 0.5 copy.61
  81.2 0.2 broadcast_in_dim.25
  81.4 0.7 pad_maximum_fusion
  82.2 38.4 %all_to_all.21 = bf16[64,150,128]{2,1,0:T(8,128)(2,1)S(1)} all-to-all(bf16[64,150,128]{2,1,0:T(8,128)(2,1)S(1)} %pad_maximum_fusion), channel_id=1, replica_groups={{0,1,2,3,4,5,6,7,16,17,18,19,20,21,22,23,32,33,34,35,36,37,38,39,48,49,..., dimensions={0} | all-to-all | bytes 4915200 | tf_op jit(solution)/shard_map/all_to_all | solution.py:260
  120.6 0.1 slice.8
  120.7 0.2 copy.72
  120.9 0.1 copy.63
  121.0 0.1 copy.67.own_q.own_o
  121.2 0.3 collective-permute-start.1
  121.4 0.7 slice.9
  122.1 0.4 copy.73
  122.5 0.3 copy.66
  122.8 0.2 copy.69.rest_1_
  123.1 0.7 collective-permute-done.1.far_q.far_o
  123.7 17.6 %end_node.1 = bf16[8,5,2,40,128]{4,3,2,1,0:T(8,128)(2,1)S(1)} custom-call(bf16[8,10,40,128]{3,2,1,0:T(8,128)(2,1)S(1)} %copy.67.own_q.own_o, bf16[8,10,40,128]{3,2,1,0:T(8,128)(2,1)S(1)} %copy.67.own_q.own_o, bf16[8,10,40,128]{3,2,1,0:T(8,128)(2,1)S(1)} %collective-permute-done.1.far_q.far_o, ...), custom_call_target="tpu_custom_call" | custom-call | flops 8000000000 | bytes 6000000 | tf_op jit(solution)/shard_map/end_node/pallas_call | solution.py:227
  141.3 18.5 %all_to_all.22 = bf16[8,400,128]{2,1,0:T(8,128)(2,1)S(1)} all-to-all(bf16[8,400,128]{2,1,0:T(8,128)(2,1)S(1)} %bitcast.38), channel_id=1, replica_groups={{0,16,32,48,64,80,96,112},{8,24,40,56,72,88,104,120},{1,17,33,49,65,81,..., dimensions={0} | all-to-all | bytes 1638400 | tf_op jit(solution)/shard_map/all_to_all | solution.py:255
  159.8 0.2 fusion.1
  160.0 0.1 copy.70
  160.1 1.0 copy.71
  (16 shorter events, 0.2 us)
Async XLA Ops:
  0.0 8.3 %copy-start.4 = (bf16[40,80,128]{2,1,0:T(8,128)(2,1)S(1)}, bf16[40,80,128]{2,1,0:T(8,128)(2,1)}, u32[]{:S(2)}) copy-start(bf16[40,80,128]{2,1,0:T(8,128)(2,1)} %block.1) | copy-start | bytes 2457604
  35.9 4.9 %copy-start = (bf16[8,520,128]{2,1,0:T(8,128)(2,1)S(1)}, bf16[8,520,128]{2,1,0:T(8,128)(2,1)}, u32[]{:S(2)}) copy-start(bf16[8,520,128]{2,1,0:T(8,128)(2,1)} %all_to_all.20) | copy-start | bytes 3194884
  35.9 5.0 %copy-start.5 = (s32[640]{0:T(1024)S(1)}, s32[640]{0:T(1024)}, u32[]{:S(2)}) copy-start(s32[640]{0:T(1024)} %param.10) | copy-start | bytes 7684
  35.9 25.7 %copy-start.1 = (bf16[2,128,4]{2,1,0:T(8,128)(2,1)S(1)}, bf16[2,128,4]{2,1,0:T(8,128)(2,1)}, u32[]{:S(2)}) copy-start(bf16[2,128,4]{2,1,0:T(8,128)(2,1)} %copy.52.head_bias.next_bias) | copy-start | bytes 6148
  35.9 25.7 %copy-start.2 = (f32[2,128]{1,0:T(2,128)S(1)}, f32[2,128]{1,0:T(2,128)}, u32[]{:S(2)}) copy-start(f32[2,128]{1,0:T(2,128)} %gain.5) | copy-start | bytes 3076
  35.9 25.7 %copy-start.3 = (bf16[2,5,128,128]{3,2,1,0:T(8,128)(2,1)S(1)}, bf16[2,5,128,128]{3,2,1,0:T(8,128)(2,1)}, u32[]{:S(2)}) copy-start(bf16[2,5,128,128]{3,2,1,0:T(8,128)(2,1)} %get-tuple-element.10.rest_0_) | copy-start | bytes 983044
  35.9 25.7 %all-to-all-start.1 = ((bf16[8,800,128]{2,1,0:T(8,128)(2,1)}), bf16[8,800,128]{2,1,0:T(8,128)(2,1)S(1)}, u32[]{:S(2)}, u32[]{:S(2)}) async-start(bf16[8,800,128]{2,1,0:T(8,128)(2,1)} %bitcast.39), calls=%async_computation.1 | async-start | bytes 3276800 | tf_op jit(solution)/shard_map/all_to_all | solution.py:255
  40.8 2.9 %collective-permute-start = (bf16[8,13,40,128]{3,2,1,0:T(8,128)(2,1)S(1)}, bf16[8,13,40,128]{3,2,1,0:T(8,128)(2,1)}, u32[]{:S(2)}, u32[]{:S(2)}) collective-permute-start(bf16[8,13,40,128]{3,2,1,0:T(8,128)(2,1)S(1)} %bitcast.34), channel_id=1, source_target_pairs={{0,8},{8,0},{16,24},{24,16},{32,40},{40,32},{48,56},{56,48},{64,72... | collective-permute-start | bytes 3194888 | tf_op jit(solution)/shard_map/ppermute | solution.py:300
  121.2 2.6 %collective-permute-start.1 = (bf16[8,10,40,128]{3,2,1,0:T(8,128)(2,1)S(1)}, bf16[8,10,40,128]{3,2,1,0:T(8,128)(2,1)S(1)}, u32[]{:S(2)}, u32[]{:S(2)}) collective-permute-start(bf16[8,10,40,128]{3,2,1,0:T(8,128)(2,1)S(1)} %copy.67.own_q.own_o), channel_id=1, source_target_pairs={{0,8},{8,0},{16,24},{24,16},{32,40},{40,32},{48,56},{56,48},{64,72... | collective-permute-start | bytes 2457608 | tf_op jit(solution)/shard_map/ppermute | solution.py:320

commit v5 on v4

--- a/solution.py
+++ b/solution.py
@@ -98,8 +98,12 @@
     scores = [score(p[0], jnp.concatenate(p[2], axis=0)) for p in pre]
     summed = []
     for p, sc in zip(pre, scores):
-        weights = [softmax(sc[:, h * N : (h + 1) * N], bias_s[h]) for h in range(H)]
-        summed.append(mix(weights, p[3]))
+        parts = []
+        for first in (0, 160):
+            piece = slice(first, first + 160)
+            weights = [softmax(sc[piece, h * N : (h + 1) * N], bias_s[h, piece]) for h in range(H)]
+            parts.append(mix(weights, p[3]))
+        summed.append(jnp.concatenate(parts, axis=0))
     return [finish(q, m, p[1], w_out) for (q, o), m, p in zip(rows, summed, pre)]
 
 
@@ -168,9 +172,7 @@
 
 
 def head_rows(head_bias, normed):
-    return lax.dot_general(
-        head_bias, normed, (((0,), (1,)), ((), ())), preferred_element_type=jnp.float32
-    )
+    return lax.dot_general(head_bias, normed, CONTRACT_LAST, preferred_element_type=jnp.float32)
 
 
 def merged(block):
@@ -180,12 +182,9 @@
 def tile_kernel(block, gain, head_bias, *rest):
     weights, (tile, stacked) = rest[:5], rest[5:]
 
-    @pl.when(pl.program_id(0) == 0)
-    def _():
-        for position, weight in enumerate(weights):
-            stacked[:, position] = weight[...]
-
-    tokens = block[...].astype(jnp.float32).reshape(8 * 2 * PART, C)
+    for position, weight in enumerate(weights):
+        stacked[:, position] = weight[...]
+    tokens = block[...].astype(jnp.float32).reshape(2 * PART * PART, C)
     normed = normalize(tokens, gain[0:1])
     tile[...] = head_rows(head_bias[0], normed)
 
@@ -268,19 +267,15 @@
     core = lax.axis_index("row") % 2
     mask_row = jnp.where(token_mask > 0, 0.0, masked_score).astype(jnp.float32)
     mask_row = by_core(mask_row.reshape(8, 2, PART), 1, core).transpose(1, 0, 2).reshape(1, N)
+    head_bias = w_bias.transpose(0, 2, 1)
     weights = [w_query, w_key, w_value, w_gate, w_out]
 
     tile, weights = pl.pallas_call(
         tile_kernel,
-        grid=(5,),
-        in_specs=[
-            pl.BlockSpec((8, 2 * PART, C), lambda step: (step, 0, 0)),
-            whole(ln_gain),
-            whole(w_bias),
-        ]
-        + [whole(weight) for weight in weights],
+        grid=(1,),
+        in_specs=[whole(member) for member in (pair_input, ln_gain, head_bias, *weights)],
         out_specs=[
-            pl.BlockSpec((H, 16 * PART), lambda step: (0, step)),
+            pl.BlockSpec((H, 2 * PART * PART), lambda step: (0, 0)),
             pl.BlockSpec((2, 5, C, C), lambda step: (0, 0, 0, 0)),
         ],
         out_shape=[
@@ -288,7 +283,7 @@
             jax.ShapeDtypeStruct((2, 5, C, C), jnp.bfloat16),
         ],
         name="bias_tile",
-    )(pair_input, ln_gain, w_bias, *weights)
+    )(pair_input, ln_gain, head_bias, *weights)
     tile = by_core(tile.reshape(H, PART, 2, PART), 2, core).astype(jnp.bfloat16)
     tile = jnp.pad(
         tile.transpose(1, 0, 2, 3).reshape(PART, HALF), ((0, 0), (0, 3 * C - HALF))
@@ -307,7 +302,7 @@
         name="spread_tile",
     )(xa)
     bias = to_rows(tile)
-    after, tile = attend(0, xa, xs, mask_row, ln_gain, w_bias, weights, bias)
+    after, tile = attend(0, xa, xs, mask_row, ln_gain, head_bias, weights, bias)
 
     sent = after.reshape(8, OWN, 2, 8, OWN, C).transpose(3, 0, 2, 4, 1, 5)
     tile = tile.astype(jnp.bfloat16).reshape(2 * OWN, 2 * CHUNKS, C)

time: 162 us -> 156 us (0.963)
  Pallas kernels: 43.5 us -> 39.3 us
    pallas_call x2, Pallas kernels: 36 us -> 33.6 us  [attend(): pl.pallas_call((start_kernel, end_kernel)[section], grid=(OWN,), in_specs...]
    pallas_call x1, Pallas kernels: 4.84 us -> 3.02 us  [body(): pl.pallas_call(tile_kernel, grid=(1,), in_specs=[whole(member) for member...]
where the time goes in v5:
time: 156 us; the launch traced here: 155 us
  blocking collectives  81.4 us (52%)
  Pallas kernels  39.3 us (25%)
  waiting for transfers between devices  21.1 us (14%)
  local copies, waits for them, and re-layouts  6.67 us (4%)
  starting transfers between devices  5.25 us (3%)
    all_to_all x1, blocking collectives, to_all(): lax.all_to_all(array, ('row', 'col'), 0, 0, axis_index_groups=CORE_PLANES...  38.4 us
    pallas_call x2, Pallas kernels, attend(): pl.pallas_call((start_kernel, end_kernel)[section], grid=(OWN,), in_specs...  33.6 us
    all_to_all x1, blocking collectives, to_columns(): return lax.all_to_all(flat, 'col', 0, 0, tiled=True).reshape(array.shape)  24.5 us
    all_to_all x1, blocking collectives, to_rows(): lax.all_to_all(flat, 'row', 0, 0, axis_index_groups=SAME_CORE, tiled=True)  18.5 us
    all_to_all x1, waiting for transfers between devices, to_rows(): lax.all_to_all(flat, 'row', 0, 0, axis_index_groups=SAME_CORE, tiled=True)  17.9 us
    all_to_all x1, starting transfers between devices, to_rows(): lax.all_to_all(flat, 'row', 0, 0, axis_index_groups=SAME_CORE, tiled=True)  4.9 us
    ppermute x2, waiting for transfers between devices, body(): xs = lax.ppermute(xa, 'row', PARTNER)  3.21 us
  transfers between devices with their start and end apart: 3, of which 3 were waited for; matrix products, arithmetic and copies ran while one was open for 1% of the time, Pallas kernels for 0%

profile of v5, /device:TPU:8, one launch (start us, length us, event | category | flops | bytes accessed | tf_op | source)
XLA Modules:
  0.0 155.4 jit_solution(10283774685582823014)
XLA Ops:
  0.0 0.0 copy-start.4
  0.0 3.0 %bias_tile.1 = (f32[4,3200]{1,0:T(4,128)}, bf16[2,5,128,128]{3,2,1,0:T(8,128)(2,1)}) custom-call(bf16[40,80,128]{2,1,0:T(8,128)(2,1)} %block.1, f32[2,128]{1,0:T(2,128)} %gain.5, bf16[2,4,128]{2,1,0:T(4,128)(2,1)} %bitcast.40, bf16[2,128,128]{2,1,0:T(8,128)(2,1)} %rest_0_.1, bf16[2,128,128]{2,1,0:T(8,128)(2,1)} %rest_1_.1, bf16[2,128,128]{2,1,0:T(8,128)(2,1)} %rest_2_.1, ...), custom_call_target="tpu_custom_call" | custom-call | tf_op jit(solution)/shard_map/bias_tile/pallas_call | solution.py:273
  3.0 1.0 reshape.68
  4.0 0.1 copy.46
  4.1 0.6 rev.16
  4.7 0.1 fusion.2
  4.8 0.1 reshape.69
  5.0 0.0 copy-done.4
  5.0 0.2 fusion
  5.2 0.1 copy.45
  5.3 0.1 pad_maximum_fusion.1
  5.4 24.5 %all_to_all.20 = bf16[8,520,128]{2,1,0:T(8,128)(2,1)} all-to-all(bf16[8,520,128]{2,1,0:T(8,128)(2,1)S(1)} %bitcast.45), channel_id=1, replica_groups=mesh['row'=16,'col'=8] {'col'}, dimensions={0} | all-to-all | bytes 2129920 | tf_op jit(solution)/shard_map/all_to_all | solution.py:249
  29.9 2.7 %spread_tile.1 = bf16[8,4,5,40,128]{4,3,2,1,0:T(8,128)(2,1)} custom-call(bf16[8,13,40,128]{3,2,1,0:T(8,128)(2,1)} %bitcast.34), custom_call_target="tpu_custom_call" | custom-call | tf_op jit(solution)/shard_map/spread_tile/pallas_call | solution.py:296
  32.6 0.0 copy-start.3
  32.6 4.9 %all-to-all-start.1 = ((bf16[8,800,128]{2,1,0:T(8,128)(2,1)}), bf16[8,800,128]{2,1,0:T(8,128)(2,1)S(1)}, u32[]{:S(2)}, u32[]{:S(2)}) async-start(bf16[8,800,128]{2,1,0:T(8,128)(2,1)} %bitcast.42), calls=%async_computation.1 | async-start | bytes 3276800 | tf_op jit(solution)/shard_map/all_to_all | solution.py:254
  37.5 0.0 copy-done
  37.5 0.1 collective-permute-start
  37.6 0.0 copy-done.5
  37.6 0.1 reshape.73
  37.8 0.1 reshape.74.mask
  37.9 2.5 %collective-permute-done.far_q.far_o = bf16[8,13,40,128]{3,2,1,0:T(8,128)(2,1)} collective-permute-done((bf16[8,13,40,128]{3,2,1,0:T(8,128)(2,1)S(1)}, bf16[8,13,40,128]{3,2,1,0:T(8,128)(2,1)}, u32[]{:S(2)}, u32[]{:S(2)}) %collective-permute-start) | collective-permute-done | bytes 1064992 | tf_op jit(solution)/shard_map/ppermute | solution.py:295
  40.4 17.9 %all-to-all-done.1 = bf16[8,800,128]{2,1,0:T(8,128)(2,1)S(1)} async-done(((bf16[8,800,128]{2,1,0:T(8,128)(2,1)}), bf16[8,800,128]{2,1,0:T(8,128)(2,1)S(1)}, u32[]{:S(2)}, u32[]{:S(2)}) %all-to-all-start.1) | async-done | bytes 1638432 | tf_op jit(solution)/shard_map/all_to_all | solution.py:254
  58.3 0.0 copy-done.1
  58.3 0.0 copy-done.2
  58.3 0.0 copy-done.3
  58.3 17.0 %start_node.1 = (bf16[8,5,2,40,128]{4,3,2,1,0:T(8,128)(2,1)S(1)}, f32[2,5,4,320]{3,2,1,0:T(4,128)S(1)}) custom-call(bf16[8,13,40,128]{3,2,1,0:T(8,128)(2,1)S(1)} %bitcast.36, bf16[8,13,40,128]{3,2,1,0:T(8,128)(2,1)S(1)} %bitcast.37, bf16[8,13,40,128]{3,2,1,0:T(8,128)(2,1)} %collective-permute-done.far_q.far_o, ...), custom_call_target="tpu_custom_call" | custom-call | flops 8000000000 | bytes 6000000 | tf_op jit(solution)/shard_map/start_node/pallas_call | solution.py:226
  75.3 0.2 copy.50
  75.5 0.2 copy.51
  75.8 0.1 reshape.79
  75.9 0.5 copy.53
  76.5 0.2 broadcast_in_dim.25
  76.7 0.7 pad_maximum_fusion
  77.4 38.4 %all_to_all.21 = bf16[64,150,128]{2,1,0:T(8,128)(2,1)S(1)} all-to-all(bf16[64,150,128]{2,1,0:T(8,128)(2,1)S(1)} %pad_maximum_fusion), channel_id=1, replica_groups={{0,1,2,3,4,5,6,7,16,17,18,19,20,21,22,23,32,33,34,35,36,37,38,39,48,49,..., dimensions={0} | all-to-all | bytes 4915200 | tf_op jit(solution)/shard_map/all_to_all | solution.py:259
  115.9 0.1 slice.8
  116.0 0.2 copy.64
  116.2 0.1 copy.55
  116.3 0.1 copy.59.own_q.own_o
  116.4 0.3 collective-permute-start.1
  116.7 0.7 slice.9
  117.4 0.4 copy.65
  117.8 0.3 copy.58
  118.1 0.2 copy.61.rest_1_
  118.3 0.7 collective-permute-done.1.far_q.far_o
  119.0 16.6 %end_node.1 = bf16[8,5,2,40,128]{4,3,2,1,0:T(8,128)(2,1)S(1)} custom-call(bf16[8,10,40,128]{3,2,1,0:T(8,128)(2,1)S(1)} %copy.59.own_q.own_o, bf16[8,10,40,128]{3,2,1,0:T(8,128)(2,1)S(1)} %copy.59.own_q.own_o, bf16[8,10,40,128]{3,2,1,0:T(8,128)(2,1)S(1)} %collective-permute-done.1.far_q.far_o, ...), custom_call_target="tpu_custom_call" | custom-call | flops 8000000000 | bytes 6000000 | tf_op jit(solution)/shard_map/end_node/pallas_call | solution.py:226
  135.6 18.5 %all_to_all.22 = bf16[8,400,128]{2,1,0:T(8,128)(2,1)S(1)} all-to-all(bf16[8,400,128]{2,1,0:T(8,128)(2,1)S(1)} %bitcast.39), channel_id=1, replica_groups={{0,16,32,48,64,80,96,112},{8,24,40,56,72,88,104,120},{1,17,33,49,65,81,..., dimensions={0} | all-to-all | bytes 1638400 | tf_op jit(solution)/shard_map/all_to_all | solution.py:254
  154.1 0.2 fusion.1
  154.3 0.1 copy.62
  154.4 1.0 copy.63
  (15 shorter events, 0.2 us)
Async XLA Ops:
  0.0 5.0 %copy-start.4 = (bf16[40,80,128]{2,1,0:T(8,128)(2,1)S(1)}, bf16[40,80,128]{2,1,0:T(8,128)(2,1)}, u32[]{:S(2)}) copy-start(bf16[40,80,128]{2,1,0:T(8,128)(2,1)} %block.1) | copy-start | bytes 2457604
  32.6 4.9 %copy-start = (bf16[8,520,128]{2,1,0:T(8,128)(2,1)S(1)}, bf16[8,520,128]{2,1,0:T(8,128)(2,1)}, u32[]{:S(2)}) copy-start(bf16[8,520,128]{2,1,0:T(8,128)(2,1)} %all_to_all.20) | copy-start | bytes 3194884
  32.6 5.0 %copy-start.5 = (s32[640]{0:T(1024)S(1)}, s32[640]{0:T(1024)}, u32[]{:S(2)}) copy-start(s32[640]{0:T(1024)} %param.10) | copy-start | bytes 7684
  32.6 25.7 %copy-start.1 = (bf16[2,128,4]{1,2,0:T(4,128)(2,1)S(1)}, bf16[2,128,4]{1,2,0:T(4,128)(2,1)}, u32[]{:S(2)}) copy-start(bf16[2,128,4]{1,2,0:T(4,128)(2,1)} %param.16) | copy-start | bytes 6148
  32.6 25.7 %copy-start.2 = (f32[2,128]{1,0:T(2,128)S(1)}, f32[2,128]{1,0:T(2,128)}, u32[]{:S(2)}) copy-start(f32[2,128]{1,0:T(2,128)} %gain.5) | copy-start | bytes 3076
  32.6 25.7 %copy-start.3 = (bf16[2,5,128,128]{3,2,1,0:T(8,128)(2,1)S(1)}, bf16[2,5,128,128]{3,2,1,0:T(8,128)(2,1)}, u32[]{:S(2)}) copy-start(bf16[2,5,128,128]{3,2,1,0:T(8,128)(2,1)} %get-tuple-element.10.rest_0_) | copy-start | bytes 983044
  32.6 25.7 %all-to-all-start.1 = ((bf16[8,800,128]{2,1,0:T(8,128)(2,1)}), bf16[8,800,128]{2,1,0:T(8,128)(2,1)S(1)}, u32[]{:S(2)}, u32[]{:S(2)}) async-start(bf16[8,800,128]{2,1,0:T(8,128)(2,1)} %bitcast.42), calls=%async_computation.1 | async-start | bytes 3276800 | tf_op jit(solution)/shard_map/all_to_all | solution.py:254
  37.5 2.9 %collective-permute-start = (bf16[8,13,40,128]{3,2,1,0:T(8,128)(2,1)S(1)}, bf16[8,13,40,128]{3,2,1,0:T(8,128)(2,1)}, u32[]{:S(2)}, u32[]{:S(2)}) collective-permute-start(bf16[8,13,40,128]{3,2,1,0:T(8,128)(2,1)S(1)} %bitcast.35), channel_id=1, source_target_pairs={{0,8},{8,0},{16,24},{24,16},{32,40},{40,32},{48,56},{56,48},{64,72... | collective-permute-start | bytes 3194888 | tf_op jit(solution)/shard_map/ppermute | solution.py:295
  116.4 2.6 %collective-permute-start.1 = (bf16[8,10,40,128]{3,2,1,0:T(8,128)(2,1)S(1)}, bf16[8,10,40,128]{3,2,1,0:T(8,128)(2,1)S(1)}, u32[]{:S(2)}, u32[]{:S(2)}) collective-permute-start(bf16[8,10,40,128]{3,2,1,0:T(8,128)(2,1)S(1)} %copy.59.own_q.own_o), channel_id=1, source_target_pairs={{0,8},{8,0},{16,24},{24,16},{32,40},{40,32},{48,56},{56,48},{64,72... | collective-permute-start | bytes 2457608 | tf_op jit(solution)/shard_map/ppermute | solution.py:315

commit v6 on v5

--- a/solution.py
+++ b/solution.py
@@ -107,86 +107,108 @@
     return [finish(q, m, p[1], w_out) for (q, o), m, p in zip(rows, summed, pre)]
 
 
-def start_kernel(own_q, own_o, far_q, far_o, mask, gain, next_bias, *rest):
+def start_kernel(xa, xs, mask, gain, next_bias, *rest):
     weights, bias = rest[:2]
     out, tile, bias_s = rest[2:]
 
-    @pl.when(pl.program_id(0) == 0)
-    def _():
-        for place in range(8):
-            for head in range(H):
-                for part in range(CHUNKS):
-                    lanes = slice(part * C, (part + 1) * C)
-                    bias_s[head, place * PART : (place + 1) * PART, lanes] = (
-                        bias[place, head, part].astype(jnp.float32) * LOG2E + mask[:, lanes]
-                    )
-
-    afters = attend_rows(
-        ((merged(own_q), merged(own_o)), (merged(far_q), merged(far_o))),
-        bias_s,
-        gain[0:1],
-        *(weights[position] for position in range(5)),
-    )
-    for slot in range(2):
-        after = afters[slot]
-        out[:, 0, slot] = after.reshape(8, PART, C).astype(jnp.bfloat16)
-        normed = normalize(after, gain[1:2])
-        tile[slot, 0] = head_rows(next_bias[1], normed)
-
-
-def end_kernel(own_q, own_o, far_q, far_o, mask, gain, *rest):
+    for place in range(8):
+        for head in range(H):
+            for part in range(CHUNKS):
+                lanes = slice(part * C, (part + 1) * C)
+                bias_s[head, place * PART : (place + 1) * PART, lanes] = (
+                    bias[place, head, part].astype(jnp.float32) * LOG2E + mask[:, lanes]
+                )
+
+    def pair(step):
+        afters = attend_rows(
+            row_pair(xa, xs, step),
+            bias_s,
+            gain[0:1],
+            *(weights[0, position] for position in range(5)),
+        )
+        for slot in range(2):
+            after = afters[slot]
+            out[:, step, slot] = after.reshape(8, PART, C).astype(jnp.bfloat16)
+            normed = normalize(after, gain[1:2])
+            tile[slot, step] = head_rows(next_bias[1], normed)
+
+    pair(0)
+    pl.loop(1, OWN)(pair)
+
+
+def end_kernel(xa, xs, mask, gain, *rest):
     weights, bias = rest[:2]
     out, bias_s, turned_s = rest[2:]
 
-    @pl.when(pl.program_id(0) == 0)
-    def _():
-        row = lax.broadcasted_iota(jnp.int32, (HALF, 2 * HALF), 0)
-        col = lax.broadcasted_iota(jnp.int32, (HALF, 2 * HALF), 1)
-        for pair in range(2):
-            for place in range(8):
-                for side in range(2):
-                    first = side * HALF + place * PART
-                    for part in range(CHUNKS):
-                        turned_s[pair, first : first + PART, part * C : (part + 1) * C] = bias[
-                            place, pair, side, part
-                        ].astype(jnp.float32)
-        for head in range(H):
-            chosen = jnp.where(row + (head % 2) * HALF == col, 1.0, 0.0).astype(jnp.bfloat16)
-            turned = lax.dot_general(
-                chosen,
-                turned_s[head // 2].astype(jnp.bfloat16),
-                CONTRACT_LAST,
-                preferred_element_type=jnp.float32,
-            )
-            bias_s[head] = turned * LOG2E + mask[...]
-
-    afters = attend_rows(
-        ((merged(own_q), merged(own_o)), (merged(far_q), merged(far_o))),
-        bias_s,
-        gain[1:2],
-        *(weights[position] for position in range(5)),
-    )
-    for slot in range(2):
-        after = afters[slot]
-        out[:, 0, slot] = after.reshape(8, PART, C).astype(jnp.bfloat16)
+    row = lax.broadcasted_iota(jnp.int32, (HALF, 2 * HALF), 0)
+    col = lax.broadcasted_iota(jnp.int32, (HALF, 2 * HALF), 1)
+    for pair in range(2):
+        for place in range(8):
+            for side in range(2):
+                first = side * HALF + place * PART
+                for part in range(CHUNKS):
+                    turned_s[pair, first : first + PART, part * C : (part + 1) * C] = bias[
+                        place, pair, side, part
+                    ].astype(jnp.float32)
+    for head in range(H):
+        chosen = jnp.where(row + (head % 2) * HALF == col, 1.0, 0.0).astype(jnp.bfloat16)
+        turned = lax.dot_general(
+            chosen,
+            turned_s[head // 2].astype(jnp.bfloat16),
+            CONTRACT_LAST,
+            preferred_element_type=jnp.float32,
+        )
+        bias_s[head] = turned * LOG2E + mask[...]
+
+    def pair(step):
+        afters = attend_rows(
+            row_pair(xa, xs, step),
+            bias_s,
+            gain[1:2],
+            *(weights[1, position] for position in range(5)),
+        )
+        for slot in range(2):
+            after = afters[slot]
+            out[:, step, slot] = after.reshape(8, PART, C).astype(jnp.bfloat16)
+
+    pair(0)
+    pl.loop(1, OWN)(pair)
 
 
 def head_rows(head_bias, normed):
     return lax.dot_general(head_bias, normed, CONTRACT_LAST, preferred_element_type=jnp.float32)
 
 
-def merged(block):
-    return block[...].astype(jnp.float32).reshape(HALF, C)
-
-
-def tile_kernel(block, gain, head_bias, *rest):
-    weights, (tile, stacked) = rest[:5], rest[5:]
-
+def row_pair(xa, xs, step):
+    own = [xa[:, position].astype(jnp.float32).reshape(HALF, C) for position in (step, OWN + step)]
+    far = [xs[:, position].astype(jnp.float32).reshape(HALF, C) for position in (OWN + step, step)]
+    return own, far
+
+
+def open_kernel(core, block, gain, head_bias, *rest):
+    weights, (send, stacked, tile_s) = rest[:5], rest[5:]
     for position, weight in enumerate(weights):
         stacked[:, position] = weight[...]
-    tokens = block[...].astype(jnp.float32).reshape(2 * PART * PART, C)
-    normed = normalize(tokens, gain[0:1])
-    tile[...] = head_rows(head_bias[0], normed)
+    tokens = block[...].astype(jnp.float32)
+    swapped = core[0] == 1
+    low, high = tokens[:, :PART], tokens[:, PART:]
+    halves = [jnp.where(swapped, high, low), jnp.where(swapped, low, high)]
+    for column in range(8):
+        for side in range(2):
+            for row in range(OWN):
+                send[column, side * OWN + row] = halves[side][column * OWN + row].astype(jnp.bfloat16)
+    normed = normalize(jnp.concatenate(halves, axis=1).reshape(2 * PART * PART, C), gain[0:1])
+    by_head = head_rows(head_bias[0], normed)
+    tile_s[...] = jnp.zeros_like(tile_s)
+    for row in range(PART):
+        for head in range(H):
+            tile_s[row : row + 1, head * 2 * PART : (head + 1) * 2 * PART] = by_head[
+                head : head + 1, row * 2 * PART : (row + 1) * 2 * PART
+            ]
+    for part in range(3):
+        lanes = tile_s[:, part * C : (part + 1) * C].astype(jnp.bfloat16)
+        for column in range(8):
+            send[column, 2 * OWN + part] = lanes
 
 
 def spread_kernel(arrived, spread):
@@ -210,26 +232,20 @@
 
 
 def attend(section, xa, xs, mask, gain, next_bias, weights, bias):
-    first = pl.BlockSpec((8, None, PART, C), lambda step: (0, step, 0, 0))
-    second = pl.BlockSpec((8, None, PART, C), lambda step: (0, OWN + step, 0, 0))
-    weight = pl.BlockSpec((None, 5, C, C), lambda step: (section, 0, 0, 0))
     out_shape = [jax.ShapeDtypeStruct((8, OWN, 2, PART, C), jnp.bfloat16)]
-    out_specs = [pl.BlockSpec((8, 1, 2, PART, C), lambda step: (0, step, 0, 0, 0))]
     scratch = [pltpu.VMEM((H, HALF, N), jnp.float32)]
-    shared = [mask, gain]
+    operands = [xa, xs, mask, gain]
     if section == 0:
-        shared.append(next_bias)
+        operands.append(next_bias)
         out_shape.append(jax.ShapeDtypeStruct((2, OWN, H, HALF), jnp.float32))
-        out_specs.append(pl.BlockSpec((2, 1, H, HALF), lambda step: (0, step, 0, 0)))
     else:
         scratch.append(pltpu.VMEM((2, N, 2 * HALF), jnp.float32))
+    operands += [weights, bias]
+    resident = pl.BlockSpec(memory_space=pltpu.VMEM)
     return pl.pallas_call(
         (start_kernel, end_kernel)[section],
-        grid=(OWN,),
-        in_specs=[first, second, second, first]
-        + [whole(member) for member in shared]
-        + [weight, whole(bias)],
-        out_specs=out_specs,
+        in_specs=[resident] * len(operands),
+        out_specs=[resident] * len(out_shape),
         scratch_shapes=scratch,
         out_shape=out_shape,
         compiler_params=pltpu.CompilerParams(vmem_limit_bytes=VMEM),
@@ -237,7 +253,7 @@
             flops=8_000_000_000, bytes_accessed=6_000_000, transcendentals=8_000_000
         ),
         name=("start_node", "end_node")[section],
-    )(xa, xa, xs, xs, *shared, weights, bias)
+    )(*operands)
 
 
 def by_core(array, axis, core):
@@ -270,34 +286,24 @@
     head_bias = w_bias.transpose(0, 2, 1)
     weights = [w_query, w_key, w_value, w_gate, w_out]
 
-    tile, weights = pl.pallas_call(
-        tile_kernel,
-        grid=(1,),
-        in_specs=[whole(member) for member in (pair_input, ln_gain, head_bias, *weights)],
-        out_specs=[
-            pl.BlockSpec((H, 2 * PART * PART), lambda step: (0, 0)),
-            pl.BlockSpec((2, 5, C, C), lambda step: (0, 0, 0, 0)),
-        ],
+    resident = pl.BlockSpec(memory_space=pltpu.VMEM)
+    sent, weights = pl.pallas_call(
+        open_kernel,
+        in_specs=[pl.BlockSpec(memory_space=pltpu.SMEM)] + [resident] * 8,
+        out_specs=[resident] * 2,
         out_shape=[
-            jax.ShapeDtypeStruct((H, 2 * PART * PART), jnp.float32),
+            jax.ShapeDtypeStruct((8, 2 * OWN + 3, PART, C), jnp.bfloat16),
             jax.ShapeDtypeStruct((2, 5, C, C), jnp.bfloat16),
         ],
-        name="bias_tile",
-    )(pair_input, ln_gain, head_bias, *weights)
-    tile = by_core(tile.reshape(H, PART, 2, PART), 2, core).astype(jnp.bfloat16)
-    tile = jnp.pad(
-        tile.transpose(1, 0, 2, 3).reshape(PART, HALF), ((0, 0), (0, 3 * C - HALF))
-    )
-    tile = tile.reshape(PART, 3, C).transpose(1, 0, 2)
-    halves = by_core(pair_input.reshape(8, OWN, 2, PART, C), 2, core)
-    halves = halves.transpose(0, 2, 1, 3, 4).reshape(8, 2 * OWN, PART, C)
-    xa = to_columns(jnp.concatenate([halves, copies(tile)], axis=1))
+        scratch_shapes=[pltpu.VMEM((PART, 3 * C), jnp.float32)],
+        name="open",
+    )(core.reshape(1).astype(jnp.int32), pair_input, ln_gain, head_bias, *weights)
+    xa = to_columns(sent)
     xs = lax.ppermute(xa, "row", PARTNER)
     tile = pl.pallas_call(
         spread_kernel,
-        grid=(1,),
-        in_specs=[pl.BlockSpec((8, 13, PART, C), lambda step: (0, 0, 0, 0))],
-        out_specs=pl.BlockSpec((8, H, CHUNKS, PART, C), lambda step: (0,) * 5),
+        in_specs=[pl.BlockSpec(memory_space=pltpu.VMEM)],
+        out_specs=pl.BlockSpec(memory_space=pltpu.VMEM),
         out_shape=jax.ShapeDtypeStruct((8, H, CHUNKS, PART, C), jnp.bfloat16),
         name="spread_tile",
     )(xa)

time: 156 us -> 153 us (0.981)
  local copies, waits for them, and re-layouts: 6.67 us -> 4.76 us
where the time goes in v6:
time: 153 us
  blocking collectives  81.6 us (53%)
  Pallas kernels  39 us (25%)
  waiting for transfers between devices  21.1 us (14%)
  starting transfers between devices  5.25 us (3%)
  local copies, waits for them, and re-layouts  4.76 us (3%)
    all_to_all x1, blocking collectives, to_all(): lax.all_to_all(array, ('row', 'col'), 0, 0, axis_index_groups=CORE_PLANES...  38.4 us
    pallas_call x2, Pallas kernels, attend(): pl.pallas_call((start_kernel, end_kernel)[section], in_specs=[resident] *...  32.9 us
    all_to_all x1, blocking collectives, to_columns(): return lax.all_to_all(flat, 'col', 0, 0, tiled=True).reshape(array.shape)  24.7 us
    all_to_all x1, blocking collectives, to_rows(): lax.all_to_all(flat, 'row', 0, 0, axis_index_groups=SAME_CORE, tiled=True)  18.5 us
    all_to_all x1, waiting for transfers between devices, to_rows(): lax.all_to_all(flat, 'row', 0, 0, axis_index_groups=SAME_CORE, tiled=True)  17.9 us
    all_to_all x1, starting transfers between devices, to_rows(): lax.all_to_all(flat, 'row', 0, 0, axis_index_groups=SAME_CORE, tiled=True)  4.9 us
    pallas_call x1, Pallas kernels, body(): pl.pallas_call(open_kernel, in_specs=[pl.BlockSpec(memory_space=pltpu.SME...  3.45 us
    ppermute x2, waiting for transfers between devices, body(): xs = lax.ppermute(xa, 'row', PARTNER)  3.21 us
  transfers between devices with their start and end apart: 3, of which 3 were waited for; matrix products, arithmetic and copies ran while one was open for 1% of the time, Pallas kernels for 0%

profile of v6, /device:TPU:8, one launch (start us, length us, event | category | flops | bytes accessed | tf_op | source)
XLA Modules:
  0.0 152.9 jit_solution(11013405303219097)
XLA Ops:
  0.0 3.5 %open.1 = (bf16[8,13,40,128]{3,2,1,0:T(8,128)(2,1)}, bf16[2,5,128,128]{3,2,1,0:T(8,128)(2,1)}) custom-call(s32[1]{0:T(128)} %bitcast.core, bf16[40,80,128]{2,1,0:T(8,128)(2,1)} %block.1, f32[2,128]{1,0:T(2,128)} %gain.5, bf16[2,4,128]{2,1,0:T(4,128)(2,1)} %bitcast.33, bf16[2,128,128]{2,1,0:T(8,128)(2,1)} %rest_0_.1, bf16[2,128,128]{2,1,0:T(8,128)(2,1)} %rest_1_.1, ...), custom_call_target="tpu_custom_call" | custom-call | tf_op jit(solution)/shard_map/open/pallas_call | solution.py:290
  3.5 24.7 %all_to_all.20 = bf16[8,520,128]{2,1,0:T(8,128)(2,1)} all-to-all(bf16[8,520,128]{2,1,0:T(8,128)(2,1)} %bitcast.44), channel_id=1, replica_groups=mesh['row'=16,'col'=8] {'col'}, dimensions={0} | all-to-all | bytes 2129920 | tf_op jit(solution)/shard_map/all_to_all | solution.py:265
  28.1 2.7 %spread_tile.1 = bf16[8,4,5,40,128]{4,3,2,1,0:T(8,128)(2,1)} custom-call(bf16[8,13,40,128]{3,2,1,0:T(8,128)(2,1)} %bitcast.28), custom_call_target="tpu_custom_call" | custom-call | tf_op jit(solution)/shard_map/spread_tile/pallas_call | solution.py:303
  30.8 0.0 copy-start
  30.8 0.0 copy-start.4
  30.8 0.0 copy-start.1
  30.8 0.0 copy-start.2
  30.8 0.0 copy-start.3
  30.9 4.9 %all-to-all-start.1 = ((bf16[8,800,128]{2,1,0:T(8,128)(2,1)}), bf16[8,800,128]{2,1,0:T(8,128)(2,1)S(1)}, u32[]{:S(2)}, u32[]{:S(2)}) async-start(bf16[8,800,128]{2,1,0:T(8,128)(2,1)} %bitcast.35), calls=%async_computation.1 | async-start | bytes 3276800 | tf_op jit(solution)/shard_map/all_to_all | solution.py:270
  35.7 0.0 copy-done
  35.8 0.1 collective-permute-start
  35.9 0.0 copy-done.4
  35.9 0.1 reshape.56
  36.0 0.1 reshape.57.mask
  36.1 2.5 %collective-permute-done.xs = bf16[8,13,40,128]{3,2,1,0:T(8,128)(2,1)} collective-permute-done((bf16[8,13,40,128]{3,2,1,0:T(8,128)(2,1)S(1)}, bf16[8,13,40,128]{3,2,1,0:T(8,128)(2,1)}, u32[]{:S(2)}, u32[]{:S(2)}) %collective-permute-start) | collective-permute-done | bytes 1064992 | tf_op jit(solution)/shard_map/ppermute | solution.py:302
  38.6 17.9 %all-to-all-done.1 = bf16[8,800,128]{2,1,0:T(8,128)(2,1)S(1)} async-done(((bf16[8,800,128]{2,1,0:T(8,128)(2,1)}), bf16[8,800,128]{2,1,0:T(8,128)(2,1)S(1)}, u32[]{:S(2)}, u32[]{:S(2)}) %all-to-all-start.1) | async-done | bytes 1638432 | tf_op jit(solution)/shard_map/all_to_all | solution.py:270
  56.6 0.0 copy-done.1
  56.6 0.0 copy-done.2
  56.6 0.0 copy-done.3
  56.6 17.0 %start_node.1 = (bf16[8,5,2,40,128]{4,3,2,1,0:T(8,128)(2,1)S(1)}, f32[2,5,4,320]{3,2,1,0:T(4,128)S(1)}) custom-call(bf16[8,13,40,128]{3,2,1,0:T(8,128)(2,1)S(1)} %bitcast.30, bf16[8,13,40,128]{3,2,1,0:T(8,128)(2,1)} %collective-permute-done.xs, f32[1,640]{1,0:T(1,128)S(1)} %reshape.57.mask, f32[2,128]{1,0:T(2,128)S(1)} %copy-done.2, ...), custom_call_target="tpu_custom_call" | custom-call | flops 8000000000 | bytes 6000000 | tf_op jit(solution)/shard_map/start_node/pallas_call | solution.py:245
  73.6 0.2 copy.34
  73.8 0.2 copy.35
  74.1 0.1 reshape.62
  74.2 0.5 copy.37
  74.8 0.2 broadcast_in_dim.18
  75.0 0.7 pad_maximum_fusion
  75.8 38.4 %all_to_all.21 = bf16[64,150,128]{2,1,0:T(8,128)(2,1)S(1)} all-to-all(bf16[64,150,128]{2,1,0:T(8,128)(2,1)S(1)} %pad_maximum_fusion), channel_id=1, replica_groups={{0,1,2,3,4,5,6,7,16,17,18,19,20,21,22,23,32,33,34,35,36,37,38,39,48,49,..., dimensions={0} | all-to-all | bytes 4915200 | tf_op jit(solution)/shard_map/all_to_all | solution.py:275
  114.2 0.1 slice.8
  114.3 0.2 copy.47
  114.5 0.1 copy.39
  114.6 0.1 copy.43.xa
  114.7 0.3 collective-permute-start.1
  115.0 0.7 slice.9
  115.7 0.4 copy.48
  116.1 0.3 copy.42
  116.4 0.2 copy.44.rest_1_
  116.7 0.7 collective-permute-done.1.xs
  117.3 15.8 %end_node.1 = bf16[8,5,2,40,128]{4,3,2,1,0:T(8,128)(2,1)S(1)} custom-call(bf16[8,10,40,128]{3,2,1,0:T(8,128)(2,1)S(1)} %copy.43.xa, bf16[8,10,40,128]{3,2,1,0:T(8,128)(2,1)S(1)} %collective-permute-done.1.xs, f32[1,640]{1,0:T(1,128)S(1)} %reshape.57.mask, f32[2,128]{1,0:T(2,128)S(1)} %copy-done.2, bf16[2,5,128,128]{3,2,1,0:T(8,128)(2,1)S(1)} %copy-done.3, ...), custom_call_target="tpu_custom_call" | custom-call | flops 8000000000 | bytes 6000000 | tf_op jit(solution)/shard_map/end_node/pallas_call | solution.py:245
  133.2 18.5 %all_to_all.22 = bf16[8,400,128]{2,1,0:T(8,128)(2,1)S(1)} all-to-all(bf16[8,400,128]{2,1,0:T(8,128)(2,1)S(1)} %bitcast.32), channel_id=1, replica_groups={{0,16,32,48,64,80,96,112},{8,24,40,56,72,88,104,120},{1,17,33,49,65,81,..., dimensions={0} | all-to-all | bytes 1638400 | tf_op jit(solution)/shard_map/all_to_all | solution.py:270
  151.7 0.2 fusion
  151.9 0.1 copy.45
  151.9 1.0 copy.46
  (7 shorter events, 0.1 us)
Async XLA Ops:
  30.8 4.9 %copy-start = (bf16[8,520,128]{2,1,0:T(8,128)(2,1)S(1)}, bf16[8,520,128]{2,1,0:T(8,128)(2,1)}, u32[]{:S(2)}) copy-start(bf16[8,520,128]{2,1,0:T(8,128)(2,1)} %all_to_all.20) | copy-start | bytes 3194884
  30.8 5.0 %copy-start.4 = (s32[640]{0:T(1024)S(1)}, s32[640]{0:T(1024)}, u32[]{:S(2)}) copy-start(s32[640]{0:T(1024)} %param.10) | copy-start | bytes 7684
  30.8 25.7 %copy-start.1 = (bf16[2,128,4]{1,2,0:T(4,128)(2,1)S(1)}, bf16[2,128,4]{1,2,0:T(4,128)(2,1)}, u32[]{:S(2)}) copy-start(bf16[2,128,4]{1,2,0:T(4,128)(2,1)} %param.16) | copy-start | bytes 6148
  30.8 25.7 %copy-start.2 = (f32[2,128]{1,0:T(2,128)S(1)}, f32[2,128]{1,0:T(2,128)}, u32[]{:S(2)}) copy-start(f32[2,128]{1,0:T(2,128)} %gain.5) | copy-start | bytes 3076
  30.8 25.7 %copy-start.3 = (bf16[2,5,128,128]{3,2,1,0:T(8,128)(2,1)S(1)}, bf16[2,5,128,128]{3,2,1,0:T(8,128)(2,1)}, u32[]{:S(2)}) copy-start(bf16[2,5,128,128]{3,2,1,0:T(8,128)(2,1)} %get-tuple-element.10.rest_0_) | copy-start | bytes 983044
  30.9 25.7 %all-to-all-start.1 = ((bf16[8,800,128]{2,1,0:T(8,128)(2,1)}), bf16[8,800,128]{2,1,0:T(8,128)(2,1)S(1)}, u32[]{:S(2)}, u32[]{:S(2)}) async-start(bf16[8,800,128]{2,1,0:T(8,128)(2,1)} %bitcast.35), calls=%async_computation.1 | async-start | bytes 3276800 | tf_op jit(solution)/shard_map/all_to_all | solution.py:270
  35.8 2.9 %collective-permute-start = (bf16[8,13,40,128]{3,2,1,0:T(8,128)(2,1)S(1)}, bf16[8,13,40,128]{3,2,1,0:T(8,128)(2,1)}, u32[]{:S(2)}, u32[]{:S(2)}) collective-permute-start(bf16[8,13,40,128]{3,2,1,0:T(8,128)(2,1)S(1)} %bitcast.29), channel_id=1, source_target_pairs={{0,8},{8,0},{16,24},{24,16},{32,40},{40,32},{48,56},{56,48},{64,72... | collective-permute-start | bytes 3194888 | tf_op jit(solution)/shard_map/ppermute | solution.py:302
  114.7 2.6 %collective-permute-start.1 = (bf16[8,10,40,128]{3,2,1,0:T(8,128)(2,1)S(1)}, bf16[8,10,40,128]{3,2,1,0:T(8,128)(2,1)S(1)}, u32[]{:S(2)}, u32[]{:S(2)}) collective-permute-start(bf16[8,10,40,128]{3,2,1,0:T(8,128)(2,1)S(1)} %copy.43.xa), channel_id=1, source_target_pairs={{0,8},{8,0},{16,24},{24,16},{32,40},{40,32},{48,56},{56,48},{64,72... | collective-permute-start | bytes 2457608 | tf_op jit(solution)/shard_map/ppermute | solution.py:321

commit v7 on v6

--- a/solution.py
+++ b/solution.py
@@ -140,8 +140,6 @@
     weights, bias = rest[:2]
     out, bias_s, turned_s = rest[2:]
 
-    row = lax.broadcasted_iota(jnp.int32, (HALF, 2 * HALF), 0)
-    col = lax.broadcasted_iota(jnp.int32, (HALF, 2 * HALF), 1)
     for pair in range(2):
         for place in range(8):
             for side in range(2):
@@ -151,13 +149,8 @@
                         place, pair, side, part
                     ].astype(jnp.float32)
     for head in range(H):
-        chosen = jnp.where(row + (head % 2) * HALF == col, 1.0, 0.0).astype(jnp.bfloat16)
-        turned = lax.dot_general(
-            chosen,
-            turned_s[head // 2].astype(jnp.bfloat16),
-            CONTRACT_LAST,
-            preferred_element_type=jnp.float32,
-        )
+        first = (head % 2) * HALF
+        turned = turned_s[head // 2, :, first : first + HALF].T
         bias_s[head] = turned * LOG2E + mask[...]
 
     def pair(step):

time: 153 us -> 153 us (level)
  no operation moved by 1% of the time
where the time goes in v7:
time: 153 us; the launch traced here: 152 us
  blocking collectives  81.6 us (53%)
  Pallas kernels  38.6 us (25%)
  waiting for transfers between devices  21.1 us (14%)
  starting transfers between devices  5.25 us (3%)
  local copies, waits for them, and re-layouts  4.76 us (3%)
    all_to_all x1, blocking collectives, to_all(): lax.all_to_all(array, ('row', 'col'), 0, 0, axis_index_groups=CORE_PLANES...  38.4 us
    pallas_call x2, Pallas kernels, attend(): pl.pallas_call((start_kernel, end_kernel)[section], in_specs=[resident] *...  32.4 us
    all_to_all x1, blocking collectives, to_columns(): return lax.all_to_all(flat, 'col', 0, 0, tiled=True).reshape(array.shape)  24.7 us
    all_to_all x1, blocking collectives, to_rows(): lax.all_to_all(flat, 'row', 0, 0, axis_index_groups=SAME_CORE, tiled=True)  18.5 us
    all_to_all x1, waiting for transfers between devices, to_rows(): lax.all_to_all(flat, 'row', 0, 0, axis_index_groups=SAME_CORE, tiled=True)  17.9 us
    all_to_all x1, starting transfers between devices, to_rows(): lax.all_to_all(flat, 'row', 0, 0, axis_index_groups=SAME_CORE, tiled=True)  4.9 us
    pallas_call x1, Pallas kernels, body(): pl.pallas_call(open_kernel, in_specs=[pl.BlockSpec(memory_space=pltpu.SME...  3.45 us
    ppermute x2, waiting for transfers between devices, body(): xs = lax.ppermute(xa, 'row', PARTNER)  3.21 us
  transfers between devices with their start and end apart: 3, of which 3 were waited for; matrix products, arithmetic and copies ran while one was open for 1% of the time, Pallas kernels for 0%

profile of v7, /device:TPU:8, one launch (start us, length us, event | category | flops | bytes accessed | tf_op | source)
XLA Modules:
  0.0 152.4 jit_solution(3237789313886604098)
XLA Ops:
  0.0 3.5 %open.1 = (bf16[8,13,40,128]{3,2,1,0:T(8,128)(2,1)}, bf16[2,5,128,128]{3,2,1,0:T(8,128)(2,1)}) custom-call(s32[1]{0:T(128)} %bitcast.core, bf16[40,80,128]{2,1,0:T(8,128)(2,1)} %block.1, f32[2,128]{1,0:T(2,128)} %gain.5, bf16[2,4,128]{2,1,0:T(4,128)(2,1)} %bitcast.33, bf16[2,128,128]{2,1,0:T(8,128)(2,1)} %rest_0_.1, bf16[2,128,128]{2,1,0:T(8,128)(2,1)} %rest_1_.1, ...), custom_call_target="tpu_custom_call" | custom-call | tf_op jit(solution)/shard_map/open/pallas_call | solution.py:283
  3.5 24.7 %all_to_all.20 = bf16[8,520,128]{2,1,0:T(8,128)(2,1)} all-to-all(bf16[8,520,128]{2,1,0:T(8,128)(2,1)} %bitcast.44), channel_id=1, replica_groups=mesh['row'=16,'col'=8] {'col'}, dimensions={0} | all-to-all | bytes 2129920 | tf_op jit(solution)/shard_map/all_to_all | solution.py:258
  28.1 2.7 %spread_tile.1 = bf16[8,4,5,40,128]{4,3,2,1,0:T(8,128)(2,1)} custom-call(bf16[8,13,40,128]{3,2,1,0:T(8,128)(2,1)} %bitcast.28), custom_call_target="tpu_custom_call" | custom-call | tf_op jit(solution)/shard_map/spread_tile/pallas_call | solution.py:296
  30.8 0.0 copy-start
  30.8 0.0 copy-start.4
  30.8 0.0 copy-start.1
  30.8 0.0 copy-start.2
  30.8 0.0 copy-start.3
  30.9 4.9 %all-to-all-start.1 = ((bf16[8,800,128]{2,1,0:T(8,128)(2,1)}), bf16[8,800,128]{2,1,0:T(8,128)(2,1)S(1)}, u32[]{:S(2)}, u32[]{:S(2)}) async-start(bf16[8,800,128]{2,1,0:T(8,128)(2,1)} %bitcast.35), calls=%async_computation.1 | async-start | bytes 3276800 | tf_op jit(solution)/shard_map/all_to_all | solution.py:263
  35.7 0.0 copy-done
  35.8 0.1 collective-permute-start
  35.9 0.0 copy-done.4
  35.9 0.1 reshape.56
  36.0 0.1 reshape.57.mask
  36.1 2.5 %collective-permute-done.xs = bf16[8,13,40,128]{3,2,1,0:T(8,128)(2,1)} collective-permute-done((bf16[8,13,40,128]{3,2,1,0:T(8,128)(2,1)S(1)}, bf16[8,13,40,128]{3,2,1,0:T(8,128)(2,1)}, u32[]{:S(2)}, u32[]{:S(2)}) %collective-permute-start) | collective-permute-done | bytes 1064992 | tf_op jit(solution)/shard_map/ppermute | solution.py:295
  38.6 17.9 %all-to-all-done.1 = bf16[8,800,128]{2,1,0:T(8,128)(2,1)S(1)} async-done(((bf16[8,800,128]{2,1,0:T(8,128)(2,1)}), bf16[8,800,128]{2,1,0:T(8,128)(2,1)S(1)}, u32[]{:S(2)}, u32[]{:S(2)}) %all-to-all-start.1) | async-done | bytes 1638432 | tf_op jit(solution)/shard_map/all_to_all | solution.py:263
  56.6 0.0 copy-done.1
  56.6 0.0 copy-done.2
  56.6 0.0 copy-done.3
  56.6 17.0 %start_node.1 = (bf16[8,5,2,40,128]{4,3,2,1,0:T(8,128)(2,1)S(1)}, f32[2,5,4,320]{3,2,1,0:T(4,128)S(1)}) custom-call(bf16[8,13,40,128]{3,2,1,0:T(8,128)(2,1)S(1)} %bitcast.30, bf16[8,13,40,128]{3,2,1,0:T(8,128)(2,1)} %collective-permute-done.xs, f32[1,640]{1,0:T(1,128)S(1)} %reshape.57.mask, f32[2,128]{1,0:T(2,128)S(1)} %copy-done.2, ...), custom_call_target="tpu_custom_call" | custom-call | flops 8000000000 | bytes 6000000 | tf_op jit(solution)/shard_map/start_node/pallas_call | solution.py:238
  73.6 0.2 copy.34
  73.8 0.2 copy.35
  74.1 0.1 reshape.62
  74.2 0.5 copy.37
  74.8 0.2 broadcast_in_dim.18
  75.0 0.7 pad_maximum_fusion
  75.8 38.4 %all_to_all.21 = bf16[64,150,128]{2,1,0:T(8,128)(2,1)S(1)} all-to-all(bf16[64,150,128]{2,1,0:T(8,128)(2,1)S(1)} %pad_maximum_fusion), channel_id=1, replica_groups={{0,1,2,3,4,5,6,7,16,17,18,19,20,21,22,23,32,33,34,35,36,37,38,39,48,49,..., dimensions={0} | all-to-all | bytes 4915200 | tf_op jit(solution)/shard_map/all_to_all | solution.py:268
  114.2 0.1 slice.8
  114.3 0.2 copy.47
  114.5 0.1 copy.39
  114.6 0.1 copy.43.xa
  114.7 0.3 collective-permute-start.1
  115.0 0.7 slice.9
  115.7 0.4 copy.48
  116.1 0.3 copy.42
  116.4 0.2 copy.44.rest_1_
  116.7 0.7 collective-permute-done.1.xs
  117.3 15.4 %end_node.1 = bf16[8,5,2,40,128]{4,3,2,1,0:T(8,128)(2,1)S(1)} custom-call(bf16[8,10,40,128]{3,2,1,0:T(8,128)(2,1)S(1)} %copy.43.xa, bf16[8,10,40,128]{3,2,1,0:T(8,128)(2,1)S(1)} %collective-permute-done.1.xs, f32[1,640]{1,0:T(1,128)S(1)} %reshape.57.mask, f32[2,128]{1,0:T(2,128)S(1)} %copy-done.2, bf16[2,5,128,128]{3,2,1,0:T(8,128)(2,1)S(1)} %copy-done.3, ...), custom_call_target="tpu_custom_call" | custom-call | flops 8000000000 | bytes 6000000 | tf_op jit(solution)/shard_map/end_node/pallas_call | solution.py:238
  132.7 18.5 %all_to_all.22 = bf16[8,400,128]{2,1,0:T(8,128)(2,1)S(1)} all-to-all(bf16[8,400,128]{2,1,0:T(8,128)(2,1)S(1)} %bitcast.32), channel_id=1, replica_groups={{0,16,32,48,64,80,96,112},{8,24,40,56,72,88,104,120},{1,17,33,49,65,81,..., dimensions={0} | all-to-all | bytes 1638400 | tf_op jit(solution)/shard_map/all_to_all | solution.py:263
  151.2 0.2 fusion
  151.4 0.1 copy.45
  151.4 1.0 copy.46
  (7 shorter events, 0.1 us)
Async XLA Ops:
  30.8 4.9 %copy-start = (bf16[8,520,128]{2,1,0:T(8,128)(2,1)S(1)}, bf16[8,520,128]{2,1,0:T(8,128)(2,1)}, u32[]{:S(2)}) copy-start(bf16[8,520,128]{2,1,0:T(8,128)(2,1)} %all_to_all.20) | copy-start | bytes 3194884
  30.8 5.0 %copy-start.4 = (s32[640]{0:T(1024)S(1)}, s32[640]{0:T(1024)}, u32[]{:S(2)}) copy-start(s32[640]{0:T(1024)} %param.10) | copy-start | bytes 7684
  30.8 25.7 %copy-start.1 = (bf16[2,128,4]{1,2,0:T(4,128)(2,1)S(1)}, bf16[2,128,4]{1,2,0:T(4,128)(2,1)}, u32[]{:S(2)}) copy-start(bf16[2,128,4]{1,2,0:T(4,128)(2,1)} %param.16) | copy-start | bytes 6148
  30.8 25.7 %copy-start.2 = (f32[2,128]{1,0:T(2,128)S(1)}, f32[2,128]{1,0:T(2,128)}, u32[]{:S(2)}) copy-start(f32[2,128]{1,0:T(2,128)} %gain.5) | copy-start | bytes 3076
  30.8 25.7 %copy-start.3 = (bf16[2,5,128,128]{3,2,1,0:T(8,128)(2,1)S(1)}, bf16[2,5,128,128]{3,2,1,0:T(8,128)(2,1)}, u32[]{:S(2)}) copy-start(bf16[2,5,128,128]{3,2,1,0:T(8,128)(2,1)} %get-tuple-element.10.rest_0_) | copy-start | bytes 983044
  30.9 25.7 %all-to-all-start.1 = ((bf16[8,800,128]{2,1,0:T(8,128)(2,1)}), bf16[8,800,128]{2,1,0:T(8,128)(2,1)S(1)}, u32[]{:S(2)}, u32[]{:S(2)}) async-start(bf16[8,800,128]{2,1,0:T(8,128)(2,1)} %bitcast.35), calls=%async_computation.1 | async-start | bytes 3276800 | tf_op jit(solution)/shard_map/all_to_all | solution.py:263
  35.8 2.9 %collective-permute-start = (bf16[8,13,40,128]{3,2,1,0:T(8,128)(2,1)S(1)}, bf16[8,13,40,128]{3,2,1,0:T(8,128)(2,1)}, u32[]{:S(2)}, u32[]{:S(2)}) collective-permute-start(bf16[8,13,40,128]{3,2,1,0:T(8,128)(2,1)S(1)} %bitcast.29), channel_id=1, source_target_pairs={{0,8},{8,0},{16,24},{24,16},{32,40},{40,32},{48,56},{56,48},{64,72... | collective-permute-start | bytes 3194888 | tf_op jit(solution)/shard_map/ppermute | solution.py:295
  114.7 2.6 %collective-permute-start.1 = (bf16[8,10,40,128]{3,2,1,0:T(8,128)(2,1)S(1)}, bf16[8,10,40,128]{3,2,1,0:T(8,128)(2,1)S(1)}, u32[]{:S(2)}, u32[]{:S(2)}) collective-permute-start(bf16[8,10,40,128]{3,2,1,0:T(8,128)(2,1)S(1)} %copy.43.xa), channel_id=1, source_target_pairs={{0,8},{8,0},{16,24},{24,16},{32,40},{40,32},{48,56},{56,48},{64,72... | collective-permute-start | bytes 2457608 | tf_op jit(solution)/shard_map/ppermute | solution.py:314

commit v8 on v7

--- a/solution.py
+++ b/solution.py
@@ -48,14 +48,12 @@
 
 
 def prepare(queries_in, others_in, gain, w_query, w_key, w_value, w_gate):
-    own = normalize(queries_in, gain)
-    other = normalize(others_in, gain)
-    own_all = dot(own, jnp.concatenate([w_query, w_gate, w_key, w_value], axis=1))
-    other_all = dot(other, jnp.concatenate([w_key, w_value], axis=1))
+    normed = normalize(jnp.concatenate([queries_in, others_in], axis=0), gain)
+    own_all = dot(normed[:HALF], jnp.concatenate([w_query, w_gate], axis=1))
+    both = dot(normed, jnp.concatenate([w_key, w_value], axis=1)).astype(jnp.bfloat16)
+    keys, values = both[:, :C], both[:, C:]
     queries = own_all[:, :C].astype(jnp.bfloat16).astype(jnp.float32) * SCALE
     gating = jax.nn.sigmoid(own_all[:, C : 2 * C])
-    keys = jnp.concatenate([own_all[:, 2 * C : 3 * C], other_all[:, :C]], axis=0).astype(jnp.bfloat16)
-    values = jnp.concatenate([own_all[:, 3 * C :], other_all[:, C:]], axis=0).astype(jnp.bfloat16)
     coarse = queries.astype(jnp.bfloat16)
     fine = (queries - coarse.astype(jnp.float32)).astype(jnp.bfloat16)
     both_queries = jnp.concatenate([coarse, fine], axis=1)
@@ -129,8 +127,8 @@
         for slot in range(2):
             after = afters[slot]
             out[:, step, slot] = after.reshape(8, PART, C).astype(jnp.bfloat16)
-            normed = normalize(after, gain[1:2])
-            tile[slot, step] = head_rows(next_bias[1], normed)
+        normed = normalize(jnp.concatenate(afters, axis=0), gain[1:2])
+        tile[step] = head_rows(next_bias[1], normed)
 
     pair(0)
     pl.loop(1, OWN)(pair)
@@ -230,7 +228,7 @@
     operands = [xa, xs, mask, gain]
     if section == 0:
         operands.append(next_bias)
-        out_shape.append(jax.ShapeDtypeStruct((2, OWN, H, HALF), jnp.float32))
+        out_shape.append(jax.ShapeDtypeStruct((OWN, H, 2 * HALF), jnp.float32))
     else:
         scratch.append(pltpu.VMEM((2, N, 2 * HALF), jnp.float32))
     operands += [weights, bias]
@@ -304,7 +302,8 @@
     after, tile = attend(0, xa, xs, mask_row, ln_gain, head_bias, weights, bias)
 
     sent = after.reshape(8, OWN, 2, 8, OWN, C).transpose(3, 0, 2, 4, 1, 5)
-    tile = tile.astype(jnp.bfloat16).reshape(2 * OWN, 2 * CHUNKS, C)
+    tile = tile.astype(jnp.bfloat16).reshape(OWN, H, 2, HALF).transpose(2, 0, 1, 3)
+    tile = tile.reshape(2 * OWN, 2 * CHUNKS, C)
     tile = jnp.broadcast_to(
         tile.transpose(1, 0, 2).reshape(1, 100, C), (64, 100, C)
     )

time: 153 us -> 153 us (level)
  no operation moved by 1% of the time
where the time goes in v8:
time: 153 us
  blocking collectives  81.6 us (53%)
  Pallas kernels  38.6 us (25%)
  waiting for transfers between devices  21.1 us (14%)
  starting transfers between devices  5.25 us (3%)
  local copies, waits for them, and re-layouts  4.88 us (3%)
    all_to_all x1, blocking collectives, to_all(): lax.all_to_all(array, ('row', 'col'), 0, 0, axis_index_groups=CORE_PLANES...  38.4 us
    pallas_call x2, Pallas kernels, attend(): pl.pallas_call((start_kernel, end_kernel)[section], in_specs=[resident] *...  32.5 us
    all_to_all x1, blocking collectives, to_columns(): return lax.all_to_all(flat, 'col', 0, 0, tiled=True).reshape(array.shape)  24.7 us
    all_to_all x1, blocking collectives, to_rows(): lax.all_to_all(flat, 'row', 0, 0, axis_index_groups=SAME_CORE, tiled=True)  18.5 us
    all_to_all x1, waiting for transfers between devices, to_rows(): lax.all_to_all(flat, 'row', 0, 0, axis_index_groups=SAME_CORE, tiled=True)  17.9 us
    all_to_all x1, starting transfers between devices, to_rows(): lax.all_to_all(flat, 'row', 0, 0, axis_index_groups=SAME_CORE, tiled=True)  4.9 us
    pallas_call x1, Pallas kernels, body(): pl.pallas_call(open_kernel, in_specs=[pl.BlockSpec(memory_space=pltpu.SME...  3.45 us
    ppermute x2, waiting for transfers between devices, body(): xs = lax.ppermute(xa, 'row', PARTNER)  3.21 us
  transfers between devices with their start and end apart: 3, of which 3 were waited for; matrix products, arithmetic and copies ran while one was open for 1% of the time, Pallas kernels for 0%

profile of v8, /device:TPU:8, one launch (start us, length us, event | category | flops | bytes accessed | tf_op | source)
XLA Modules:
  0.0 152.7 jit_solution(15320760751384273883)
XLA Ops:
  0.0 3.5 %open.1 = (bf16[8,13,40,128]{3,2,1,0:T(8,128)(2,1)}, bf16[2,5,128,128]{3,2,1,0:T(8,128)(2,1)}) custom-call(s32[1]{0:T(128)} %bitcast.core, bf16[40,80,128]{2,1,0:T(8,128)(2,1)} %block.1, f32[2,128]{1,0:T(2,128)} %gain.5, bf16[2,4,128]{2,1,0:T(4,128)(2,1)} %bitcast.34, bf16[2,128,128]{2,1,0:T(8,128)(2,1)} %rest_0_.1, bf16[2,128,128]{2,1,0:T(8,128)(2,1)} %rest_1_.1, ...), custom_call_target="tpu_custom_call" | custom-call | tf_op jit(solution)/shard_map/open/pallas_call | solution.py:281
  3.5 24.7 %all_to_all.20 = bf16[8,520,128]{2,1,0:T(8,128)(2,1)} all-to-all(bf16[8,520,128]{2,1,0:T(8,128)(2,1)} %bitcast.45), channel_id=1, replica_groups=mesh['row'=16,'col'=8] {'col'}, dimensions={0} | all-to-all | bytes 2129920 | tf_op jit(solution)/shard_map/all_to_all | solution.py:256
  28.1 2.7 %spread_tile.1 = bf16[8,4,5,40,128]{4,3,2,1,0:T(8,128)(2,1)} custom-call(bf16[8,13,40,128]{3,2,1,0:T(8,128)(2,1)} %bitcast.29), custom_call_target="tpu_custom_call" | custom-call | tf_op jit(solution)/shard_map/spread_tile/pallas_call | solution.py:294
  30.8 0.0 copy-start
  30.8 0.0 copy-start.4
  30.8 0.0 copy-start.1
  30.8 0.0 copy-start.2
  30.8 0.0 copy-start.3
  30.9 4.9 %all-to-all-start.1 = ((bf16[8,800,128]{2,1,0:T(8,128)(2,1)}), bf16[8,800,128]{2,1,0:T(8,128)(2,1)S(1)}, u32[]{:S(2)}, u32[]{:S(2)}) async-start(bf16[8,800,128]{2,1,0:T(8,128)(2,1)} %bitcast.36), calls=%async_computation.1 | async-start | bytes 3276800 | tf_op jit(solution)/shard_map/all_to_all | solution.py:261
  35.7 0.0 copy-done
  35.8 0.1 collective-permute-start
  35.9 0.0 copy-done.4
  35.9 0.1 reshape.59
  36.0 0.1 reshape.60.mask
  36.1 2.5 %collective-permute-done.xs = bf16[8,13,40,128]{3,2,1,0:T(8,128)(2,1)} collective-permute-done((bf16[8,13,40,128]{3,2,1,0:T(8,128)(2,1)S(1)}, bf16[8,13,40,128]{3,2,1,0:T(8,128)(2,1)}, u32[]{:S(2)}, u32[]{:S(2)}) %collective-permute-start) | collective-permute-done | bytes 1064992 | tf_op jit(solution)/shard_map/ppermute | solution.py:293
  38.6 17.9 %all-to-all-done.1 = bf16[8,800,128]{2,1,0:T(8,128)(2,1)S(1)} async-done(((bf16[8,800,128]{2,1,0:T(8,128)(2,1)}), bf16[8,800,128]{2,1,0:T(8,128)(2,1)S(1)}, u32[]{:S(2)}, u32[]{:S(2)}) %all-to-all-start.1) | async-done | bytes 1638432 | tf_op jit(solution)/shard_map/all_to_all | solution.py:261
  56.6 0.0 copy-done.1
  56.6 0.0 copy-done.2
  56.6 0.0 copy-done.3
  56.6 17.1 %start_node.1 = (bf16[8,5,2,40,128]{4,3,2,1,0:T(8,128)(2,1)S(1)}, f32[5,4,640]{2,1,0:T(4,128)S(1)}) custom-call(bf16[8,13,40,128]{3,2,1,0:T(8,128)(2,1)S(1)} %bitcast.31, bf16[8,13,40,128]{3,2,1,0:T(8,128)(2,1)} %collective-permute-done.xs, f32[1,640]{1,0:T(1,128)S(1)} %reshape.60.mask, f32[2,128]{1,0:T(2,128)S(1)} %copy-done.2, ...), custom_call_target="tpu_custom_call" | custom-call | flops 8000000000 | bytes 6000000 | tf_op jit(solution)/shard_map/start_node/pallas_call | solution.py:236
  73.6 0.2 copy.36
  73.9 0.2 copy.37
  74.1 0.1 reshape.65
  74.2 0.1 reshape.66
  74.4 0.5 copy.40
  74.9 0.2 broadcast_in_dim.18
  75.1 0.7 pad_maximum_fusion
  75.9 38.4 %all_to_all.21 = bf16[64,150,128]{2,1,0:T(8,128)(2,1)S(1)} all-to-all(bf16[64,150,128]{2,1,0:T(8,128)(2,1)S(1)} %pad_maximum_fusion), channel_id=1, replica_groups={{0,1,2,3,4,5,6,7,16,17,18,19,20,21,22,23,32,33,34,35,36,37,38,39,48,49,..., dimensions={0} | all-to-all | bytes 4915200 | tf_op jit(solution)/shard_map/all_to_all | solution.py:266
  114.3 0.1 slice.8
  114.4 0.2 copy.50
  114.6 0.1 copy.42
  114.8 0.1 copy.46.xa
  114.9 0.3 collective-permute-start.1
  115.1 0.7 slice.9
  115.8 0.4 copy.51
  116.2 0.3 copy.45
  116.6 0.2 copy.47.rest_1_
  116.8 0.7 collective-permute-done.1.xs
  117.5 15.4 %end_node.1 = bf16[8,5,2,40,128]{4,3,2,1,0:T(8,128)(2,1)S(1)} custom-call(bf16[8,10,40,128]{3,2,1,0:T(8,128)(2,1)S(1)} %copy.46.xa, bf16[8,10,40,128]{3,2,1,0:T(8,128)(2,1)S(1)} %collective-permute-done.1.xs, f32[1,640]{1,0:T(1,128)S(1)} %reshape.60.mask, f32[2,128]{1,0:T(2,128)S(1)} %copy-done.2, bf16[2,5,128,128]{3,2,1,0:T(8,128)(2,1)S(1)} %copy-done.3, ...), custom_call_target="tpu_custom_call" | custom-call | flops 8000000000 | bytes 6000000 | tf_op jit(solution)/shard_map/end_node/pallas_call | solution.py:236
  132.9 18.5 %all_to_all.22 = bf16[8,400,128]{2,1,0:T(8,128)(2,1)S(1)} all-to-all(bf16[8,400,128]{2,1,0:T(8,128)(2,1)S(1)} %bitcast.33), channel_id=1, replica_groups={{0,16,32,48,64,80,96,112},{8,24,40,56,72,88,104,120},{1,17,33,49,65,81,..., dimensions={0} | all-to-all | bytes 1638400 | tf_op jit(solution)/shard_map/all_to_all | solution.py:261
  151.4 0.2 fusion
  151.6 0.1 copy.48
  151.7 1.0 copy.49
  (8 shorter events, 0.1 us)
Async XLA Ops:
  30.8 4.9 %copy-start = (bf16[8,520,128]{2,1,0:T(8,128)(2,1)S(1)}, bf16[8,520,128]{2,1,0:T(8,128)(2,1)}, u32[]{:S(2)}) copy-start(bf16[8,520,128]{2,1,0:T(8,128)(2,1)} %all_to_all.20) | copy-start | bytes 3194884
  30.8 5.0 %copy-start.4 = (s32[640]{0:T(1024)S(1)}, s32[640]{0:T(1024)}, u32[]{:S(2)}) copy-start(s32[640]{0:T(1024)} %param.10) | copy-start | bytes 7684
  30.8 25.7 %copy-start.1 = (bf16[2,128,4]{1,2,0:T(4,128)(2,1)S(1)}, bf16[2,128,4]{1,2,0:T(4,128)(2,1)}, u32[]{:S(2)}) copy-start(bf16[2,128,4]{1,2,0:T(4,128)(2,1)} %param.16) | copy-start | bytes 6148
  30.8 25.7 %copy-start.2 = (f32[2,128]{1,0:T(2,128)S(1)}, f32[2,128]{1,0:T(2,128)}, u32[]{:S(2)}) copy-start(f32[2,128]{1,0:T(2,128)} %gain.5) | copy-start | bytes 3076
  30.8 25.7 %copy-start.3 = (bf16[2,5,128,128]{3,2,1,0:T(8,128)(2,1)S(1)}, bf16[2,5,128,128]{3,2,1,0:T(8,128)(2,1)}, u32[]{:S(2)}) copy-start(bf16[2,5,128,128]{3,2,1,0:T(8,128)(2,1)} %get-tuple-element.10.rest_0_) | copy-start | bytes 983044
  30.9 25.7 %all-to-all-start.1 = ((bf16[8,800,128]{2,1,0:T(8,128)(2,1)}), bf16[8,800,128]{2,1,0:T(8,128)(2,1)S(1)}, u32[]{:S(2)}, u32[]{:S(2)}) async-start(bf16[8,800,128]{2,1,0:T(8,128)(2,1)} %bitcast.36), calls=%async_computation.1 | async-start | bytes 3276800 | tf_op jit(solution)/shard_map/all_to_all | solution.py:261
  35.8 2.9 %collective-permute-start = (bf16[8,13,40,128]{3,2,1,0:T(8,128)(2,1)S(1)}, bf16[8,13,40,128]{3,2,1,0:T(8,128)(2,1)}, u32[]{:S(2)}, u32[]{:S(2)}) collective-permute-start(bf16[8,13,40,128]{3,2,1,0:T(8,128)(2,1)S(1)} %bitcast.30), channel_id=1, source_target_pairs={{0,8},{8,0},{16,24},{24,16},{32,40},{40,32},{48,56},{56,48},{64,72... | collective-permute-start | bytes 3194888 | tf_op jit(solution)/shard_map/ppermute | solution.py:293
  114.9 2.6 %collective-permute-start.1 = (bf16[8,10,40,128]{3,2,1,0:T(8,128)(2,1)S(1)}, bf16[8,10,40,128]{3,2,1,0:T(8,128)(2,1)S(1)}, u32[]{:S(2)}, u32[]{:S(2)}) collective-permute-start(bf16[8,10,40,128]{3,2,1,0:T(8,128)(2,1)S(1)} %copy.46.xa), channel_id=1, source_target_pairs={{0,8},{8,0},{16,24},{24,16},{32,40},{40,32},{48,56},{56,48},{64,72... | collective-permute-start | bytes 2457608 | tf_op jit(solution)/shard_map/ppermute | solution.py:313

commit v9 on v7

--- a/solution.py
+++ b/solution.py
@@ -308,11 +308,11 @@
     tile = jnp.broadcast_to(
         tile.transpose(1, 0, 2).reshape(1, 100, C), (64, 100, C)
     )
-    got = to_all(jnp.concatenate([sent.reshape(64, 2 * OWN * OWN, C), tile], axis=1))
-    xa = got[:, : 2 * OWN * OWN].reshape(8, 8, 2 * OWN, OWN, C)
+    got = to_all(jnp.concatenate([tile, sent.reshape(64, 2 * OWN * OWN, C)], axis=1))
+    xa = got[:, 100:].reshape(8, 8, 2 * OWN, OWN, C)
     xa = xa.transpose(0, 2, 1, 3, 4).reshape(8, 2 * OWN, PART, C)
     xs = lax.ppermute(xa, "row", PARTNER)
-    bias = got[:, 2 * OWN * OWN :].reshape(8, 8, 2, CHUNKS, 2, OWN, C)
+    bias = got[:, :100].reshape(8, 8, 2, CHUNKS, 2, OWN, C)
     bias = bias.transpose(0, 2, 4, 3, 1, 5, 6).reshape(8, 2, 2, CHUNKS, PART, C)
     (after,) = attend(1, xa, xs, mask_row, ln_gain, None, weights, bias)
     block = by_core(to_rows(after), 2, core)

time: 153 us -> 154 us (level)
  no operation moved by 1% of the time
where the time goes in v9:
time: 154 us; the launch traced here: 153 us
  blocking collectives  81.6 us (53%)
  Pallas kernels  38.6 us (25%)
  waiting for transfers between devices  21.6 us (14%)
  local copies, waits for them, and re-layouts  5.46 us (4%)
  starting transfers between devices  5.25 us (3%)
    all_to_all x1, blocking collectives, to_all(): lax.all_to_all(array, ('row', 'col'), 0, 0, axis_index_groups=CORE_PLANES...  38.4 us
    pallas_call x2, Pallas kernels, attend(): pl.pallas_call((start_kernel, end_kernel)[section], in_specs=[resident] *...  32.4 us
    all_to_all x1, blocking collectives, to_columns(): return lax.all_to_all(flat, 'col', 0, 0, tiled=True).reshape(array.shape)  24.7 us
    all_to_all x1, blocking collectives, to_rows(): lax.all_to_all(flat, 'row', 0, 0, axis_index_groups=SAME_CORE, tiled=True)  18.5 us
    all_to_all x1, waiting for transfers between devices, to_rows(): lax.all_to_all(flat, 'row', 0, 0, axis_index_groups=SAME_CORE, tiled=True)  17.9 us
    all_to_all x1, starting transfers between devices, to_rows(): lax.all_to_all(flat, 'row', 0, 0, axis_index_groups=SAME_CORE, tiled=True)  4.9 us
    ppermute x2, waiting for transfers between devices, body(): xs = lax.ppermute(xa, 'row', PARTNER)  3.72 us
    pallas_call x1, Pallas kernels, body(): pl.pallas_call(open_kernel, in_specs=[pl.BlockSpec(memory_space=pltpu.SME...  3.46 us
  transfers between devices with their start and end apart: 3, of which 3 were waited for; matrix products, arithmetic and copies ran while one was open for 1% of the time, Pallas kernels for 0%

profile of v9, /device:TPU:8, one launch (start us, length us, event | category | flops | bytes accessed | tf_op | source)
XLA Modules:
  0.0 153.4 jit_solution(15900086932467488786)
XLA Ops:
  0.0 3.5 %open.1 = (bf16[8,13,40,128]{3,2,1,0:T(8,128)(2,1)}, bf16[2,5,128,128]{3,2,1,0:T(8,128)(2,1)}) custom-call(s32[1]{0:T(128)} %bitcast.core, bf16[40,80,128]{2,1,0:T(8,128)(2,1)} %block.1, f32[2,128]{1,0:T(2,128)} %gain.5, bf16[2,4,128]{2,1,0:T(4,128)(2,1)} %bitcast.33, bf16[2,128,128]{2,1,0:T(8,128)(2,1)} %rest_0_.1, bf16[2,128,128]{2,1,0:T(8,128)(2,1)} %rest_1_.1, ...), custom_call_target="tpu_custom_call" | custom-call | tf_op jit(solution)/shard_map/open/pallas_call | solution.py:283
  3.5 24.7 %all_to_all.20 = bf16[8,520,128]{2,1,0:T(8,128)(2,1)} all-to-all(bf16[8,520,128]{2,1,0:T(8,128)(2,1)} %bitcast.44), channel_id=1, replica_groups=mesh['row'=16,'col'=8] {'col'}, dimensions={0} | all-to-all | bytes 2129920 | tf_op jit(solution)/shard_map/all_to_all | solution.py:258
  28.1 2.7 %spread_tile.1 = bf16[8,4,5,40,128]{4,3,2,1,0:T(8,128)(2,1)} custom-call(bf16[8,13,40,128]{3,2,1,0:T(8,128)(2,1)} %bitcast.28), custom_call_target="tpu_custom_call" | custom-call | tf_op jit(solution)/shard_map/spread_tile/pallas_call | solution.py:296
  30.8 0.0 copy-start
  30.8 0.0 copy-start.5
  30.8 0.0 copy-start.1
  30.8 0.0 copy-start.2
  30.8 4.9 %all-to-all-start.1 = ((bf16[8,800,128]{2,1,0:T(8,128)(2,1)}), bf16[8,800,128]{2,1,0:T(8,128)(2,1)S(1)}, u32[]{:S(2)}, u32[]{:S(2)}) async-start(bf16[8,800,128]{2,1,0:T(8,128)(2,1)} %bitcast.35), calls=%async_computation.1 | async-start | bytes 3276800 | tf_op jit(solution)/shard_map/all_to_all | solution.py:263
  35.7 0.0 copy-done
  35.7 0.1 collective-permute-start
  35.8 0.0 copy-done.5
  35.9 0.1 reshape.56
  36.0 0.1 reshape.57.mask
  36.1 2.5 %collective-permute-done.xs = bf16[8,13,40,128]{3,2,1,0:T(8,128)(2,1)} collective-permute-done((bf16[8,13,40,128]{3,2,1,0:T(8,128)(2,1)S(1)}, bf16[8,13,40,128]{3,2,1,0:T(8,128)(2,1)}, u32[]{:S(2)}, u32[]{:S(2)}) %collective-permute-start) | collective-permute-done | bytes 1064992 | tf_op jit(solution)/shard_map/ppermute | solution.py:295
  38.6 17.9 %all-to-all-done.1 = bf16[8,800,128]{2,1,0:T(8,128)(2,1)S(1)} async-done(((bf16[8,800,128]{2,1,0:T(8,128)(2,1)}), bf16[8,800,128]{2,1,0:T(8,128)(2,1)S(1)}, u32[]{:S(2)}, u32[]{:S(2)}) %all-to-all-start.1) | async-done | bytes 1638432 | tf_op jit(solution)/shard_map/all_to_all | solution.py:263
  56.6 0.0 copy-done.1
  56.6 0.0 copy-done.2
  56.6 0.0 copy-start.3
  56.6 1.0 copy-done.3
  57.5 17.0 %start_node.1 = (bf16[8,5,2,40,128]{4,3,2,1,0:T(8,128)(2,1)S(1)}, f32[2,5,4,320]{3,2,1,0:T(4,128)S(1)}) custom-call(bf16[8,13,40,128]{3,2,1,0:T(8,128)(2,1)S(1)} %bitcast.30, bf16[8,13,40,128]{3,2,1,0:T(8,128)(2,1)} %collective-permute-done.xs, f32[1,640]{1,0:T(1,128)S(1)} %reshape.57.mask, f32[2,128]{1,0:T(2,128)S(1)} %copy-done.2, ...), custom_call_target="tpu_custom_call" | custom-call | flops 8000000000 | bytes 6000000 | tf_op jit(solution)/shard_map/start_node/pallas_call | solution.py:238
  74.6 0.1 reshape.60
  74.7 0.2 copy.35
  75.0 0.2 copy.36
  75.2 0.5 copy.37
  75.7 0.2 broadcast_in_dim.18
  76.0 0.5 pad_maximum_fusion
  76.4 38.4 %all_to_all.21 = bf16[64,150,128]{2,1,0:T(8,128)(2,1)S(1)} all-to-all(bf16[64,150,128]{2,1,0:T(8,128)(2,1)S(1)} %pad_maximum_fusion), channel_id=1, replica_groups={{0,1,2,3,4,5,6,7,16,17,18,19,20,21,22,23,32,33,34,35,36,37,38,39,48,49,..., dimensions={0} | all-to-all | bytes 4915200 | tf_op jit(solution)/shard_map/all_to_all | solution.py:268
  114.9 0.3 slice.8
  115.2 0.2 copy.47
  115.4 0.1 copy.39
  115.6 0.1 copy.43.xa
  115.7 0.3 collective-permute-start.1
  116.0 0.1 slice.9
  116.1 0.4 copy.48
  116.5 0.3 copy.42
  116.9 0.0 copy-start.4
  116.9 0.2 copy.44.rest_1_
  117.1 1.2 collective-permute-done.1.xs
  118.3 0.0 copy-done.4
  118.3 15.4 %end_node.1 = bf16[8,5,2,40,128]{4,3,2,1,0:T(8,128)(2,1)S(1)} custom-call(bf16[8,10,40,128]{3,2,1,0:T(8,128)(2,1)S(1)} %copy.43.xa, bf16[8,10,40,128]{3,2,1,0:T(8,128)(2,1)S(1)} %collective-permute-done.1.xs, f32[1,640]{1,0:T(1,128)S(1)} %reshape.57.mask, f32[2,128]{1,0:T(2,128)S(1)} %copy-done.2, bf16[2,5,128,128]{3,2,1,0:T(8,128)(2,1)S(1)} %copy-done.4, ...), custom_call_target="tpu_custom_call" | custom-call | flops 8000000000 | bytes 6000000 | tf_op jit(solution)/shard_map/end_node/pallas_call | solution.py:238
  133.7 18.5 %all_to_all.22 = bf16[8,400,128]{2,1,0:T(8,128)(2,1)S(1)} all-to-all(bf16[8,400,128]{2,1,0:T(8,128)(2,1)S(1)} %bitcast.32), channel_id=1, replica_groups={{0,16,32,48,64,80,96,112},{8,24,40,56,72,88,104,120},{1,17,33,49,65,81,..., dimensions={0} | all-to-all | bytes 1638400 | tf_op jit(solution)/shard_map/all_to_all | solution.py:263
  152.1 0.2 fusion
  152.3 0.1 copy.45
  152.4 1.0 copy.46
  (7 shorter events, 0.1 us)
Async XLA Ops:
  30.8 4.9 %copy-start = (bf16[8,520,128]{2,1,0:T(8,128)(2,1)S(1)}, bf16[8,520,128]{2,1,0:T(8,128)(2,1)}, u32[]{:S(2)}) copy-start(bf16[8,520,128]{2,1,0:T(8,128)(2,1)} %all_to_all.20) | copy-start | bytes 3194884
  30.8 5.0 %copy-start.5 = (s32[640]{0:T(1024)S(1)}, s32[640]{0:T(1024)}, u32[]{:S(2)}) copy-start(s32[640]{0:T(1024)} %param.10) | copy-start | bytes 7684
  30.8 25.7 %copy-start.1 = (bf16[2,128,4]{1,2,0:T(4,128)(2,1)S(1)}, bf16[2,128,4]{1,2,0:T(4,128)(2,1)}, u32[]{:S(2)}) copy-start(bf16[2,128,4]{1,2,0:T(4,128)(2,1)} %param.16) | copy-start | bytes 6148
  30.8 25.7 %copy-start.2 = (f32[2,128]{1,0:T(2,128)S(1)}, f32[2,128]{1,0:T(2,128)}, u32[]{:S(2)}) copy-start(f32[2,128]{1,0:T(2,128)} %gain.5) | copy-start | bytes 3076
  30.8 25.7 %all-to-all-start.1 = ((bf16[8,800,128]{2,1,0:T(8,128)(2,1)}), bf16[8,800,128]{2,1,0:T(8,128)(2,1)S(1)}, u32[]{:S(2)}, u32[]{:S(2)}) async-start(bf16[8,800,128]{2,1,0:T(8,128)(2,1)} %bitcast.35), calls=%async_computation.1 | async-start | bytes 3276800 | tf_op jit(solution)/shard_map/all_to_all | solution.py:263
  35.7 2.9 %collective-permute-start = (bf16[8,13,40,128]{3,2,1,0:T(8,128)(2,1)S(1)}, bf16[8,13,40,128]{3,2,1,0:T(8,128)(2,1)}, u32[]{:S(2)}, u32[]{:S(2)}) collective-permute-start(bf16[8,13,40,128]{3,2,1,0:T(8,128)(2,1)S(1)} %bitcast.29), channel_id=1, source_target_pairs={{0,8},{8,0},{16,24},{24,16},{32,40},{40,32},{48,56},{56,48},{64,72... | collective-permute-start | bytes 3194888 | tf_op jit(solution)/shard_map/ppermute | solution.py:295
  56.6 1.0 copy-start.3
  115.7 2.6 %collective-permute-start.1 = (bf16[8,10,40,128]{3,2,1,0:T(8,128)(2,1)S(1)}, bf16[8,10,40,128]{3,2,1,0:T(8,128)(2,1)S(1)}, u32[]{:S(2)}, u32[]{:S(2)}) collective-permute-start(bf16[8,10,40,128]{3,2,1,0:T(8,128)(2,1)S(1)} %copy.43.xa), channel_id=1, source_target_pairs={{0,8},{8,0},{16,24},{24,16},{32,40},{40,32},{48,56},{56,48},{64,72... | collective-permute-start | bytes 2457608 | tf_op jit(solution)/shard_map/ppermute | solution.py:314
  116.9 1.4 copy-start.4
